TPU v7x, 128 devices: a whole 4x4x4 slice. The times are simulated.
128 devices in a mesh: seq: 16 (over x, y), chan: 8 (over z, core).
Axes of the slice: x: 4, y: 4, z: 4, core: 2. Of those that a mesh axis runs over, the one named last changes fastest.
Arguments:
- tokens: bfloat16 [16384, 1024], P('seq', 'chan'), may hold values from -64 to 64
- norm_gain: float32 [1024], replicated, may hold values from 0.1 to 1.9
- in_weight: bfloat16 [3, 1024, 1024], P(None, None, 'chan'), may hold values from -0.1875 to 0.1875
- short_kernel: float32 [3, 3, 1024], P(None, None, 'chan'), may hold values from -3 to 3
- filter_fwd: float32 [16384, 1024], P('seq', 'chan'), may hold values from -0.75 to 0.75
- filter_bwd: float32 [16384, 1024], P('seq', 'chan'), may hold values from -0.75 to 0.75
- skip_gain: float32 [1024], P('chan'), may hold values from -1 to 1
- out_weight: bfloat16 [1024, 1024], P('chan'), may hold values from -0.1875 to 0.1875
Outputs:
- layer_out: float32 [16384, 1024], P('seq', 'chan')
All inputs are finite; a program needn't handle non-finite values.
Results may differ from a plain program's by a relative error of at most 0.0035.
Values may be sent and summed in bfloat16 or wider, within the bound.
No kernel may reach another device: no remote copies, remote signals or barrier semaphores. Data moves between devices by JAX's collectives and lax.ppermute only.
A program may use at most 128 MiB of HBM per device.

v0:
```python
import jax
import jax.numpy as jnp
from jax import lax
from jax.sharding import PartitionSpec as P

HIGHEST = lax.Precision.HIGHEST


def from_behind(value, axis, steps):
    count = lax.axis_size(axis)
    first, last = (max(0, -steps), min(count, count - steps))
    return lax.ppermute(value, axis, [(source, source + steps) for source in range(first, last)])


def partner(value, axis, apart):
    mask = 2**apart
    pairs = [(source, source ^ mask) for source in range(lax.axis_size(axis))]
    return lax.ppermute(value, axis, pairs)


def angles(index_array, period):
    return (index_array % period).astype(jnp.float32) * (2.0 * jnp.pi / period)


def rotate(real_part, imag_part, phases):
    cosine = jnp.cos(phases)
    sine_part = jnp.sin(phases)
    return (real_part * cosine - imag_part * sine_part, real_part * sine_part + imag_part * cosine)


def dft_tables(size, direction):
    points = jnp.arange(size, dtype=jnp.int32)
    phases = angles(points[:, None] * points[None, :], size)
    return (jnp.cos(phases), direction * jnp.sin(phases))


def local_dft(real_part, imag_part, direction):
    slots, length, width = real_part.shape
    first = 1
    candidate = 1
    while candidate * candidate <= length:
        if length % candidate == 0:
            first = candidate
        candidate = candidate + 1
    second = length // first
    real_four = real_part.reshape(slots, first, second, width)
    imag_four = imag_part.reshape(slots, first, second, width)
    cos_first, sin_first = dft_tables(first, direction)
    step_real = jnp.einsum("pa,zabc->zpbc", cos_first, real_four, precision=HIGHEST) - jnp.einsum(
        "pa,zabc->zpbc", sin_first, imag_four, precision=HIGHEST
    )
    step_imag = jnp.einsum("pa,zabc->zpbc", cos_first, imag_four, precision=HIGHEST) + jnp.einsum(
        "pa,zabc->zpbc", sin_first, real_four, precision=HIGHEST
    )
    twiddle = angles(
        jnp.arange(first, dtype=jnp.int32)[:, None] * jnp.arange(second, dtype=jnp.int32)[None, :],
        length,
    )
    step_real, step_imag = rotate(step_real, step_imag, direction * twiddle[None, :, :, None])
    cos_second, sin_second = dft_tables(second, direction)
    out_real = jnp.einsum("qb,zpbc->zqpc", cos_second, step_real, precision=HIGHEST) - jnp.einsum(
        "qb,zpbc->zqpc", sin_second, step_imag, precision=HIGHEST
    )
    out_imag = jnp.einsum("qb,zpbc->zqpc", cos_second, step_imag, precision=HIGHEST) + jnp.einsum(
        "qb,zpbc->zqpc", sin_second, step_real, precision=HIGHEST
    )
    return (out_real.reshape(slots, length, width), out_imag.reshape(slots, length, width))


def local(
    tokens, norm_gain, in_weight, short_kernel, filter_fwd, filter_bwd, skip_gain, out_weight
):
    seq_count = lax.axis_size("seq")
    seq_index = lax.axis_index("seq")
    block_rows, local_width = tokens.shape
    period = 2 * seq_count * block_rows
    bit_count = seq_count.bit_length() - 1
    full_rows = lax.all_gather(tokens, "chan", axis=1, tiled=True)
    widened = full_rows.astype(jnp.float32)
    inv_rms = lax.rsqrt(jnp.mean(widened * widened, axis=-1, keepdims=True) + 1e-05)
    normed = (widened * inv_rms * norm_gain).astype(jnp.bfloat16)
    projected = jnp.einsum("td,jdc->jtc", normed, in_weight, preferred_element_type=jnp.float32)
    earlier = from_behind(projected[:, block_rows - 2 :, :], "seq", 1)
    extended = jnp.concatenate([earlier, projected], axis=1)
    short_mix = (
        short_kernel[0][:, None, :] * extended[:, 2:, :]
        + short_kernel[1][:, None, :] * extended[:, 1:-1, :]
        + short_kernel[2][:, None, :] * extended[:, :-2, :]
    )
    signal = short_mix[0] * short_mix[1]
    combined = False
    stacked = jnp.concatenate([signal, filter_fwd, filter_bwd], axis=1)
    half_turn = angles(seq_index, 2 * seq_count)
    freq_real = jnp.stack([stacked, stacked * jnp.cos(half_turn)])
    freq_imag = jnp.stack([jnp.zeros_like(stacked), -stacked * jnp.sin(half_turn)])
    for section_bit in reversed(range(bit_count)):
        partner_real, partner_imag = partner((freq_real, freq_imag), "seq", section_bit)
        pair_span = 1 << section_bit
        upper_half = seq_index // pair_span % 2 == 1
        section_phase = angles(seq_index % pair_span, 2 * pair_span)
        diff_real, diff_imag = rotate(
            partner_real - freq_real, partner_imag - freq_imag, -section_phase
        )
        freq_real = jnp.where(upper_half, diff_real, freq_real + partner_real)
        freq_imag = jnp.where(upper_half, diff_imag, freq_imag + partner_imag)
    slot_index = jnp.zeros((), jnp.int32)
    for section_bit in range(bit_count):
        slot_index = slot_index + seq_index // (1 << section_bit) % 2 * (
            1 << bit_count - 1 - section_bit
        )
    offsets = jnp.arange(block_rows, dtype=jnp.int32)
    low_freq = 2 * slot_index + jnp.arange(2, dtype=jnp.int32)
    twist = angles(low_freq[:, None] * offsets[None, :], period)[:, :, None]
    freq_real, freq_imag = rotate(freq_real, freq_imag, -twist)
    spec_real, spec_imag = local_dft(freq_real, freq_imag, -1.0)
    signal_real = spec_real[:, :, :local_width]
    signal_imag = spec_imag[:, :, :local_width]
    fwd_real = spec_real[:, :, local_width : 2 * local_width]
    fwd_imag = spec_imag[:, :, local_width : 2 * local_width]
    bwd_real = spec_real[:, :, 2 * local_width :]
    bwd_imag = spec_imag[:, :, 2 * local_width :]
    whole_freq = low_freq[:, None] + 2 * seq_count * offsets[None, :]
    turn_phase = angles(whole_freq, period)[:, :, None]
    back_real, back_imag = rotate(bwd_real, -bwd_imag, turn_phase)
    gain_real = fwd_real + back_real
    gain_imag = fwd_imag + back_imag
    prod_real = signal_real * gain_real - signal_imag * gain_imag
    prod_imag = signal_real * gain_imag + signal_imag * gain_real
    time_real, time_imag = local_dft(prod_real, prod_imag, 1.0)
    time_real, time_imag = rotate(time_real, time_imag, twist)
    for section_bit in range(bit_count):
        partner_real, partner_imag = partner((time_real, time_imag), "seq", section_bit)
        pair_span = 1 << section_bit
        upper_half = seq_index // pair_span % 2 == 1
        section_phase = angles(seq_index % pair_span, 2 * pair_span)
        turned_real, turned_imag = rotate(partner_real, partner_imag, section_phase)
        mine_real, mine_imag = rotate(time_real, time_imag, section_phase)
        time_real = jnp.where(upper_half, partner_real - mine_real, time_real + turned_real) * 0.5
        time_imag = jnp.where(upper_half, partner_imag - mine_imag, time_imag + turned_imag) * 0.5
    half_turn = angles(seq_index, 2 * seq_count)
    conv_out = (
        time_real[0] + jnp.cos(half_turn) * time_real[1] - jnp.sin(half_turn) * time_imag[1]
    ) * (seq_count / period)
    long_mix = conv_out + skip_gain * signal
    gated_out = (short_mix[2] * long_mix).astype(jnp.bfloat16)
    partial_out = jnp.dot(gated_out, out_weight, preferred_element_type=jnp.float32)
    projected_out = lax.psum_scatter(partial_out, "chan", scatter_dimension=1, tiled=True)
    return tokens.astype(jnp.float32) + projected_out


def solution(mesh):
    return jax.shard_map(
        local,
        mesh=mesh,
        in_specs=(
            P("seq", "chan"),
            P(),
            P(None, None, "chan"),
            P(None, None, "chan"),
            P("seq", "chan"),
            P("seq", "chan"),
            P("chan"),
            P("chan", None),
        ),
        out_specs=P("seq", "chan"),
        check_vma=False,
    )
```

profile of v0, /device:TPU:1, one launch (start us, length us, event | category | flops | bytes accessed | tf_op | source)
XLA Modules:
  0.0 925.9 jit_solution(15624795669458705864)
XLA Ops:
  7.3 32.9 %all-gather.2.cloned.1.call-done = bf16[1024,1024]{1,0:T(8,128)(2,1)} async-done(((bf16[1024,128]{1,0:T(8,128)(2,1)}), bf16[1024,1024]{1,0:T(8,128)(2,1)}) %all-gather.2.cloned.1.call-update) | async-done | bytes 2097168 | tf_op jit(solution)/shard_map/all_gather | solution.py:78
  53.9 5.3 collective-permute-start.1
  61.3 65.2 %collective-permute-done.1 = f32[2,1024,384]{2,1,0:T(8,128)} collective-permute-done((f32[2,1024,384]{2,1,0:T(8,128)}, f32[2,1024,384]{2,1,0:T(8,128)}, u32[]{:S(2)}, u32[]{:S(2)}) %collective-permute-start.1) | collective-permute-done | bytes 3145760 | tf_op jit(solution)/shard_map/ppermute | solution.py:18
  126.5 67.4 %collective-permute-done.2 = f32[2,1024,384]{2,1,0:T(8,128)} collective-permute-done((f32[2,1024,384]{2,1,0:T(8,128)}, f32[2,1024,384]{2,1,0:T(8,128)}, u32[]{:S(2)}, u32[]{:S(2)}) %collective-permute-start.2) | collective-permute-done | bytes 3145760 | tf_op jit(solution)/shard_map/ppermute | solution.py:18
  193.9 5.5 add_select_fusion.6
  201.1 66.2 %collective-permute-done.3 = f32[2,1024,384]{2,1,0:T(8,128)} collective-permute-done((f32[2,1024,384]{2,1,0:T(8,128)}, f32[2,1024,384]{2,1,0:T(8,128)}, u32[]{:S(2)}, u32[]{:S(2)}) %collective-permute-start.3) | collective-permute-done | bytes 3145760 | tf_op jit(solution)/shard_map/ppermute | solution.py:18
  267.3 67.4 %collective-permute-done.4 = f32[2,1024,384]{2,1,0:T(8,128)} collective-permute-done((f32[2,1024,384]{2,1,0:T(8,128)}, f32[2,1024,384]{2,1,0:T(8,128)}, u32[]{:S(2)}, u32[]{:S(2)}) %collective-permute-start.4) | collective-permute-done | bytes 3145760 | tf_op jit(solution)/shard_map/ppermute | solution.py:18
  334.7 7.6 add_select_fusion.4
  345.4 65.3 %collective-permute-done.5 = f32[2,1024,384]{2,1,0:T(8,128)} collective-permute-done((f32[2,1024,384]{2,1,0:T(8,128)}, f32[2,1024,384]{2,1,0:T(8,128)}, u32[]{:S(2)}, u32[]{:S(2)}) %collective-permute-start.5) | collective-permute-done | bytes 3145760 | tf_op jit(solution)/shard_map/ppermute | solution.py:18
  410.7 67.4 %collective-permute-done.6 = f32[2,1024,384]{2,1,0:T(8,128)} collective-permute-done((f32[2,1024,384]{2,1,0:T(8,128)S(1)}, f32[2,1024,384]{2,1,0:T(8,128)}, u32[]{:S(2)}, u32[]{:S(2)}) %collective-permute-start.6) | collective-permute-done | bytes 3145760 | tf_op jit(solution)/shard_map/ppermute | solution.py:18
  478.1 7.7 add_select_fusion.2
  488.4 63.3 %collective-permute-done.7 = f32[2,1024,384]{2,1,0:T(8,128)S(1)} collective-permute-done((f32[2,1024,384]{2,1,0:T(8,128)}, f32[2,1024,384]{2,1,0:T(8,128)S(1)}, u32[]{:S(2)}, u32[]{:S(2)}) %collective-permute-start.7) | collective-permute-done | bytes 3145760 | tf_op jit(solution)/shard_map/ppermute | solution.py:18
  551.7 67.5 %collective-permute-done.8 = f32[2,1024,384]{2,1,0:T(8,128)} collective-permute-done((f32[2,1024,384]{2,1,0:T(8,128)}, f32[2,1024,384]{2,1,0:T(8,128)}, u32[]{:S(2)}, u32[]{:S(2)}) %collective-permute-start.8) | collective-permute-done | bytes 3145760 | tf_op jit(solution)/shard_map/ppermute | solution.py:18
  619.2 4.5 multiply_add_fusion
  624.9 4.9 fusion.17
  629.8 4.9 fusion.15
  634.8 5.1 fusion.26
  639.9 6.0 fusion.3
  645.9 5.2 fusion.7
  651.1 4.9 fusion.5
  656.0 5.0 subtract_bitcast_fusion
  663.2 5.0 add_bitcast_fusion
  689.7 18.4 %collective-permute-done.10 = f32[2,1024,128]{2,1,0:T(8,128)S(1)} collective-permute-done((f32[2,1024,128]{2,1,0:T(8,128)S(1)}, f32[2,1024,128]{2,1,0:T(8,128)S(1)}, u32[]{:S(2)}, u32[]{:S(2)}) %collective-permute-start.10) | collective-permute-done | bytes 1048608 | tf_op jit(solution)/shard_map/ppermute | solution.py:18
  708.0 22.5 %collective-permute-done.9 = f32[2,1024,128]{2,1,0:T(8,128)S(1)} collective-permute-done((f32[2,1024,128]{2,1,0:T(8,128)S(1)}, f32[2,1024,128]{2,1,0:T(8,128)S(1)}, u32[]{:S(2)}, u32[]{:S(2)}) %collective-permute-start.9) | collective-permute-done | bytes 1048608 | tf_op jit(solution)/shard_map/ppermute | solution.py:18
  735.5 16.1 %collective-permute-done.11 = f32[2,1024,128]{2,1,0:T(8,128)S(1)} collective-permute-done((f32[2,1024,128]{2,1,0:T(8,128)}, f32[2,1024,128]{2,1,0:T(8,128)S(1)}, u32[]{:S(2)}, u32[]{:S(2)}) %collective-permute-start.11) | collective-permute-done | bytes 1048608 | tf_op jit(solution)/shard_map/ppermute | solution.py:18
  751.6 22.6 %collective-permute-done.12 = f32[2,1024,128]{2,1,0:T(8,128)} collective-permute-done((f32[2,1024,128]{2,1,0:T(8,128)}, f32[2,1024,128]{2,1,0:T(8,128)}, u32[]{:S(2)}, u32[]{:S(2)}) %collective-permute-start.12) | collective-permute-done | bytes 1048608 | tf_op jit(solution)/shard_map/ppermute | solution.py:18
  779.4 15.2 %collective-permute-done.13 = f32[2,1024,128]{2,1,0:T(8,128)S(1)} collective-permute-done((f32[2,1024,128]{2,1,0:T(8,128)}, f32[2,1024,128]{2,1,0:T(8,128)S(1)}, u32[]{:S(2)}, u32[]{:S(2)}) %collective-permute-start.13) | collective-permute-done | bytes 1048608 | tf_op jit(solution)/shard_map/ppermute | solution.py:18
  794.6 22.5 %collective-permute-done.14 = f32[2,1024,128]{2,1,0:T(8,128)S(1)} collective-permute-done((f32[2,1024,128]{2,1,0:T(8,128)S(1)}, f32[2,1024,128]{2,1,0:T(8,128)S(1)}, u32[]{:S(2)}, u32[]{:S(2)}) %collective-permute-start.14) | collective-permute-done | bytes 1048608 | tf_op jit(solution)/shard_map/ppermute | solution.py:18
  825.4 14.0 %collective-permute-done.15 = f32[2,1024,128]{2,1,0:T(8,128)} collective-permute-done((f32[2,1024,128]{2,1,0:T(8,128)}, f32[2,1024,128]{2,1,0:T(8,128)}, u32[]{:S(2)}, u32[]{:S(2)}) %collective-permute-start.15) | collective-permute-done | bytes 1048608 | tf_op jit(solution)/shard_map/ppermute | solution.py:18
  839.4 22.5 %collective-permute-done.16 = f32[2,1024,128]{2,1,0:T(8,128)} collective-permute-done((f32[2,1024,128]{2,1,0:T(8,128)}, f32[2,1024,128]{2,1,0:T(8,128)}, u32[]{:S(2)}, u32[]{:S(2)}) %collective-permute-start.16) | collective-permute-done | bytes 1048608 | tf_op jit(solution)/shard_map/ppermute | solution.py:18
  863.8 4.4 fusion.76
  868.3 48.7 %reduce-scatter.2.cloned.1.call-done = f32[1024,128]{1,0:T(8,128)} async-done(((f32[1024,1024]{1,0:T(8,128)}), f32[1024,128]{1,0:T(8,128)}) %reduce-scatter.2.cloned.1.call-update) | async-done | bytes 524304 | tf_op jit(solution)/shard_map/reduce_scatter | solution.py:147
  (93 shorter events, 69.7 us)
Async XLA Ops:
  6.5 35.7 %copy-start = (bf16[3,1024,128]{2,1,0:T(8,128)(2,1)S(1)}, bf16[3,1024,128]{2,1,0:T(8,128)(2,1)}, u32[]{:S(2)}) copy-start(bf16[3,1024,128]{2,1,0:T(8,128)(2,1)} %param.10) | copy-start | bytes 2359300
  6.5 33.6 %all-gather.2.cloned.1.call-start = ((), (), s32[]{:S(2)}) async-start(), calls=%async_computation.1 | async-start | bytes 2359296 | tf_op jit(solution)/shard_map/all_gather | solution.py:78
  7.3 909.7 %reduce-scatter.2.cloned.1.call-start = ((), (), s32[]{:S(2)}) async-start(), calls=%async_computation.2 | async-start | bytes 4718592 | tf_op jit(solution)/shard_map/reduce_scatter | solution.py:147
  42.3 6.0 copy-start.12
  45.2 3.8 collective-permute-start
  49.0 1.7 copy-start.6
  49.0 1.7 copy-start.7
  49.5 1.1 copy-start.3
  50.8 1.2 copy-start.2
  53.9 72.6 %collective-permute-start.1 = (f32[2,1024,384]{2,1,0:T(8,128)}, f32[2,1024,384]{2,1,0:T(8,128)}, u32[]{:S(2)}, u32[]{:S(2)}) collective-permute-start(f32[2,1024,384]{2,1,0:T(8,128)} %pad_maximum_fusion), channel_id=1, source_target_pairs={{0,64},{8,72},{16,80},{24,88},{32,96},{40,104},{48,112},{56,120},{... | collective-permute-start | bytes 9437192 | tf_op jit(solution)/shard_map/ppermute | solution.py:18
  61.1 132.8 %collective-permute-start.2 = (f32[2,1024,384]{2,1,0:T(8,128)}, f32[2,1024,384]{2,1,0:T(8,128)}, u32[]{:S(2)}, u32[]{:S(2)}) collective-permute-start(f32[2,1024,384]{2,1,0:T(8,128)} %stack.13), channel_id=1, source_target_pairs={{0,64},{8,72},{16,80},{24,88},{32,96},{40,104},{48,112},{56,120},{... | collective-permute-start | bytes 9437192 | tf_op jit(solution)/shard_map/ppermute | solution.py:18
  199.4 67.9 %collective-permute-start.3 = (f32[2,1024,384]{2,1,0:T(8,128)}, f32[2,1024,384]{2,1,0:T(8,128)}, u32[]{:S(2)}, u32[]{:S(2)}) collective-permute-start(f32[2,1024,384]{2,1,0:T(8,128)} %get-tuple-element.28), channel_id=1, source_target_pairs={{0,32},{8,40},{16,48},{24,56},{32,0},{40,8},{48,16},{56,24},{64,96... | collective-permute-start | bytes 9437192 | tf_op jit(solution)/shard_map/ppermute | solution.py:18
  200.6 134.1 %collective-permute-start.4 = (f32[2,1024,384]{2,1,0:T(8,128)}, f32[2,1024,384]{2,1,0:T(8,128)}, u32[]{:S(2)}, u32[]{:S(2)}) collective-permute-start(f32[2,1024,384]{2,1,0:T(8,128)} %get-tuple-element.27), channel_id=1, source_target_pairs={{0,32},{8,40},{16,48},{24,56},{32,0},{40,8},{48,16},{56,24},{64,96... | collective-permute-start | bytes 9437192 | tf_op jit(solution)/shard_map/ppermute | solution.py:18
  342.3 68.4 %collective-permute-start.5 = (f32[2,1024,384]{2,1,0:T(8,128)}, f32[2,1024,384]{2,1,0:T(8,128)}, u32[]{:S(2)}, u32[]{:S(2)}) collective-permute-start(f32[2,1024,384]{2,1,0:T(8,128)} %get-tuple-element.26), channel_id=1, source_target_pairs={{0,16},{8,24},{16,0},{24,8},{32,48},{40,56},{48,32},{56,40},{64,80... | collective-permute-start | bytes 9437192 | tf_op jit(solution)/shard_map/ppermute | solution.py:18
  342.6 135.5 %collective-permute-start.6 = (f32[2,1024,384]{2,1,0:T(8,128)S(1)}, f32[2,1024,384]{2,1,0:T(8,128)}, u32[]{:S(2)}, u32[]{:S(2)}) collective-permute-start(f32[2,1024,384]{2,1,0:T(8,128)S(1)} %get-tuple-element.25), channel_id=1, source_target_pairs={{0,16},{8,24},{16,0},{24,8},{32,48},{40,56},{48,32},{56,40},{64,80... | collective-permute-start | bytes 9437192 | tf_op jit(solution)/shard_map/ppermute | solution.py:18
  485.8 65.9 %collective-permute-start.7 = (f32[2,1024,384]{2,1,0:T(8,128)}, f32[2,1024,384]{2,1,0:T(8,128)S(1)}, u32[]{:S(2)}, u32[]{:S(2)}) collective-permute-start(f32[2,1024,384]{2,1,0:T(8,128)} %get-tuple-element.24), channel_id=1, source_target_pairs={{0,8},{8,0},{16,24},{24,16},{32,40},{40,32},{48,56},{56,48},{64,72... | collective-permute-start | bytes 9437192 | tf_op jit(solution)/shard_map/ppermute | solution.py:18
  485.8 133.4 %collective-permute-start.8 = (f32[2,1024,384]{2,1,0:T(8,128)}, f32[2,1024,384]{2,1,0:T(8,128)}, u32[]{:S(2)}, u32[]{:S(2)}) collective-permute-start(f32[2,1024,384]{2,1,0:T(8,128)} %get-tuple-element.23), channel_id=1, source_target_pairs={{0,8},{8,0},{16,24},{24,16},{32,40},{40,32},{48,56},{56,48},{64,72... | collective-permute-start | bytes 9437192 | tf_op jit(solution)/shard_map/ppermute | solution.py:18
  688.1 19.9 %collective-permute-start.10 = (f32[2,1024,128]{2,1,0:T(8,128)S(1)}, f32[2,1024,128]{2,1,0:T(8,128)S(1)}, u32[]{:S(2)}, u32[]{:S(2)}) collective-permute-start(f32[2,1024,128]{2,1,0:T(8,128)S(1)} %get-tuple-element.40), channel_id=1, source_target_pairs={{0,8},{8,0},{16,24},{24,16},{32,40},{40,32},{48,56},{56,48},{64,72... | collective-permute-start | bytes 3145736 | tf_op jit(solution)/shard_map/ppermute | solution.py:18
  688.5 42.0 %collective-permute-start.9 = (f32[2,1024,128]{2,1,0:T(8,128)S(1)}, f32[2,1024,128]{2,1,0:T(8,128)S(1)}, u32[]{:S(2)}, u32[]{:S(2)}) collective-permute-start(f32[2,1024,128]{2,1,0:T(8,128)S(1)} %get-tuple-element.39), channel_id=1, source_target_pairs={{0,8},{8,0},{16,24},{24,16},{32,40},{40,32},{48,56},{56,48},{64,72... | collective-permute-start | bytes 3145736 | tf_op jit(solution)/shard_map/ppermute | solution.py:18
  732.4 19.2 %collective-permute-start.11 = (f32[2,1024,128]{2,1,0:T(8,128)}, f32[2,1024,128]{2,1,0:T(8,128)S(1)}, u32[]{:S(2)}, u32[]{:S(2)}) collective-permute-start(f32[2,1024,128]{2,1,0:T(8,128)} %get-tuple-element.13), channel_id=1, source_target_pairs={{0,16},{8,24},{16,0},{24,8},{32,48},{40,56},{48,32},{56,40},{64,80... | collective-permute-start | bytes 3145736 | tf_op jit(solution)/shard_map/ppermute | solution.py:18
  732.4 41.8 %collective-permute-start.12 = (f32[2,1024,128]{2,1,0:T(8,128)}, f32[2,1024,128]{2,1,0:T(8,128)}, u32[]{:S(2)}, u32[]{:S(2)}) collective-permute-start(f32[2,1024,128]{2,1,0:T(8,128)} %get-tuple-element.35), channel_id=1, source_target_pairs={{0,16},{8,24},{16,0},{24,8},{32,48},{40,56},{48,32},{56,40},{64,80... | collective-permute-start | bytes 3145736 | tf_op jit(solution)/shard_map/ppermute | solution.py:18
  751.6 22.6 %copy-start.8 = (f32[2,1024,128]{2,1,0:T(8,128)}, f32[2,1024,128]{2,1,0:T(8,128)S(1)}, u32[]{:S(2)}) copy-start(f32[2,1024,128]{2,1,0:T(8,128)S(1)} %collective-permute-done.11) | copy-start | bytes 3145732
  777.8 16.8 %collective-permute-start.13 = (f32[2,1024,128]{2,1,0:T(8,128)}, f32[2,1024,128]{2,1,0:T(8,128)S(1)}, u32[]{:S(2)}, u32[]{:S(2)}) collective-permute-start(f32[2,1024,128]{2,1,0:T(8,128)} %get-tuple-element.9), channel_id=1, source_target_pairs={{0,32},{8,40},{16,48},{24,56},{32,0},{40,8},{48,16},{56,24},{64,96... | collective-permute-start | bytes 3145736 | tf_op jit(solution)/shard_map/ppermute | solution.py:18
  777.8 39.3 %collective-permute-start.14 = (f32[2,1024,128]{2,1,0:T(8,128)S(1)}, f32[2,1024,128]{2,1,0:T(8,128)S(1)}, u32[]{:S(2)}, u32[]{:S(2)}) collective-permute-start(f32[2,1024,128]{2,1,0:T(8,128)S(1)} %get-tuple-element.33), channel_id=1, source_target_pairs={{0,32},{8,40},{16,48},{24,56},{32,0},{40,8},{48,16},{56,24},{64,96... | collective-permute-start | bytes 3145736 | tf_op jit(solution)/shard_map/ppermute | solution.py:18
  794.6 22.5 %copy-start.9 = (f32[2,1024,128]{2,1,0:T(8,128)}, f32[2,1024,128]{2,1,0:T(8,128)S(1)}, u32[]{:S(2)}) copy-start(f32[2,1024,128]{2,1,0:T(8,128)S(1)} %collective-permute-done.13) | copy-start | bytes 3145732
  817.0 1.0 copy-start.10
  822.3 41.5 %copy-start.5 = (f32[1,1024,128]{2,1,0:T(8,128)S(1)}, f32[1,1024,128]{2,1,0:T(8,128)}, u32[]{:S(2)}) copy-start(f32[1,1024,128]{2,1,0:T(8,128)} %copy-done.4) | copy-start | bytes 1572868
  822.3 41.5 %copy-start.13 = (f32[128]{0:T(128)S(1)}, f32[128]{0:T(128)}, u32[]{:S(2)}) copy-start(f32[128]{0:T(128)} %param.14) | copy-start | bytes 1540
  822.3 17.1 %collective-permute-start.15 = (f32[2,1024,128]{2,1,0:T(8,128)}, f32[2,1024,128]{2,1,0:T(8,128)}, u32[]{:S(2)}, u32[]{:S(2)}) collective-permute-start(f32[2,1024,128]{2,1,0:T(8,128)} %get-tuple-element.5), channel_id=1, source_target_pairs={{0,64},{8,72},{16,80},{24,88},{32,96},{40,104},{48,112},{56,120},{... | collective-permute-start | bytes 3145736 | tf_op jit(solution)/shard_map/ppermute | solution.py:18
  823.5 38.4 %collective-permute-start.16 = (f32[2,1024,128]{2,1,0:T(8,128)}, f32[2,1024,128]{2,1,0:T(8,128)}, u32[]{:S(2)}, u32[]{:S(2)}) collective-permute-start(f32[2,1024,128]{2,1,0:T(8,128)} %get-tuple-element.31), channel_id=1, source_target_pairs={{0,64},{8,72},{16,80},{24,88},{32,96},{40,104},{48,112},{56,120},{... | collective-permute-start | bytes 3145736 | tf_op jit(solution)/shard_map/ppermute | solution.py:18
  863.8 55.0 %copy-start.1 = (bf16[3,1024,128]{2,1,0:T(8,128)(2,1)S(1)}, bf16[3,1024,128]{2,1,0:T(8,128)(2,1)}, u32[]{:S(2)}) copy-start(bf16[3,1024,128]{2,1,0:T(8,128)(2,1)} %param.10) | copy-start | bytes 2359300
  868.3 48.7 %copy-start.11 = (bf16[1024,128]{1,0:T(8,128)(2,1)S(1)}, bf16[1024,128]{1,0:T(8,128)(2,1)}, u32[]{:S(2)}) copy-start(bf16[1024,128]{1,0:T(8,128)(2,1)} %param.8) | copy-start | bytes 786436
  (1 other events, 0.8 us)
Sparse Core Ops, SparseCore 0:
  9.0 31.0 all-gather.1
  868.4 48.4 reduce-scatter.1
where the time goes:
time: 936 us; the launch traced here: 926 us
  waiting for transfers between devices  766 us (82%)
  matrix products  62.7 us (7%)
  other arithmetic  47.9 us (5%)
  starting transfers between devices  23.3 us (2%)
  between operations  15.2 us (2%)
  local copies, waits for them, and re-layouts  10.5 us (1%)
    ppermute x16, waiting for transfers between devices, partner(): return lax.ppermute(value, axis, pairs)  683 us
    reduce_scatter x1, waiting for transfers between devices, local(): lax.psum_scatter(partial_out, 'chan', scatter_dimension=1, tiled=True)  48.7 us
    all_gather x1, waiting for transfers between devices, local(): full_rows = lax.all_gather(tokens, 'chan', axis=1, tiled=True)  32.9 us
    select_n x3, other arithmetic, local(): freq_imag = jnp.where(upper_half, diff_imag, freq_imag + partner_imag)  20.8 us
    ppermute x16, starting transfers between devices, partner(): return lax.ppermute(value, axis, pairs)  20.2 us
  transfers between devices with their start and end apart: 19, of which 19 were waited for; matrix products, arithmetic and copies ran while one was open for 0% of the time, Pallas kernels for 0%

commit v1 on v0

v1 whole, which is shorter than its diff:
```python
import functools

import jax
import jax.numpy as jnp
import ml_dtypes
import numpy as np
from jax import lax
from jax.experimental import pallas as pl
from jax.experimental.pallas import tpu as pltpu
from jax.sharding import PartitionSpec as P

HALO = 16
LANES = 128
VMEM_LIMIT = 56 * 1024 * 1024
VMEM = pl.BlockSpec(memory_space=pltpu.VMEM)
F32 = jnp.float32
BF16 = jnp.bfloat16


def params():
    return pltpu.CompilerParams(vmem_limit_bytes=VMEM_LIMIT)


def split_np(table):
    high = table.astype(np.float32).astype(ml_dtypes.bfloat16)
    low = (table - high.astype(np.float64)).astype(np.float32).astype(ml_dtypes.bfloat16)
    return high, low


@functools.cache
def tables():
    n = LANES
    period = 2 * n * n
    k = np.arange(n, dtype=np.float64)
    first = 2 * np.pi * np.outer(k + 0.5, k) / (2 * n)
    forward = np.concatenate([np.cos(first), -np.sin(first)], axis=0)
    backward = np.concatenate([np.cos(first).T, -np.sin(first).T], axis=1) * (2.0 / period)
    second = 2 * np.pi * np.outer(k, k) / n
    cosine, sine = np.cos(second), np.sin(second)
    mix = np.block([[cosine, -sine], [sine, cosine]])
    unmix = np.block([[cosine, sine], [-sine, cosine]])
    turn = 2 * np.pi * np.outer(k + 0.5, k) / period
    twiddle = np.stack([np.cos(turn), -np.sin(turn)]).astype(np.float32)
    step = 2 * np.pi * (k[:, None] + 0.5 + 2 * n * k[None, :]) / period
    ahead = np.stack([np.cos(step), np.sin(step)]).astype(np.float32)
    forward_hi, forward_lo = split_np(forward)
    backward_hi, backward_lo = split_np(backward)
    mix_hi, mix_lo = split_np(mix)
    unmix_hi, unmix_lo = split_np(unmix)
    return {
        "forward": np.concatenate([forward_hi, forward_lo, forward_hi], axis=1),
        "backward": np.concatenate([backward_hi, backward_lo, backward_hi], axis=1),
        "mix": np.concatenate([mix_hi, mix_lo], axis=0),
        "unmix": np.concatenate([unmix_hi, unmix_lo], axis=0),
        "twiddle": twiddle,
        "ahead": ahead,
    }


def halves(value):
    high = value.astype(BF16)
    return high, (value - high.astype(F32)).astype(BF16)


def dot(left, right):
    return jnp.dot(left, right, preferred_element_type=F32)


def left_dot(table, value):
    high, low = halves(value)
    return dot(table, jnp.concatenate([high, high, low], axis=0))


def right_dot(value, table_ref):
    high, low = halves(value)
    depth = value.shape[1]
    table_hi = table_ref[:depth]
    return dot(jnp.concatenate([high, low, high], axis=1), jnp.concatenate([table_hi, table_hi, table_ref[depth:]], axis=0))


def transform(pair, forward_ref, mix_ref, twiddle_ref):
    n = LANES
    parts = left_dot(forward_ref[...], jnp.concatenate(pair, axis=1))
    cosine, sine = twiddle_ref[0], twiddle_ref[1]
    rows = []
    for i in range(2):
        real = parts[:n, i * n : (i + 1) * n]
        imag = parts[n:, i * n : (i + 1) * n]
        rows.append(jnp.concatenate([real * cosine - imag * sine, real * sine + imag * cosine], axis=1))
    return right_dot(jnp.concatenate(rows, axis=0), mix_ref)


def spread_kernel(fwd_ref, bwd_ref, out_ref):
    for which, source in enumerate((fwd_ref, bwd_ref)):
        for block in range(source.shape[0] // LANES):
            turned = source[block * LANES : (block + 1) * LANES, :].T
            out_ref[which, pl.ds(block, LANES, stride=8), :] = turned


def filter_kernel(skip_ref, filt_ref, forward_ref, mix_ref, twiddle_ref, ahead_ref, gain_ref):
    n = LANES
    for c in range(8):
        pair = [filt_ref[which, :, c].reshape(n, n) for which in range(2)]
        spectra = transform(pair, forward_ref, mix_ref, twiddle_ref)
        back_real, back_imag = spectra[n:, :n], -spectra[n:, n:]
        cosine, sine = ahead_ref[0], ahead_ref[1]
        gain_ref[c, 0] = spectra[:n, :n] + (back_real * cosine - back_imag * sine) + skip_ref[c]
        gain_ref[c, 1] = spectra[:n, n:] + (back_real * sine + back_imag * cosine)


def conv_kernel(sig_ref, gain_ref, forward_ref, mix_ref, unmix_ref, backward_ref, twiddle_ref, out_ref):
    n = LANES
    cosine, sine = twiddle_ref[0], twiddle_ref[1]
    for c in range(0, 8, 2):
        pair = [sig_ref[:, c + i].reshape(n, n) for i in range(2)]
        spectra = transform(pair, forward_ref, mix_ref, twiddle_ref)
        rows = []
        for i in range(2):
            real, imag = spectra[i * n : (i + 1) * n, :n], spectra[i * n : (i + 1) * n, n:]
            gain_real, gain_imag = gain_ref[c + i, 0], gain_ref[c + i, 1]
            rows.append(
                jnp.concatenate(
                    [real * gain_real - imag * gain_imag, real * gain_imag + imag * gain_real], axis=1
                )
            )
        parts = right_dot(jnp.concatenate(rows, axis=0), unmix_ref)
        columns = []
        for i in range(2):
            real, imag = parts[i * n : (i + 1) * n, :n], parts[i * n : (i + 1) * n, n:]
            columns.append(
                jnp.concatenate([real * cosine + imag * sine, imag * cosine - real * sine], axis=0)
            )
        times = left_dot(backward_ref[...], jnp.concatenate(columns, axis=1))
        for i in range(2):
            out_ref[:, c + i] = times[:, i * n : (i + 1) * n].reshape(16, 8, n)


def project_kernel(tokens_ref, gain_ref, weight_ref, short_ref, signal_ref, gate_ref, projected_ref):
    count, rows, width = tokens_ref.shape
    weight = jnp.concatenate([weight_ref[j] for j in range(3)], axis=1)
    starts = [0] + [HALO + LANES * i for i in range((rows - HALO) // LANES)]
    for start in starts:
        size = HALO if start == 0 else LANES
        pieces = [tokens_ref[j, start : start + size, :].astype(F32) for j in range(count)]
        total = sum(jnp.sum(piece * piece, axis=1, keepdims=True) for piece in pieces)
        inv_rms = lax.rsqrt(total * (1.0 / (count * width)) + 1e-05)
        normed = jnp.concatenate(
            [(pieces[j] * inv_rms * gain_ref[j : j + 1, :]).astype(BF16) for j in range(count)], axis=1
        )
        projected_ref[start : start + size, :] = dot(normed, weight)
        if start == 0:
            continue
        mixes = []
        for j in range(3):
            columns = slice(j * LANES, (j + 1) * LANES)
            mixes.append(
                sum(
                    short_ref[i, j : j + 1, :] * projected_ref[start - i : start - i + size, columns]
                    for i in range(3)
                )
            )
        block = (start - HALO) // LANES
        signal_ref[pl.ds(block, LANES, stride=8), :] = (mixes[0] * mixes[1]).T
        gate_ref[start - HALO : start - HALO + size, :] = mixes[2]


def gate_kernel(conv_ref, gate_ref, out_ref):
    for block in range(gate_ref.shape[0] // LANES):
        rows = slice(block * LANES, (block + 1) * LANES)
        conv = conv_ref[pl.ds(block, LANES, stride=8), :].T
        out_ref[rows, :] = (gate_ref[rows, :] * conv).astype(BF16)


def output_kernel(index_ref, gated_ref, weight_ref, tokens_ref, out_ref):
    columns = pl.ds(pl.multiple_of(index_ref[0] * LANES, LANES), LANES)
    count, rows, _ = gated_ref.shape
    weight = weight_ref[:, columns]
    for start in range(0, rows, 256):
        gated = jnp.concatenate([gated_ref[j, start : start + 256, :] for j in range(count)], axis=1)
        out_ref[start : start + 256, :] = tokens_ref[start : start + 256, :].astype(F32) + dot(gated, weight)


def local(tokens, norm_gain, in_weight, short_kernel, filter_fwd, filter_bwd, skip_gain, out_weight):
    seq_count = lax.axis_size("seq")
    seq_index = lax.axis_index("seq")
    chan_index = lax.axis_index("chan")
    block_rows, width = tokens.shape
    table = {name: jnp.asarray(value) for name, value in tables().items()}

    halo = lax.ppermute(tokens[block_rows - HALO :], "seq", [(i, i + 1) for i in range(seq_count - 1)])
    gathered = lax.all_gather(jnp.concatenate([halo, tokens], axis=0), "chan", axis=0)
    weights = lax.all_gather(out_weight, "chan", axis=0, tiled=True)

    spread = pl.pallas_call(
        spread_kernel,
        out_shape=jax.ShapeDtypeStruct((2, block_rows, width), F32),
        in_specs=[VMEM] * 2,
        out_specs=VMEM,
        compiler_params=params(),
    )(filter_fwd, filter_bwd)
    filters = lax.all_to_all(spread.reshape(2, seq_count, 8, 8, width), "seq", 1, 1)
    my_skip = lax.dynamic_slice(skip_gain, (seq_index * 8,), (8,))
    gain = pl.pallas_call(
        filter_kernel,
        out_shape=jax.ShapeDtypeStruct((8, 2, LANES, LANES), F32),
        in_specs=[pl.BlockSpec(memory_space=pltpu.SMEM)] + [VMEM] * 5,
        out_specs=VMEM,
        compiler_params=params(),
    )(my_skip, filters, table["forward"], table["mix"], table["twiddle"], table["ahead"])

    signal, gate = pl.pallas_call(
        project_kernel,
        out_shape=(
            jax.ShapeDtypeStruct((block_rows, width), F32),
            jax.ShapeDtypeStruct((block_rows, width), F32),
        ),
        in_specs=[VMEM] * 4,
        out_specs=(VMEM, VMEM),
        scratch_shapes=[pltpu.VMEM((block_rows + HALO, 3 * width), F32)],
        compiler_params=params(),
    )(gathered, norm_gain.reshape(-1, width), in_weight, short_kernel)

    signal = lax.all_to_all(signal.reshape(seq_count, 8, 8, width), "seq", 0, 0)
    conv = pl.pallas_call(
        conv_kernel,
        out_shape=jax.ShapeDtypeStruct((seq_count, 8, 8, width), F32),
        in_specs=[VMEM] * 7,
        out_specs=VMEM,
        compiler_params=params(),
    )(signal, gain, table["forward"], table["mix"], table["unmix"], table["backward"], table["twiddle"])
    conv = lax.all_to_all(conv, "seq", 0, 0)
    gated = pl.pallas_call(
        gate_kernel,
        out_shape=jax.ShapeDtypeStruct((block_rows, width), BF16),
        in_specs=[VMEM] * 2,
        out_specs=VMEM,
        compiler_params=params(),
    )(conv.reshape(block_rows, width), gate)
    all_gated = lax.all_gather(gated, "chan", axis=0)
    return pl.pallas_call(
        output_kernel,
        out_shape=jax.ShapeDtypeStruct((block_rows, width), F32),
        in_specs=[pl.BlockSpec(memory_space=pltpu.SMEM)] + [VMEM] * 3,
        out_specs=VMEM,
        compiler_params=params(),
    )(chan_index.reshape(1), all_gated, weights, tokens)


def solution(mesh):
    return jax.shard_map(
        local,
        mesh=mesh,
        in_specs=(
            P("seq", "chan"),
            P(),
            P(None, None, "chan"),
            P(None, None, "chan"),
            P("seq", "chan"),
            P("seq", "chan"),
            P("chan"),
            P("chan", None),
        ),
        out_specs=P("seq", "chan"),
        check_vma=False,
    )
```

time: 936 us -> 124 us (0.13); the launches traced: 926 us -> 124 us
  waiting for transfers between devices: 766 us -> 48.1 us
  matrix products: 62.7 us -> 0 us
  other arithmetic: 47.9 us -> 1.67 us
  Pallas kernels: 0 us -> 24.1 us
  blocking collectives: 0 us -> 13.4 us
    ppermute x17 -> x1, waiting for transfers between devices: 684 us -> 0.74 us  [local(): lax.ppermute(tokens[block_rows - HALO:], 'seq', [(i, i + 1) for i in rang...]
    dot_general x18 -> x0, matrix products: 62.7 us -> none  [the longest x2 7.7 us: local_dft(): jnp.einsum('pa,zabc->zpbc', cos_first, imag_four, precision=HIGHEST)]
    reduce_scatter x1 -> x0, waiting for transfers between devices: 48.7 us -> none  [local(): lax.psum_scatter(partial_out, 'chan', scatter_dimension=1, tiled=True)]
    pallas_call x0 -> x6, Pallas kernels: none -> 24.1 us  [the longest x1 6.31 us: local(): pl.pallas_call(conv_kernel, out_shape=jax.ShapeDtypeStruct((seq_count, 8,...]
    select_n x3 -> x0, other arithmetic: 20.8 us -> none  [local(): freq_imag = jnp.where(upper_half, diff_imag, freq_imag + partner_imag)]
    ppermute x17 -> x1, starting transfers between devices: 23.3 us -> 4.02 us  [local(): lax.ppermute(tokens[block_rows - HALO:], 'seq', [(i, i + 1) for i in rang...]
    all_to_all x0 -> x2, starting transfers between devices: none -> 13.7 us  [the longest x1 7.16 us: local(): lax.all_to_all(spread.reshape(2, seq_count, 8, 8, width), 'seq', 1, 1)]
    all_to_all x0 -> x1, blocking collectives: none -> 13.4 us  [local(): conv = lax.all_to_all(conv, 'seq', 0, 0)]
  transfers between devices with their start and end apart: 19 -> 6, of which waited for: 19 -> 4; matrix products, arithmetic and copies ran while one was open for 0% -> 3% of each run, Pallas kernels for 0% -> 16%
where the time goes in v1:
time: 124 us
  waiting for transfers between devices  48.1 us (39%)
  Pallas kernels  24.1 us (19%)
  starting transfers between devices  17.8 us (14%)
  blocking collectives  13.4 us (11%)
  between operations  13.2 us (11%)
  local copies, waits for them, and re-layouts  5.45 us (4%)
  other arithmetic  1.67 us (1%)
    all_gather x1, waiting for transfers between devices, local(): all_gated = lax.all_gather(gated, 'chan', axis=0)  25.6 us
    all_gather x1, waiting for transfers between devices, local(): lax.all_gather(jnp.concatenate([halo, tokens], axis=0), 'chan', axis=0)  17.1 us
    all_to_all x1, blocking collectives, local(): conv = lax.all_to_all(conv, 'seq', 0, 0)  13.4 us
    all_to_all x1, starting transfers between devices, local(): lax.all_to_all(spread.reshape(2, seq_count, 8, 8, width), 'seq', 1, 1)  7.16 us
    all_to_all x1, starting transfers between devices, local(): signal = lax.all_to_all(signal.reshape(seq_count, 8, 8, width), 'seq', 0, 0)  6.53 us
    pallas_call x1, Pallas kernels, local(): pl.pallas_call(conv_kernel, out_shape=jax.ShapeDtypeStruct((seq_count, 8,...  6.31 us
    pallas_call x1, Pallas kernels, local(): pl.pallas_call(filter_kernel, out_shape=jax.ShapeDtypeStruct((8, 2, LANES...  4.68 us
    pallas_call x1, Pallas kernels, local(): pl.pallas_call(project_kernel, out_shape=(jax.ShapeDtypeStruct((block_row...  4.66 us
  transfers between devices with their start and end apart: 6, of which 4 were waited for; matrix products, arithmetic and copies ran while one was open for 3% of the time, Pallas kernels for 16%

profile of v1, /device:TPU:1, one launch (start us, length us, event | category | flops | bytes accessed | tf_op | source)
XLA Modules:
  0.0 123.7 jit_solution(13632554502292420119)
XLA Ops:
  6.5 0.0 all-gather.8.cloned.1.call-start
  6.5 0.7 slice.3
  7.2 4.0 %collective-permute-start = (bf16[16,128]{1,0:T(8,128)(2,1)S(1)}, bf16[16,128]{1,0:T(8,128)(2,1)S(1)}, u32[]{:S(2)}, u32[]{:S(2)}) collective-permute-start(bf16[16,128]{1,0:T(8,128)(2,1)S(1)} %slice.3), channel_id=1, source_target_pairs={{0,8},{8,16},{16,24},{24,32},{32,40},{40,48},{48,56},{56,64},{64,7... | collective-permute-start | bytes 12296 | tf_op jit(solution)/shard_map/ppermute | solution.py:190
  11.3 0.7 collective-permute-done
  12.0 1.7 %pad_maximum_fusion = bf16[1040,128]{1,0:T(8,128)(2,1)} fusion(bf16[1024,128]{1,0:T(8,128)(2,1)} %tokens_ref.1, bf16[16,128]{1,0:T(8,128)(2,1)S(1)} %collective-permute-done), kind=kLoop, calls=%fused_computation | loop fusion | flops 532480 | bytes 532480 | tf_op jit(solution)/shard_map/concatenate | solution.py:191
  13.7 0.0 all-gather.8.cloned.1.call-update
  13.7 0.0 all-gather.6.cloned.1.call-start
  13.7 0.7 all-gather.6.cloned.1.call-update
  14.4 2.6 %shard_map.137 = f32[2,1024,128]{2,1,0:T(8,128)} custom-call(f32[1024,128]{1,0:T(8,128)} %fwd_ref.1, f32[1024,128]{1,0:T(8,128)} %bwd_ref.1), custom_call_target="tpu_custom_call" | custom-call | tf_op jit(solution)/shard_map/pallas_call | solution.py:194
  17.0 2.3 %copy.15 = f32[2,16,8,8,128]{4,3,2,0,1:T(8,128)} copy(f32[2,16,8,8,128]{4,3,2,1,0:T(8,128)} %bitcast.7) | data formatting | bytes 2097152 | tf_op jit(solution)/shard_map/reshape | solution.py:201
  19.3 7.2 %all-to-all-start.1 = ((f32[2,16,8,8,128]{4,3,2,0,1:T(8,128)}), f32[2,16,8,8,128]{4,3,2,0,1:T(8,128)S(1)}, u32[]{:S(2)}, u32[]{:S(2)}) async-start(f32[2,16,8,8,128]{4,3,2,0,1:T(8,128)} %copy.15), calls=%async_computation.1 | async-start | bytes 2097152 | tf_op jit(solution)/shard_map/all_to_all | solution.py:201
  26.5 0.0 copy-start.1
  26.5 17.1 %all-gather.8.cloned.1.call-done = bf16[8320,128]{1,0:T(8,128)(2,1)} async-done(((bf16[1040,128]{1,0:T(8,128)(2,1)}), bf16[8320,128]{1,0:T(8,128)(2,1)}) %all-gather.8.cloned.1.call-update) | async-done | bytes 2129936 | tf_op jit(solution)/shard_map/all_gather | solution.py:191
  43.6 4.7 %shard_map.136 = (f32[1024,128]{1,0:T(8,128)}, f32[1024,128]{1,0:T(8,128)}) custom-call(bf16[8,1040,128]{2,1,0:T(8,128)(2,1)} %bitcast.8, f32[8,128]{1,0:T(8,128)} %bitcast.12, bf16[3,1024,128]{2,1,0:T(8,128)(2,1)} %weight_ref.1, f32[3,3,128]{2,1,0:T(4,128)} %short_ref.1), custom_call_target="tpu_custom_call" | custom-call | tf_op jit(solution)/shard_map/pallas_call | solution.py:211
  48.3 0.0 all-to-all-done.1
  48.3 6.5 %all-to-all-start = ((f32[16,8,8,128]{3,2,1,0:T(8,128)}), f32[16,8,8,128]{3,2,1,0:T(8,128)S(1)}, u32[]{:S(2)}, u32[]{:S(2)}) async-start(f32[16,8,8,128]{3,2,1,0:T(8,128)} %bitcast.11), calls=%async_computation | async-start | bytes 1048576 | tf_op jit(solution)/shard_map/all_to_all | solution.py:223
  54.8 0.0 all-gather.10.cloned.1.call-start
  54.9 0.0 copy-done.1
  54.9 0.6 dynamic_slice.3.skip_ref
  55.5 1.1 copy.16.filt_ref
  56.5 4.7 %shard_map.138.gain_ref = f32[8,2,128,128]{3,2,1,0:T(8,128)} custom-call(f32[8]{0:T(128)} %dynamic_slice.3.skip_ref, f32[2,16,8,8,128]{4,3,2,1,0:T(8,128)} %copy.16.filt_ref, bf16[256,384]{1,0:T(8,128)(2,1)} %constant.27.clone.forward_ref, bf16[512,256]{1,0:T(8,128)(2,1)} %constant.29.clone.mix_ref, f32[2,128,128]{2,1,0:T(8,128)} %constant.31.clone.twiddle_ref, ...), custom_call_target="tpu_custom_call" | custom-call | tf_op jit(solution)/shard_map/pallas_call | solution.py:203
  61.2 3.9 %all-to-all-done.sig_ref = f32[16,8,8,128]{3,2,1,0:T(8,128)S(1)} async-done(((f32[16,8,8,128]{3,2,1,0:T(8,128)}), f32[16,8,8,128]{3,2,1,0:T(8,128)S(1)}, u32[]{:S(2)}, u32[]{:S(2)}) %all-to-all-start) | async-done | bytes 524320 | tf_op jit(solution)/shard_map/all_to_all | solution.py:223
  65.1 0.0 copy-start
  65.1 0.8 copy-done
  65.9 6.3 %shard_map.139 = f32[16,8,8,128]{3,2,1,0:T(8,128)} custom-call(f32[16,8,8,128]{3,2,1,0:T(8,128)} %copy-done, f32[8,2,128,128]{3,2,1,0:T(8,128)} %shard_map.138.gain_ref, bf16[256,384]{1,0:T(8,128)(2,1)} %constant.27.clone.forward_ref, bf16[512,256]{1,0:T(8,128)(2,1)} %constant.29.clone.mix_ref, bf16[512,256]{1,0:T(8,128)(2,1)} %constant.30.clone.unmix_ref, ...), custom_call_target="tpu_custom_call" | custom-call | tf_op jit(solution)/shard_map/pallas_call | solution.py:224
  72.2 13.4 %all_to_all.15 = f32[16,8,8,128]{3,2,1,0:T(8,128)} all-to-all(f32[16,8,8,128]{3,2,1,0:T(8,128)} %shard_map.139), channel_id=1, replica_groups=mesh['seq'=16,'chan'=8] {'seq'}, dimensions={0} | all-to-all | bytes 1048576 | tf_op jit(solution)/shard_map/all_to_all | solution.py:231
  85.7 2.1 %shard_map.140 = bf16[1024,128]{1,0:T(8,128)(2,1)} custom-call(f32[1024,128]{1,0:T(8,128)} %bitcast.10, f32[1024,128]{1,0:T(8,128)} %get-tuple-element.8.gate_ref), custom_call_target="tpu_custom_call" | custom-call | tf_op jit(solution)/shard_map/pallas_call | solution.py:232
  87.8 0.0 all-gather.10.cloned.1.call-update
  87.8 0.0 all-gather.6.cloned.1.call-done.weight_ref
  87.8 25.6 %all-gather.10.cloned.1.call-done = bf16[8192,128]{1,0:T(8,128)(2,1)} async-done(((bf16[1024,128]{1,0:T(8,128)(2,1)}), bf16[8192,128]{1,0:T(8,128)(2,1)}) %all-gather.10.cloned.1.call-update) | async-done | bytes 2097168 | tf_op jit(solution)/shard_map/all_gather | solution.py:239
  113.4 3.7 %shard_map.141 = f32[1024,128]{1,0:T(8,128)} custom-call(s32[1]{0:T(128)} %bitcast.index_ref, bf16[8,1024,128]{2,1,0:T(8,128)(2,1)} %bitcast.9, bf16[1024,1024]{1,0:T(8,128)(2,1)} %all-gather.6.cloned.1.call-done.weight_ref, bf16[1024,128]{1,0:T(8,128)(2,1)} %tokens_ref.1), custom_call_target="tpu_custom_call" | custom-call | tf_op jit(solution)/shard_map/pallas_call | solution.py:240
Async XLA Ops:
  6.5 37.1 %all-gather.8.cloned.1.call-start = ((), (), s32[]{:S(2)}) async-start(), calls=%async_computation.4 | async-start | bytes 2396160 | tf_op jit(solution)/shard_map/all_gather | solution.py:191
  7.2 4.8 %collective-permute-start = (bf16[16,128]{1,0:T(8,128)(2,1)S(1)}, bf16[16,128]{1,0:T(8,128)(2,1)S(1)}, u32[]{:S(2)}, u32[]{:S(2)}) collective-permute-start(bf16[16,128]{1,0:T(8,128)(2,1)S(1)} %slice.3), channel_id=1, source_target_pairs={{0,8},{8,16},{16,24},{24,32},{32,40},{40,48},{48,56},{56,64},{64,7... | collective-permute-start | bytes 12296 | tf_op jit(solution)/shard_map/ppermute | solution.py:190
  13.7 74.2 %all-gather.6.cloned.1.call-start = ((), (), s32[]{:S(2)}) async-start(), calls=%async_computation.3 | async-start | bytes 2359296 | tf_op jit(solution)/shard_map/all_gather | solution.py:192
  19.3 29.0 %all-to-all-start.1 = ((f32[2,16,8,8,128]{4,3,2,0,1:T(8,128)}), f32[2,16,8,8,128]{4,3,2,0,1:T(8,128)S(1)}, u32[]{:S(2)}, u32[]{:S(2)}) async-start(f32[2,16,8,8,128]{4,3,2,0,1:T(8,128)} %copy.15), calls=%async_computation.1 | async-start | bytes 2097152 | tf_op jit(solution)/shard_map/all_to_all | solution.py:201
  26.5 28.4 %copy-start.1 = (f32[128]{0:T(128)S(1)}, f32[128]{0:T(128)}, u32[]{:S(2)}) copy-start(f32[128]{0:T(128)} %param.20) | copy-start | bytes 1540
  48.3 16.8 %all-to-all-start = ((f32[16,8,8,128]{3,2,1,0:T(8,128)}), f32[16,8,8,128]{3,2,1,0:T(8,128)S(1)}, u32[]{:S(2)}, u32[]{:S(2)}) async-start(f32[16,8,8,128]{3,2,1,0:T(8,128)} %bitcast.11), calls=%async_computation | async-start | bytes 1048576 | tf_op jit(solution)/shard_map/all_to_all | solution.py:223
  54.8 58.6 %all-gather.10.cloned.1.call-start = ((), (), s32[]{:S(2)}) async-start(), calls=%async_computation.5 | async-start | bytes 2359296 | tf_op jit(solution)/shard_map/all_gather | solution.py:239
  65.1 0.8 copy-start
Sparse Core Ops, SparseCore 0:
  13.8 29.7 all-gather.7
  45.3 25.7 all-gather.5
  87.9 25.4 all-gather.9

commit v2 on v1

v2 whole, which is shorter than its diff:
```python
import functools

import jax
import jax.numpy as jnp
import ml_dtypes
import numpy as np
from jax import lax
from jax.experimental import pallas as pl
from jax.experimental.pallas import tpu as pltpu
from jax.sharding import PartitionSpec as P

HALO = 16
PROJECT_FLOPS = 6 * 10**9
LANES = 128
VMEM_LIMIT = 16 * 1024 * 1024
VMEM = pl.BlockSpec(memory_space=pltpu.VMEM)
F32 = jnp.float32
BF16 = jnp.bfloat16


def split_np(table):
    high = table.astype(np.float32).astype(ml_dtypes.bfloat16)
    low = (table - high.astype(np.float64)).astype(np.float32).astype(ml_dtypes.bfloat16)
    return high, low


@functools.cache
def tables():
    n = LANES
    period = 2 * n * n
    k = np.arange(n, dtype=np.float64)
    first = 2 * np.pi * np.outer(k + 0.5, k) / (2 * n)
    forward = np.concatenate([np.cos(first), -np.sin(first)], axis=0)
    backward = np.concatenate([np.cos(first).T, -np.sin(first).T], axis=1) * (2.0 / period)
    second = 2 * np.pi * np.outer(k, k) / n
    cosine, sine = np.cos(second), np.sin(second)
    mix = np.block([[cosine, -sine], [sine, cosine]])
    unmix = np.block([[cosine, sine], [-sine, cosine]])
    turn = 2 * np.pi * np.outer(k + 0.5, k) / period
    twiddle = np.stack([np.cos(turn), -np.sin(turn)]).astype(np.float32)
    step = 2 * np.pi * (k[:, None] + 0.5 + 2 * n * k[None, :]) / period
    ahead = np.stack([np.cos(step), np.sin(step)]).astype(np.float32)
    forward_hi, forward_lo = split_np(forward)
    backward_hi, backward_lo = split_np(backward)
    mix_hi, mix_lo = split_np(mix)
    unmix_hi, unmix_lo = split_np(unmix)
    return {
        "forward": np.concatenate([forward_hi, forward_lo, forward_hi], axis=1),
        "backward": np.concatenate([backward_hi, backward_lo, backward_hi], axis=1),
        "mix": np.concatenate([mix_hi, mix_lo], axis=0),
        "unmix": np.concatenate([unmix_hi, unmix_lo], axis=0),
        "twiddle": twiddle,
        "ahead": ahead,
    }


def halves(value):
    high = value.astype(BF16)
    return high, (value - high.astype(F32)).astype(BF16)


def dot(left, right):
    return jnp.dot(left, right, preferred_element_type=F32)


def left_dot(table, value):
    high, low = halves(value)
    return dot(table, jnp.concatenate([high, high, low], axis=0))


def right_dot(value, table_ref):
    high, low = halves(value)
    depth = value.shape[1]
    table_hi = table_ref[:depth]
    return dot(jnp.concatenate([high, low, high], axis=1), jnp.concatenate([table_hi, table_hi, table_ref[depth:]], axis=0))


def transform(pair, forward_ref, mix_ref, twiddle_ref):
    n = LANES
    parts = left_dot(forward_ref[...], jnp.concatenate(pair, axis=1))
    cosine, sine = twiddle_ref[0], twiddle_ref[1]
    rows = []
    for i in range(2):
        real = parts[:n, i * n : (i + 1) * n]
        imag = parts[n:, i * n : (i + 1) * n]
        rows.append(jnp.concatenate([real * cosine - imag * sine, real * sine + imag * cosine], axis=1))
    return right_dot(jnp.concatenate(rows, axis=0), mix_ref)


def spread_kernel(fwd_ref, bwd_ref, out_ref):
    for which, source in enumerate((fwd_ref, bwd_ref)):
        for block in range(source.shape[0] // LANES):
            turned = source[block * LANES : (block + 1) * LANES, :].T
            for d in range(16):
                out_ref[d, which, pl.ds(block, 8, stride=8), :] = turned[d * 8 : (d + 1) * 8, :]


def filter_kernel(skip_ref, filt_ref, forward_ref, mix_ref, twiddle_ref, ahead_ref, gain_ref):
    n = LANES
    for c in range(8):
        pair = [filt_ref[:, which, c].reshape(n, n) for which in range(2)]
        spectra = transform(pair, forward_ref, mix_ref, twiddle_ref)
        back_real, back_imag = spectra[n:, :n], -spectra[n:, n:]
        cosine, sine = ahead_ref[0], ahead_ref[1]
        gain_ref[c, 0] = spectra[:n, :n] + (back_real * cosine - back_imag * sine) + skip_ref[c]
        gain_ref[c, 1] = spectra[:n, n:] + (back_real * sine + back_imag * cosine)


def conv_kernel(sig_ref, gain_ref, forward_ref, mix_ref, unmix_ref, backward_ref, twiddle_ref, out_ref):
    n = LANES
    cosine, sine = twiddle_ref[0], twiddle_ref[1]
    extra = sig_ref[:, 8]
    before = jnp.concatenate([jnp.zeros((1, 8, n), F32), extra[:-1]], axis=0).reshape(n, n)
    mixes = extra.reshape(n, n) + pltpu.roll(before, n - 4, 1)
    first = (mixes * pltpu.roll(mixes, n - 2, 1)).reshape(16, 8, n)
    at_first = jnp.logical_and(
        lax.broadcasted_iota(jnp.int32, (16, 8, n), 1) == 0, lax.broadcasted_iota(jnp.int32, (16, 8, n), 2) < 2
    )
    for c in range(0, 8, 2):
        pair = [
            jnp.where(at_first, first[:, c + i : c + i + 1, :], sig_ref[:, c + i]).reshape(n, n) for i in range(2)
        ]
        spectra = transform(pair, forward_ref, mix_ref, twiddle_ref)
        rows = []
        for i in range(2):
            real, imag = spectra[i * n : (i + 1) * n, :n], spectra[i * n : (i + 1) * n, n:]
            gain_real, gain_imag = gain_ref[c + i, 0], gain_ref[c + i, 1]
            rows.append(
                jnp.concatenate(
                    [real * gain_real - imag * gain_imag, real * gain_imag + imag * gain_real], axis=1
                )
            )
        parts = right_dot(jnp.concatenate(rows, axis=0), unmix_ref)
        columns = []
        for i in range(2):
            real, imag = parts[i * n : (i + 1) * n, :n], parts[i * n : (i + 1) * n, n:]
            columns.append(
                jnp.concatenate([real * cosine + imag * sine, imag * cosine - real * sine], axis=0)
            )
        times = left_dot(backward_ref[...], jnp.concatenate(columns, axis=1))
        for i in range(2):
            out_ref[:, c + i] = times[:, i * n : (i + 1) * n].reshape(16, 8, n)


def piece_block(j, z, core):
    return (z + 4 - j % 4) % 4 * 2 + (core if j < 4 else 1 - core)


def project_kernel(index_ref, *refs):
    pieces = refs[:8]
    gain_ref, weight_ref, short_ref, message_ref, gate_ref, late_ref, projected_ref, stacked_ref = refs[8:]
    rows, width = pieces[0].shape
    z, core = index_ref[0] // 2, index_ref[0] % 2
    gains = []
    for j in range(8):
        block = piece_block(j, z, core)
        gains.append(gain_ref[pl.ds(block, 1), :])
        source = pl.ds(pl.multiple_of(block * width, width), width)
        for k in range(3):
            stacked_ref[j * width : (j + 1) * width, k * width : (k + 1) * width] = weight_ref[k, source, :]
    projected_ref[:HALO, :] = jnp.zeros((HALO, 3 * width), F32)
    step = 256
    for start in range(0, rows, step):
        parts = [piece[start : start + step, :].astype(F32) for piece in pieces]
        total = sum(part * part for part in parts)
        inv_rms = lax.rsqrt(jnp.sum(total, axis=1, keepdims=True) * (1.0 / (8 * width)) + 1e-05)
        normed = jnp.concatenate([(part * inv_rms * gain).astype(BF16) for part, gain in zip(parts, gains)], axis=1)
        projected_ref[HALO + start : HALO + start + step, :] = dot(normed, stacked_ref[...])
    taps = [[short_ref[i, j : j + 1, :] for j in range(3)] for i in range(3)]
    for block in range(rows // LANES):
        start = block * LANES
        mixes = []
        for j in range(3):
            columns = slice(j * width, (j + 1) * width)
            mixes.append(
                sum(
                    taps[i][j] * projected_ref[HALO + start - i : HALO + start - i + LANES, columns]
                    for i in range(3)
                )
            )
        turned = (mixes[0] * mixes[1]).T
        for d in range(16):
            message_ref[pl.ds(d * 72 + block, 8, stride=8), :] = turned[d * 8 : (d + 1) * 8, :]
        gate_ref[start : start + LANES, :] = mixes[2]
        if block == 0:
            early = [mixes[0][:2], mixes[1][:2]]
    later = []
    for j in range(3):
        columns = slice(j * width, (j + 1) * width)
        last = projected_ref[HALO + rows - 1 : HALO + rows, columns]
        before = projected_ref[HALO + rows - 2 : HALO + rows - 1, columns]
        later.append(jnp.concatenate([taps[1][j] * last + taps[2][j] * before, taps[2][j] * last], axis=0))
    extra = jnp.concatenate(early + later[:2] + [jnp.zeros((LANES - 8, width), F32)], axis=0).T
    for d in range(16):
        message_ref[d * 72 + 64 : d * 72 + 72, :] = extra[d * 8 : (d + 1) * 8, :]
    late_ref[...] = jnp.concatenate([later[2], jnp.zeros((6, width), F32)], axis=0)


def gate_kernel(conv_ref, gate_ref, late_ref, out_ref):
    late = late_ref[...]
    for block in range(gate_ref.shape[0] // LANES):
        rows = slice(block * LANES, (block + 1) * LANES)
        conv = conv_ref[pl.ds(block, LANES, stride=8), :].T
        gate = gate_ref[rows, :]
        if block == 0:
            gate = jnp.concatenate([gate[:8] + late, gate[8:]], axis=0)
        out_ref[rows, :] = (gate * conv).astype(BF16)


def output_kernel(*refs):
    gated, weight_ref, tokens_ref, out_ref = refs[:8], refs[8], refs[9], refs[10]
    rows, width = out_ref.shape
    weight = weight_ref[...]
    step = 256
    for start in range(0, rows, step):
        piece = slice(start, start + step)
        product = dot(jnp.concatenate([ref[piece, :] for ref in gated], axis=1), weight)
        out_ref[piece, :] = tokens_ref[piece, :].astype(F32) + product


def around(value, steps):
    count = lax.axis_size("chan")
    return lax.ppermute(value, "chan", [(i, (i + 2 * steps) % count) for i in range(count)])


def across(value):
    return lax.ppermute(value, "chan", [(i, i ^ 1) for i in range(lax.axis_size("chan"))])


def gather(value):
    mine = [value] + [around(value, steps) for steps in (1, 2, 3)]
    return mine + [across(piece) for piece in mine]


def after(*values):
    return lax.optimization_barrier(values)


def call(kernel, shapes, *operands, scalars=0, scratch=(), cost=None):
    smem = pl.BlockSpec(memory_space=pltpu.SMEM)
    return pl.pallas_call(
        kernel,
        out_shape=shapes,
        in_specs=[smem] * scalars + [VMEM] * (len(operands) - scalars),
        out_specs=jax.tree.map(lambda _: VMEM, shapes),
        scratch_shapes=scratch,
        cost_estimate=cost,
        compiler_params=pltpu.CompilerParams(vmem_limit_bytes=VMEM_LIMIT),
    )(*operands)


def local(tokens, norm_gain, in_weight, short_kernel, filter_fwd, filter_bwd, skip_gain, out_weight):
    seq_count = lax.axis_size("seq")
    seq_index = lax.axis_index("seq")
    chan_index = lax.axis_index("chan").reshape(1)
    rows, width = tokens.shape
    table = {name: jnp.asarray(value) for name, value in tables().items()}
    shape = jax.ShapeDtypeStruct

    pieces = [tokens] + [around(tokens, steps) for steps in (1, 2, 3)]
    spread = call(spread_kernel, shape((seq_count, 2, 64, width), F32), filter_fwd, filter_bwd)
    pieces = pieces + [across(piece) for piece in pieces]
    filters = lax.all_to_all(spread, "seq", 0, 0).reshape(seq_count, 2, 8, 8, width)
    my_skip = lax.dynamic_slice(skip_gain, (seq_index * 8,), (8,))
    gain = call(
        filter_kernel,
        shape((8, 2, LANES, LANES), F32),
        my_skip,
        filters,
        table["forward"],
        table["mix"],
        table["twiddle"],
        table["ahead"],
        scalars=1,
    )

    message, gate, late = call(
        project_kernel,
        (shape((seq_count * 72, width), F32), shape((rows, width), F32), shape((8, width), F32)),
        chan_index,
        *pieces,
        norm_gain.reshape(-1, width),
        in_weight,
        short_kernel,
        scalars=1,
        scratch=[pltpu.VMEM((rows + HALO, 3 * width), F32), pltpu.VMEM((8 * width, 3 * width), BF16)],
        cost=pl.CostEstimate(flops=PROJECT_FLOPS, bytes_accessed=1, transcendentals=0),
    )
    message, filters = after(message, filters)
    signal = lax.all_to_all(message.reshape(seq_count, 9, 8, width), "seq", 0, 0)
    late = lax.ppermute(late, "seq", [(i, i + 1) for i in range(seq_count - 1)])
    z = chan_index[0] // 2
    column = [lax.dynamic_slice(out_weight, (0, (z + steps) % 4 * 2 * width), (width, 2 * width)) for steps in range(4)]
    column = [column[0]] + [around(column[steps], steps) for steps in (1, 2, 3)]
    signal, *column = after(signal, *column)
    conv = call(
        conv_kernel,
        shape((seq_count, 8, 8, width), F32),
        signal,
        gain,
        table["forward"],
        table["mix"],
        table["unmix"],
        table["backward"],
        table["twiddle"],
    )
    conv = lax.all_to_all(conv, "seq", 0, 0)
    column = jnp.concatenate(column, axis=0)
    core = chan_index[0] % 2
    mine, theirs = [lax.dynamic_slice(column, (0, c * width), (4 * width, width)) for c in (core, 1 - core)]
    conv, theirs = after(conv, across(theirs))
    weights = jnp.concatenate([mine, theirs], axis=0)
    gated = call(gate_kernel, shape((rows, width), BF16), conv.reshape(rows, width), gate, late)
    return call(output_kernel, shape((rows, width), F32), *gather(gated), weights, tokens)


def solution(mesh):
    return jax.shard_map(
        local,
        mesh=mesh,
        in_specs=(
            P("seq", "chan"),
            P(),
            P(None, None, "chan"),
            P(None, None, "chan"),
            P("seq", "chan"),
            P("seq", "chan"),
            P("chan"),
            P("chan", None),
        ),
        out_specs=P("seq", "chan"),
        check_vma=False,
    )
```

time: 124 us -> 90.2 us (0.73)
  the two profiles are of different devices: /device:TPU:1 before, /device:TPU:3 now
where the time goes in v2:
time: 90.2 us; the launch traced here: 89.4 us
  starting transfers between devices  51.3 us (57%)
  Pallas kernels  14.5 us (16%)
  waiting for transfers between devices  13.7 us (15%)
  local copies, waits for them, and re-layouts  9.78 us (11%)
    ppermute x9, starting transfers between devices, across(): lax.ppermute(value, 'chan', [(i, i ^ 1) for i in range(lax.axis_size('cha...  15.1 us
    pallas_call x6, Pallas kernels, call(): pl.pallas_call(kernel, out_shape=shapes, in_specs=[smem] * scalars + [VME...  14.5 us
    ppermute x9, starting transfers between devices, around(): lax.ppermute(value, 'chan', [(i, (i + 2 * steps) % count) for i in range(...  13.1 us
    unnamed x37, local copies, waits for them, and re-layouts  8.12 us
    all_to_all x1, starting transfers between devices, local(): lax.all_to_all(spread, 'seq', 0, 0).reshape(seq_count, 2, 8, 8, width)  7.05 us
    all_to_all x1, starting transfers between devices, local(): conv = lax.all_to_all(conv, 'seq', 0, 0)  6.8 us
    all_to_all x1, starting transfers between devices, local(): lax.all_to_all(message.reshape(seq_count, 9, 8, width), 'seq', 0, 0)  6.08 us
    all_to_all x1, waiting for transfers between devices, local(): lax.all_to_all(spread, 'seq', 0, 0).reshape(seq_count, 2, 8, 8, width)  3.88 us
  transfers between devices with their start and end apart: 22, of which 10 were waited for; matrix products, arithmetic and copies ran while one was open for 4% of the time, Pallas kernels for 9%

profile of v2, /device:TPU:3, one launch (start us, length us, event | category | flops | bytes accessed | tf_op | source)
XLA Modules:
  0.0 89.4 jit_solution(1853073396494455126)
XLA Ops:
  0.0 1.6 %collective-permute-start = (bf16[1024,128]{1,0:T(8,128)(2,1)}, bf16[1024,128]{1,0:T(8,128)(2,1)S(1)}, u32[]{:S(2)}, u32[]{:S(2)}) collective-permute-start(bf16[1024,128]{1,0:T(8,128)(2,1)} %refs_9_.3), channel_id=1, source_target_pairs={{0,2},{1,3},{2,4},{3,5},{4,6},{5,7},{6,0},{7,1},{8,10},{9,11},{10,... | collective-permute-start | bytes 786440 | tf_op jit(solution)/shard_map/ppermute | solution.py:223
  1.6 3.3 %collective-permute-start.1 = (bf16[1024,128]{1,0:T(8,128)(2,1)}, bf16[1024,128]{1,0:T(8,128)(2,1)S(1)}, u32[]{:S(2)}, u32[]{:S(2)}) collective-permute-start(bf16[1024,128]{1,0:T(8,128)(2,1)} %refs_9_.3), channel_id=1, source_target_pairs={{0,4},{1,5},{2,6},{3,7},{4,0},{5,1},{6,2},{7,3},{8,12},{9,13},{10,... | collective-permute-start | bytes 786440 | tf_op jit(solution)/shard_map/ppermute | solution.py:223
  5.7 1.0 %copy-done.5 = f32[1024,128]{1,0:T(8,128)S(1)} copy-done((f32[1024,128]{1,0:T(8,128)S(1)}, f32[1024,128]{1,0:T(8,128)}, u32[]{:S(2)}) %copy-start.5) | copy-done | bytes 524312
  6.7 1.0 %copy-done.6 = f32[1024,128]{1,0:T(8,128)S(1)} copy-done((f32[1024,128]{1,0:T(8,128)S(1)}, f32[1024,128]{1,0:T(8,128)}, u32[]{:S(2)}) %copy-start.6) | copy-done | bytes 524312
  7.8 1.3 %shard_map.137 = f32[16,2,64,128]{3,2,1,0:T(8,128)} custom-call(f32[1024,128]{1,0:T(8,128)S(1)} %copy-done.5, f32[1024,128]{1,0:T(8,128)S(1)} %copy-done.6), custom_call_target="tpu_custom_call" | custom-call | tf_op jit(solution)/shard_map/pallas_call | solution.py:241
  9.1 7.0 %all-to-all-start = ((f32[16,2,64,128]{3,2,1,0:T(8,128)}), f32[16,2,64,128]{3,2,1,0:T(8,128)S(1)}, u32[]{:S(2)}, u32[]{:S(2)}) async-start(f32[16,2,64,128]{3,2,1,0:T(8,128)} %shard_map.137), calls=%async_computation | async-start | bytes 2097152 | tf_op jit(solution)/shard_map/all_to_all | solution.py:263
  16.2 2.2 %collective-permute-start.3 = (bf16[1024,128]{1,0:T(8,128)(2,1)S(1)}, bf16[1024,128]{1,0:T(8,128)(2,1)S(1)}, u32[]{:S(2)}, u32[]{:S(2)}) collective-permute-start(bf16[1024,128]{1,0:T(8,128)(2,1)S(1)} %copy-done.7), channel_id=1, source_target_pairs={{0,1},{1,0},{2,3},{3,2},{4,5},{5,4},{6,7},{7,6},{8,9},{9,8},{10,11... | collective-permute-start | bytes 786440 | tf_op jit(solution)/shard_map/ppermute | solution.py:227
  20.7 3.9 %shard_map.136 = (f32[1152,128]{1,0:T(8,128)}, f32[1024,128]{1,0:T(8,128)S(1)}, f32[8,128]{1,0:T(8,128)S(1)}) custom-call(s32[1]{0:T(128)} %bitcast.index_ref, bf16[1024,128]{1,0:T(8,128)(2,1)S(1)} %copy-done.7, bf16[1024,128]{1,0:T(8,128)(2,1)S(1)} %collective-permute-done.refs_1_, bf16[1024,128]{1,0:T(8,128)(2,1)S(1)} %collective-permute-done.1.refs_2_, ...), custom_call_target="tpu_custom_call" | custom-call | flops 6000000000 | bytes 1 | tf_op jit(solution)/shard_map/pallas_call | solution.py:241
  24.6 0.8 copy-done.3
  25.5 3.9 %all-to-all-done = f32[16,2,64,128]{3,2,1,0:T(8,128)S(1)} async-done(((f32[16,2,64,128]{3,2,1,0:T(8,128)}), f32[16,2,64,128]{3,2,1,0:T(8,128)S(1)}, u32[]{:S(2)}, u32[]{:S(2)}) %all-to-all-start) | async-done | bytes 1048608 | tf_op jit(solution)/shard_map/all_to_all | solution.py:263
  29.3 6.1 %all-to-all-start.1 = ((f32[16,9,8,128]{3,2,1,0:T(8,128)}), f32[16,9,8,128]{3,2,1,0:T(8,128)S(1)}, u32[]{:S(2)}, u32[]{:S(2)}) async-start(f32[16,9,8,128]{3,2,1,0:T(8,128)} %bitcast.3), calls=%async_computation.1 | async-start | bytes 1179648 | tf_op jit(solution)/shard_map/all_to_all | solution.py:290
  37.4 1.9 %collective-permute-start.9 = (bf16[128,256]{1,0:T(8,128)(2,1)}, bf16[128,256]{1,0:T(8,128)(2,1)}, u32[]{:S(2)}, u32[]{:S(2)}) collective-permute-start(bf16[128,256]{1,0:T(8,128)(2,1)} %get-tuple-element.29), channel_id=1, source_target_pairs={{0,6},{1,7},{2,0},{3,1},{4,2},{5,3},{6,4},{7,5},{8,14},{9,15},{10,... | collective-permute-start | bytes 196616 | tf_op jit(solution)/shard_map/ppermute | solution.py:223
  40.1 0.9 %copy-done.10 = f32[2,128,128]{2,1,0:T(8,128)S(1)} copy-done((f32[2,128,128]{2,1,0:T(8,128)S(1)}, f32[2,128,128]{2,1,0:T(8,128)}, u32[]{:S(2)}) %copy-start.10) | copy-done | bytes 131096
  41.0 2.8 %shard_map.138.gain_ref = f32[8,2,128,128]{3,2,1,0:T(8,128)S(1)} custom-call(f32[8]{0:T(128)S(1)} %dynamic_slice.25.skip_ref, f32[16,2,8,8,128]{4,3,2,1,0:T(8,128)S(1)} %bitcast.5, bf16[256,384]{1,0:T(8,128)(2,1)S(1)} %copy-done.1, bf16[512,256]{1,0:T(8,128)(2,1)S(1)} %copy-done, f32[2,128,128]{2,1,0:T(8,128)S(1)} %copy-done.2, f32[2,128,128]{2,1,0:T(8,128)S(1)} %copy-done.10), custom_call_target="tpu_custom_call" | custom-call | tf_op jit(solution)/shard_map/pallas_call | solution.py:241
  43.8 0.9 %copy-done.8 = bf16[512,256]{1,0:T(8,128)(2,1)S(1)} copy-done((bf16[512,256]{1,0:T(8,128)(2,1)S(1)}, bf16[512,256]{1,0:T(8,128)(2,1)}, u32[]{:S(2)}) %copy-start.8) | copy-done | bytes 262168
  44.7 0.9 %copy-done.9 = bf16[128,768]{1,0:T(8,128)(2,1)S(1)} copy-done((bf16[128,768]{1,0:T(8,128)(2,1)S(1)}, bf16[128,768]{1,0:T(8,128)(2,1)}, u32[]{:S(2)}) %copy-start.9) | copy-done | bytes 196632
  45.7 4.8 %shard_map.139 = f32[16,8,8,128]{3,2,1,0:T(8,128)} custom-call(f32[16,9,8,128]{3,2,1,0:T(8,128)S(1)} %all-to-all-done.1.sig_ref, f32[8,2,128,128]{3,2,1,0:T(8,128)S(1)} %shard_map.138.gain_ref, bf16[256,384]{1,0:T(8,128)(2,1)S(1)} %copy-done.1, bf16[512,256]{1,0:T(8,128)(2,1)S(1)} %copy-done, bf16[512,256]{1,0:T(8,128)(2,1)S(1)} %copy-done.8, ...), custom_call_target="tpu_custom_call" | custom-call | tf_op jit(solution)/shard_map/pallas_call | solution.py:241
  50.4 6.8 %all-to-all-start.2 = ((f32[16,8,8,128]{3,2,1,0:T(8,128)}), f32[16,8,8,128]{3,2,1,0:T(8,128)S(1)}, u32[]{:S(2)}, u32[]{:S(2)}) async-start(f32[16,8,8,128]{3,2,1,0:T(8,128)} %shard_map.139), calls=%async_computation.2 | async-start | bytes 1048576 | tf_op jit(solution)/shard_map/all_to_all | solution.py:307
  57.3 0.9 %constant_dynamic-update-slice_fusion.2 = bf16[512,256]{1,0:T(8,128)(2,1)S(1)} fusion(bf16[512,256]{1,0:T(8,128)(2,1)S(1)} %constant_dynamic-update-slice_fusion.3, bf16[128,256]{1,0:T(8,128)(2,1)} %collective-permute-done.7), kind=kLoop, calls=%fused_computation.3 | loop fusion | bytes 131072
  58.2 0.8 constant_dynamic-update-slice_fusion.1
  59.0 0.8 constant_dynamic-update-slice_fusion
  59.9 4.0 %collective-permute-start.10 = (bf16[512,128]{1,0:T(8,128)(2,1)S(1)}, bf16[512,128]{1,0:T(8,128)(2,1)S(1)}, u32[]{:S(2)}, u32[]{:S(2)}) collective-permute-start(bf16[512,128]{1,0:T(8,128)(2,1)S(1)} %get-tuple-element.28), channel_id=1, source_target_pairs={{0,1},{1,0},{2,3},{3,2},{4,5},{5,4},{6,7},{7,6},{8,9},{9,8},{10,11... | collective-permute-start | bytes 393224 | tf_op jit(solution)/shard_map/ppermute | solution.py:227
  63.9 3.1 %collective-permute-start.11 = (f32[8,128]{1,0:T(8,128)S(1)}, f32[8,128]{1,0:T(8,128)S(1)}, u32[]{:S(2)}, u32[]{:S(2)}) collective-permute-start(f32[8,128]{1,0:T(8,128)S(1)} %get-tuple-element.25), channel_id=1, source_target_pairs={{0,8},{8,16},{16,24},{24,32},{32,40},{40,48},{48,56},{56,64},{64,7... | collective-permute-start | bytes 12296 | tf_op jit(solution)/shard_map/ppermute | solution.py:291
  67.0 3.3 %collective-permute-done.11.late_ref = f32[8,128]{1,0:T(8,128)S(1)} collective-permute-done((f32[8,128]{1,0:T(8,128)S(1)}, f32[8,128]{1,0:T(8,128)S(1)}, u32[]{:S(2)}, u32[]{:S(2)}) %collective-permute-start.11) | collective-permute-done | bytes 4128 | tf_op jit(solution)/shard_map/ppermute | solution.py:291
  70.8 2.5 %collective-permute-start.13 = (bf16[1024,128]{1,0:T(8,128)(2,1)S(1)}, bf16[1024,128]{1,0:T(8,128)(2,1)S(1)}, u32[]{:S(2)}, u32[]{:S(2)}) collective-permute-start(bf16[1024,128]{1,0:T(8,128)(2,1)S(1)} %shard_map.140.refs_0_), channel_id=1, source_target_pairs={{0,4},{1,5},{2,6},{3,7},{4,0},{5,1},{6,2},{7,3},{8,12},{9,13},{10,... | collective-permute-start | bytes 786440 | tf_op jit(solution)/shard_map/ppermute | solution.py:223
  73.4 1.5 %collective-permute-start.14 = (bf16[1024,128]{1,0:T(8,128)(2,1)S(1)}, bf16[1024,128]{1,0:T(8,128)(2,1)S(1)}, u32[]{:S(2)}, u32[]{:S(2)}) collective-permute-start(bf16[1024,128]{1,0:T(8,128)(2,1)S(1)} %shard_map.140.refs_0_), channel_id=1, source_target_pairs={{0,6},{1,7},{2,0},{3,1},{4,2},{5,3},{6,4},{7,5},{8,14},{9,15},{10,... | collective-permute-start | bytes 786440 | tf_op jit(solution)/shard_map/ppermute | solution.py:223
  74.9 2.0 %collective-permute-start.15 = (bf16[1024,128]{1,0:T(8,128)(2,1)S(1)}, bf16[1024,128]{1,0:T(8,128)(2,1)S(1)}, u32[]{:S(2)}, u32[]{:S(2)}) collective-permute-start(bf16[1024,128]{1,0:T(8,128)(2,1)S(1)} %shard_map.140.refs_0_), channel_id=1, source_target_pairs={{0,1},{1,0},{2,3},{3,2},{4,5},{5,4},{6,7},{7,6},{8,9},{9,8},{10,11... | collective-permute-start | bytes 786440 | tf_op jit(solution)/shard_map/ppermute | solution.py:227
  76.9 1.6 %collective-permute-done.12.refs_1_ = bf16[1024,128]{1,0:T(8,128)(2,1)S(1)} collective-permute-done((bf16[1024,128]{1,0:T(8,128)(2,1)S(1)}, bf16[1024,128]{1,0:T(8,128)(2,1)S(1)}, u32[]{:S(2)}, u32[]{:S(2)}) %collective-permute-start.12) | collective-permute-done | bytes 262176 | tf_op jit(solution)/shard_map/ppermute | solution.py:223
  78.4 3.7 %collective-permute-start.16 = (bf16[1024,128]{1,0:T(8,128)(2,1)S(1)}, bf16[1024,128]{1,0:T(8,128)(2,1)S(1)}, u32[]{:S(2)}, u32[]{:S(2)}) collective-permute-start(bf16[1024,128]{1,0:T(8,128)(2,1)S(1)} %collective-permute-done.12.refs_1_), channel_id=1, source_target_pairs={{0,1},{1,0},{2,3},{3,2},{4,5},{5,4},{6,7},{7,6},{8,9},{9,8},{10,11... | collective-permute-start | bytes 786440 | tf_op jit(solution)/shard_map/ppermute | solution.py:227
  82.2 2.0 %collective-permute-done.13.refs_2_ = bf16[1024,128]{1,0:T(8,128)(2,1)S(1)} collective-permute-done((bf16[1024,128]{1,0:T(8,128)(2,1)S(1)}, bf16[1024,128]{1,0:T(8,128)(2,1)S(1)}, u32[]{:S(2)}, u32[]{:S(2)}) %collective-permute-start.13) | collective-permute-done | bytes 262176 | tf_op jit(solution)/shard_map/ppermute | solution.py:223
  84.1 2.1 %collective-permute-start.17 = (bf16[1024,128]{1,0:T(8,128)(2,1)S(1)}, bf16[1024,128]{1,0:T(8,128)(2,1)S(1)}, u32[]{:S(2)}, u32[]{:S(2)}) collective-permute-start(bf16[1024,128]{1,0:T(8,128)(2,1)S(1)} %collective-permute-done.13.refs_2_), channel_id=1, source_target_pairs={{0,1},{1,0},{2,3},{3,2},{4,5},{5,4},{6,7},{7,6},{8,9},{9,8},{10,11... | collective-permute-start | bytes 786440 | tf_op jit(solution)/shard_map/ppermute | solution.py:227
  87.9 1.5 %shard_map.141 = f32[1024,128]{1,0:T(8,128)} custom-call(bf16[1024,128]{1,0:T(8,128)(2,1)S(1)} %shard_map.140.refs_0_, bf16[1024,128]{1,0:T(8,128)(2,1)S(1)} %collective-permute-done.12.refs_1_, bf16[1024,128]{1,0:T(8,128)(2,1)S(1)} %collective-permute-done.13.refs_2_, bf16[1024,128]{1,0:T(8,128)(2,1)S(1)} %collective-permute-done.14.refs_3_, ...), custom_call_target="tpu_custom_call" | custom-call | tf_op jit(solution)/shard_map/pallas_call | solution.py:241
  (60 shorter events, 8.1 us)
Async XLA Ops:
  0.0 18.3 %collective-permute-start = (bf16[1024,128]{1,0:T(8,128)(2,1)}, bf16[1024,128]{1,0:T(8,128)(2,1)S(1)}, u32[]{:S(2)}, u32[]{:S(2)}) collective-permute-start(bf16[1024,128]{1,0:T(8,128)(2,1)} %refs_9_.3), channel_id=1, source_target_pairs={{0,2},{1,3},{2,4},{3,5},{4,6},{5,7},{6,0},{7,1},{8,10},{9,11},{10,... | collective-permute-start | bytes 786440 | tf_op jit(solution)/shard_map/ppermute | solution.py:223
  1.6 16.8 %collective-permute-start.1 = (bf16[1024,128]{1,0:T(8,128)(2,1)}, bf16[1024,128]{1,0:T(8,128)(2,1)S(1)}, u32[]{:S(2)}, u32[]{:S(2)}) collective-permute-start(bf16[1024,128]{1,0:T(8,128)(2,1)} %refs_9_.3), channel_id=1, source_target_pairs={{0,4},{1,5},{2,6},{3,7},{4,0},{5,1},{6,2},{7,3},{8,12},{9,13},{10,... | collective-permute-start | bytes 786440 | tf_op jit(solution)/shard_map/ppermute | solution.py:223
  4.9 13.9 %collective-permute-start.2 = (bf16[1024,128]{1,0:T(8,128)(2,1)}, bf16[1024,128]{1,0:T(8,128)(2,1)S(1)}, u32[]{:S(2)}, u32[]{:S(2)}) collective-permute-start(bf16[1024,128]{1,0:T(8,128)(2,1)} %refs_9_.3), channel_id=1, source_target_pairs={{0,6},{1,7},{2,0},{3,1},{4,2},{5,3},{6,4},{7,5},{8,14},{9,15},{10,... | collective-permute-start | bytes 786440 | tf_op jit(solution)/shard_map/ppermute | solution.py:223
  9.1 7.1 %copy-start.7 = (bf16[1024,128]{1,0:T(8,128)(2,1)S(1)}, bf16[1024,128]{1,0:T(8,128)(2,1)}, u32[]{:S(2)}) copy-start(bf16[1024,128]{1,0:T(8,128)(2,1)} %refs_9_.3) | copy-start | bytes 786436
  9.1 11.7 %copy-start.11 = (bf16[3,1024,128]{2,1,0:T(8,128)(2,1)S(1)}, bf16[3,1024,128]{2,1,0:T(8,128)(2,1)}, u32[]{:S(2)}) copy-start(bf16[3,1024,128]{2,1,0:T(8,128)(2,1)} %refs_9_.2) | copy-start | bytes 2359300
  9.1 11.7 %copy-start.13 = (f32[1024]{0:T(1024)S(1)}, f32[1024]{0:T(1024)}, u32[]{:S(2)}) copy-start(f32[1024]{0:T(1024)} %param.15) | copy-start | bytes 12292
  9.1 20.3 %all-to-all-start = ((f32[16,2,64,128]{3,2,1,0:T(8,128)}), f32[16,2,64,128]{3,2,1,0:T(8,128)S(1)}, u32[]{:S(2)}, u32[]{:S(2)}) async-start(f32[16,2,64,128]{3,2,1,0:T(8,128)} %shard_map.137), calls=%async_computation | async-start | bytes 2097152 | tf_op jit(solution)/shard_map/all_to_all | solution.py:263
  16.1 4.6 %copy-start.12 = (f32[3,3,128]{2,1,0:T(4,128)S(1)}, f32[3,3,128]{2,1,0:T(4,128)}, u32[]{:S(2)}) copy-start(f32[3,3,128]{2,1,0:T(4,128)} %refs_10_.1) | copy-start | bytes 13828
  16.2 3.3 %collective-permute-start.3 = (bf16[1024,128]{1,0:T(8,128)(2,1)S(1)}, bf16[1024,128]{1,0:T(8,128)(2,1)S(1)}, u32[]{:S(2)}, u32[]{:S(2)}) collective-permute-start(bf16[1024,128]{1,0:T(8,128)(2,1)S(1)} %copy-done.7), channel_id=1, source_target_pairs={{0,1},{1,0},{2,3},{3,2},{4,5},{5,4},{6,7},{7,6},{8,9},{9,8},{10,11... | collective-permute-start | bytes 786440 | tf_op jit(solution)/shard_map/ppermute | solution.py:227
  18.3 1.5 %collective-permute-start.4 = (bf16[1024,128]{1,0:T(8,128)(2,1)S(1)}, bf16[1024,128]{1,0:T(8,128)(2,1)S(1)}, u32[]{:S(2)}, u32[]{:S(2)}) collective-permute-start(bf16[1024,128]{1,0:T(8,128)(2,1)S(1)} %collective-permute-done.refs_1_), channel_id=1, source_target_pairs={{0,1},{1,0},{2,3},{3,2},{4,5},{5,4},{6,7},{7,6},{8,9},{9,8},{10,11... | collective-permute-start | bytes 786440 | tf_op jit(solution)/shard_map/ppermute | solution.py:227
  18.4 1.9 %collective-permute-start.5 = (bf16[1024,128]{1,0:T(8,128)(2,1)S(1)}, bf16[1024,128]{1,0:T(8,128)(2,1)}, u32[]{:S(2)}, u32[]{:S(2)}) collective-permute-start(bf16[1024,128]{1,0:T(8,128)(2,1)S(1)} %collective-permute-done.1.refs_2_), channel_id=1, source_target_pairs={{0,1},{1,0},{2,3},{3,2},{4,5},{5,4},{6,7},{7,6},{8,9},{9,8},{10,11... | collective-permute-start | bytes 786440 | tf_op jit(solution)/shard_map/ppermute | solution.py:227
  18.8 1.9 %collective-permute-start.6 = (bf16[1024,128]{1,0:T(8,128)(2,1)S(1)}, bf16[1024,128]{1,0:T(8,128)(2,1)}, u32[]{:S(2)}, u32[]{:S(2)}) collective-permute-start(bf16[1024,128]{1,0:T(8,128)(2,1)S(1)} %collective-permute-done.2.refs_3_), channel_id=1, source_target_pairs={{0,1},{1,0},{2,3},{3,2},{4,5},{5,4},{6,7},{7,6},{8,9},{9,8},{10,11... | collective-permute-start | bytes 786440 | tf_op jit(solution)/shard_map/ppermute | solution.py:227
  29.3 6.1 %copy-start.14 = (bf16[128,1024]{1,0:T(8,128)(2,1)S(1)}, bf16[128,1024]{1,0:T(8,128)(2,1)}, u32[]{:S(2)}) copy-start(bf16[128,1024]{1,0:T(8,128)(2,1)} %param.21) | copy-start | bytes 786436
  29.3 10.7 %copy-start.2 = (f32[2,128,128]{2,1,0:T(8,128)S(1)}, f32[2,128,128]{2,1,0:T(8,128)}, u32[]{:S(2)}) copy-start(f32[2,128,128]{2,1,0:T(8,128)} %constant.86.clone.twiddle_ref) | copy-start | bytes 393220
  29.3 14.4 %all-to-all-start.1 = ((f32[16,9,8,128]{3,2,1,0:T(8,128)}), f32[16,9,8,128]{3,2,1,0:T(8,128)S(1)}, u32[]{:S(2)}, u32[]{:S(2)}) async-start(f32[16,9,8,128]{3,2,1,0:T(8,128)} %bitcast.3), calls=%async_computation.1 | async-start | bytes 1179648 | tf_op jit(solution)/shard_map/all_to_all | solution.py:290
  35.4 4.6 %copy-start = (bf16[512,256]{1,0:T(8,128)(2,1)S(1)}, bf16[512,256]{1,0:T(8,128)(2,1)}, u32[]{:S(2)}) copy-start(bf16[512,256]{1,0:T(8,128)(2,1)} %constant.84.clone.mix_ref) | copy-start | bytes 786436
  35.4 4.6 %copy-start.1 = (bf16[256,384]{1,0:T(8,128)(2,1)S(1)}, bf16[256,384]{1,0:T(8,128)(2,1)}, u32[]{:S(2)}) copy-start(bf16[256,384]{1,0:T(8,128)(2,1)} %constant.82.clone.forward_ref) | copy-start | bytes 589828
  36.2 7.6 %collective-permute-start.7 = (bf16[128,256]{1,0:T(8,128)(2,1)}, bf16[128,256]{1,0:T(8,128)(2,1)}, u32[]{:S(2)}, u32[]{:S(2)}) collective-permute-start(bf16[128,256]{1,0:T(8,128)(2,1)} %get-tuple-element.30), channel_id=1, source_target_pairs={{0,2},{1,3},{2,4},{3,5},{4,6},{5,7},{6,0},{7,1},{8,10},{9,11},{10,... | collective-permute-start | bytes 196616 | tf_op jit(solution)/shard_map/ppermute | solution.py:223
  36.9 6.9 %collective-permute-start.8 = (bf16[128,256]{1,0:T(8,128)(2,1)}, bf16[128,256]{1,0:T(8,128)(2,1)}, u32[]{:S(2)}, u32[]{:S(2)}) collective-permute-start(bf16[128,256]{1,0:T(8,128)(2,1)} %get-tuple-element.32), channel_id=1, source_target_pairs={{0,4},{1,5},{2,6},{3,7},{4,0},{5,1},{6,2},{7,3},{8,12},{9,13},{10,... | collective-permute-start | bytes 196616 | tf_op jit(solution)/shard_map/ppermute | solution.py:223
  37.4 6.4 %collective-permute-start.9 = (bf16[128,256]{1,0:T(8,128)(2,1)}, bf16[128,256]{1,0:T(8,128)(2,1)}, u32[]{:S(2)}, u32[]{:S(2)}) collective-permute-start(bf16[128,256]{1,0:T(8,128)(2,1)} %get-tuple-element.29), channel_id=1, source_target_pairs={{0,6},{1,7},{2,0},{3,1},{4,2},{5,3},{6,4},{7,5},{8,14},{9,15},{10,... | collective-permute-start | bytes 196616 | tf_op jit(solution)/shard_map/ppermute | solution.py:223
  50.4 6.8 %copy-start.15 = (bf16[128,256]{1,0:T(8,128)(2,1)S(1)}, bf16[128,256]{1,0:T(8,128)(2,1)}, u32[]{:S(2)}) copy-start(bf16[128,256]{1,0:T(8,128)(2,1)} %get-tuple-element.19) | copy-start | bytes 196612
  50.4 16.5 %all-to-all-start.2 = ((f32[16,8,8,128]{3,2,1,0:T(8,128)}), f32[16,8,8,128]{3,2,1,0:T(8,128)S(1)}, u32[]{:S(2)}, u32[]{:S(2)}) async-start(f32[16,8,8,128]{3,2,1,0:T(8,128)} %shard_map.139), calls=%async_computation.2 | async-start | bytes 1048576 | tf_op jit(solution)/shard_map/all_to_all | solution.py:307
  57.3 13.1 %copy-start.4 = (f32[1024,128]{1,0:T(8,128)S(1)}, f32[1024,128]{1,0:T(8,128)}, u32[]{:S(2)}) copy-start(f32[1024,128]{1,0:T(8,128)} %copy-done.3) | copy-start | bytes 1572868
  59.9 7.1 %collective-permute-start.10 = (bf16[512,128]{1,0:T(8,128)(2,1)S(1)}, bf16[512,128]{1,0:T(8,128)(2,1)S(1)}, u32[]{:S(2)}, u32[]{:S(2)}) collective-permute-start(bf16[512,128]{1,0:T(8,128)(2,1)S(1)} %get-tuple-element.28), channel_id=1, source_target_pairs={{0,1},{1,0},{2,3},{3,2},{4,5},{5,4},{6,7},{7,6},{8,9},{9,8},{10,11... | collective-permute-start | bytes 393224 | tf_op jit(solution)/shard_map/ppermute | solution.py:227
  63.9 6.4 %collective-permute-start.11 = (f32[8,128]{1,0:T(8,128)S(1)}, f32[8,128]{1,0:T(8,128)S(1)}, u32[]{:S(2)}, u32[]{:S(2)}) collective-permute-start(f32[8,128]{1,0:T(8,128)S(1)} %get-tuple-element.25), channel_id=1, source_target_pairs={{0,8},{8,16},{16,24},{24,32},{32,40},{40,48},{48,56},{56,64},{64,7... | collective-permute-start | bytes 12296 | tf_op jit(solution)/shard_map/ppermute | solution.py:291
  70.5 7.9 %collective-permute-start.12 = (bf16[1024,128]{1,0:T(8,128)(2,1)S(1)}, bf16[1024,128]{1,0:T(8,128)(2,1)S(1)}, u32[]{:S(2)}, u32[]{:S(2)}) collective-permute-start(bf16[1024,128]{1,0:T(8,128)(2,1)S(1)} %shard_map.140.refs_0_), channel_id=1, source_target_pairs={{0,2},{1,3},{2,4},{3,5},{4,6},{5,7},{6,0},{7,1},{8,10},{9,11},{10,... | collective-permute-start | bytes 786440 | tf_op jit(solution)/shard_map/ppermute | solution.py:223
  70.8 13.3 %collective-permute-start.13 = (bf16[1024,128]{1,0:T(8,128)(2,1)S(1)}, bf16[1024,128]{1,0:T(8,128)(2,1)S(1)}, u32[]{:S(2)}, u32[]{:S(2)}) collective-permute-start(bf16[1024,128]{1,0:T(8,128)(2,1)S(1)} %shard_map.140.refs_0_), channel_id=1, source_target_pairs={{0,4},{1,5},{2,6},{3,7},{4,0},{5,1},{6,2},{7,3},{8,12},{9,13},{10,... | collective-permute-start | bytes 786440 | tf_op jit(solution)/shard_map/ppermute | solution.py:223
  73.4 12.9 %collective-permute-start.14 = (bf16[1024,128]{1,0:T(8,128)(2,1)S(1)}, bf16[1024,128]{1,0:T(8,128)(2,1)S(1)}, u32[]{:S(2)}, u32[]{:S(2)}) collective-permute-start(bf16[1024,128]{1,0:T(8,128)(2,1)S(1)} %shard_map.140.refs_0_), channel_id=1, source_target_pairs={{0,6},{1,7},{2,0},{3,1},{4,2},{5,3},{6,4},{7,5},{8,14},{9,15},{10,... | collective-permute-start | bytes 786440 | tf_op jit(solution)/shard_map/ppermute | solution.py:223
  74.9 11.9 %collective-permute-start.15 = (bf16[1024,128]{1,0:T(8,128)(2,1)S(1)}, bf16[1024,128]{1,0:T(8,128)(2,1)S(1)}, u32[]{:S(2)}, u32[]{:S(2)}) collective-permute-start(bf16[1024,128]{1,0:T(8,128)(2,1)S(1)} %shard_map.140.refs_0_), channel_id=1, source_target_pairs={{0,1},{1,0},{2,3},{3,2},{4,5},{5,4},{6,7},{7,6},{8,9},{9,8},{10,11... | collective-permute-start | bytes 786440 | tf_op jit(solution)/shard_map/ppermute | solution.py:227
  78.4 8.4 %collective-permute-start.16 = (bf16[1024,128]{1,0:T(8,128)(2,1)S(1)}, bf16[1024,128]{1,0:T(8,128)(2,1)S(1)}, u32[]{:S(2)}, u32[]{:S(2)}) collective-permute-start(bf16[1024,128]{1,0:T(8,128)(2,1)S(1)} %collective-permute-done.12.refs_1_), channel_id=1, source_target_pairs={{0,1},{1,0},{2,3},{3,2},{4,5},{5,4},{6,7},{7,6},{8,9},{9,8},{10,11... | collective-permute-start | bytes 786440 | tf_op jit(solution)/shard_map/ppermute | solution.py:227
  84.1 3.3 %collective-permute-start.17 = (bf16[1024,128]{1,0:T(8,128)(2,1)S(1)}, bf16[1024,128]{1,0:T(8,128)(2,1)S(1)}, u32[]{:S(2)}, u32[]{:S(2)}) collective-permute-start(bf16[1024,128]{1,0:T(8,128)(2,1)S(1)} %collective-permute-done.13.refs_2_), channel_id=1, source_target_pairs={{0,1},{1,0},{2,3},{3,2},{4,5},{5,4},{6,7},{7,6},{8,9},{9,8},{10,11... | collective-permute-start | bytes 786440 | tf_op jit(solution)/shard_map/ppermute | solution.py:227
  86.2 1.7 %collective-permute-start.18 = (bf16[1024,128]{1,0:T(8,128)(2,1)S(1)}, bf16[1024,128]{1,0:T(8,128)(2,1)S(1)}, u32[]{:S(2)}, u32[]{:S(2)}) collective-permute-start(bf16[1024,128]{1,0:T(8,128)(2,1)S(1)} %collective-permute-done.14.refs_3_), channel_id=1, source_target_pairs={{0,1},{1,0},{2,3},{3,2},{4,5},{5,4},{6,7},{7,6},{8,9},{9,8},{10,11... | collective-permute-start | bytes 786440 | tf_op jit(solution)/shard_map/ppermute | solution.py:227
  (7 other events, 6.3 us)

commit v3 on v2

v3 whole, which is shorter than its diff:
```python
import functools

import jax
import jax.numpy as jnp
import ml_dtypes
import numpy as np
from jax import lax
from jax.experimental import pallas as pl
from jax.experimental.pallas import tpu as pltpu
from jax.sharding import PartitionSpec as P

HALO = 16
PROJECT_FLOPS = 1.5e9
LANES = 128
VMEM_LIMIT = 16 * 1024 * 1024
VMEM = pl.BlockSpec(memory_space=pltpu.VMEM)
F32 = jnp.float32
BF16 = jnp.bfloat16


def split_np(table):
    high = table.astype(np.float32).astype(ml_dtypes.bfloat16)
    low = (table - high.astype(np.float64)).astype(np.float32).astype(ml_dtypes.bfloat16)
    return high, low


@functools.cache
def tables():
    n = LANES
    period = 2 * n * n
    k = np.arange(n, dtype=np.float64)
    first = 2 * np.pi * np.outer(k + 0.5, k) / (2 * n)
    forward = np.concatenate([np.cos(first), -np.sin(first)], axis=0)
    second = 2 * np.pi * np.outer(k, k) / n
    cosine, sine = np.cos(second), np.sin(second)
    mix = np.block([[cosine, -sine], [sine, cosine]])
    turn = 2 * np.pi * np.outer(k + 0.5, k) / period
    twiddle = np.stack([np.cos(turn), -np.sin(turn)]).astype(np.float32)
    forward_hi, forward_lo = split_np(forward)
    mix_hi, mix_lo = split_np(mix)
    return {
        "forward": np.concatenate([forward_hi, forward_lo], axis=1),
        "mix": np.concatenate([mix_hi, mix_lo], axis=0),
        "twiddle": twiddle,
    }


def halves(value):
    high = value.astype(BF16)
    return high, (value - high.astype(F32)).astype(BF16)


def dot(left, right):
    return jnp.dot(left, right, preferred_element_type=F32)


def left_dot(table_ref, value):
    high, low = halves(value)
    table_hi, table_lo = [table_ref[:, i * LANES : (i + 1) * LANES].T for i in range(2)]
    return dot(
        jnp.concatenate([table_hi, table_lo, table_hi], axis=1), jnp.concatenate([high, high, low], axis=0)
    )


def right_dot(value, table_ref, transposed=False):
    high, low = halves(value)
    depth = value.shape[1]
    table_hi, table_lo = table_ref[:depth], table_ref[depth:]
    left = jnp.concatenate([high, low, high], axis=1)
    if transposed:
        right = jnp.concatenate([table_hi, table_hi, table_lo], axis=1)
        return lax.dot_general(left, right, (((1,), (1,)), ((), ())), preferred_element_type=F32)
    return dot(left, jnp.concatenate([table_hi, table_hi, table_lo], axis=0))


def transform(sequences, forward_ref, mix_ref, twiddle_ref):
    n = LANES
    value = jnp.concatenate(sequences, axis=1)
    parts = dot(forward_ref[...], jnp.concatenate([value, value], axis=0))
    cosine, sine = twiddle_ref[0], twiddle_ref[1]
    rows = []
    for i in range(len(sequences)):
        real = parts[:n, i * n : (i + 1) * n]
        imag = parts[n:, i * n : (i + 1) * n]
        rows.append(jnp.concatenate([real * cosine - imag * sine, real * sine + imag * cosine], axis=1))
    return right_dot(jnp.concatenate(rows, axis=0), mix_ref)


def spread_kernel(index_ref, fwd_ref, bwd_ref, weight_ref, out_ref, *refs):
    columns_refs, turned_ref = refs[:3], refs[3]
    z = index_ref[0] // 2
    for steps, columns_ref in enumerate(columns_refs):
        start = pl.multiple_of((z + steps + 1) % 4 * 2 * LANES, 2 * LANES)
        columns_ref[...] = weight_ref[:, pl.ds(start, 2 * LANES)]
    for which, source in enumerate((fwd_ref, bwd_ref)):
        for block in range(source.shape[0] // LANES):
            turned_ref[pl.ds(block, LANES, stride=8), :] = source[block * LANES : (block + 1) * LANES, :].T
        out_ref[:, which * 64 : (which + 1) * 64, :] = turned_ref[...].reshape(16, 64, LANES).astype(BF16)


def channel_pair(ref, start):
    both = ref[:, start : start + 16, :].astype(F32)
    return both[:, :8], both[:, 8:]


def filter_kernel(filt_ref, forward_ref, mix_ref, twiddle_ref, gain_ref):
    n = LANES
    row = mix_ref[:8, :].astype(F32) + mix_ref[2 * n : 2 * n + 8, :].astype(F32)
    row_real, row_imag = row[1:2, :n], -row[1:2, n:]
    column_real, column_imag = twiddle_ref[0, :, 1:2], -twiddle_ref[1, :, 1:2]
    cosine = column_real * row_real - column_imag * row_imag
    sine = column_real * row_imag + column_imag * row_real
    for c in range(0, 8, 2):
        forth, back = [channel_pair(filt_ref, 64 * which + 8 * c) for which in range(2)]
        spectra = transform(
            [part.reshape(n, n).astype(BF16) for part in forth + back], forward_ref, mix_ref, twiddle_ref
        )
        for i in range(2):
            forth_rows = slice(i * n, (i + 1) * n)
            back_rows = slice((2 + i) * n, (3 + i) * n)
            back_real, back_imag = spectra[back_rows, :n], -spectra[back_rows, n:]
            gain_ref[c + i, 0] = spectra[forth_rows, :n] + (back_real * cosine - back_imag * sine)
            gain_ref[c + i, 1] = spectra[forth_rows, n:] + (back_real * sine + back_imag * cosine)


def conv_kernel(sig_ref, gain_ref, forward_ref, mix_ref, twiddle_ref, out_ref):
    n = LANES
    extra_high, extra_low = channel_pair(sig_ref, 64)
    extra = extra_high + extra_low
    before = jnp.concatenate([jnp.zeros((1, 8, n), F32), extra[:-1]], axis=0)
    high = before.astype(BF16).astype(F32)
    out_ref[:, 64:, :] = jnp.concatenate([high, before - high], axis=1).astype(BF16)
    before = before.reshape(n, n)
    mixes = extra.reshape(n, n) + pltpu.roll(before, n - 4, 1)
    first = (mixes * pltpu.roll(mixes, n - 2, 1)).reshape(16, 8, n)
    at_first = jnp.logical_and(
        lax.broadcasted_iota(jnp.int32, (16, 8, n), 1) == 0, lax.broadcasted_iota(jnp.int32, (16, 8, n), 2) < 2
    )
    cosine, sine = twiddle_ref[0], twiddle_ref[1]
    for c in range(0, 8, 2):
        pair = [
            jnp.where(at_first, first[:, c + i : c + i + 1, :], part).reshape(n, n).astype(BF16)
            for i, part in enumerate(channel_pair(sig_ref, 8 * c))
        ]
        spectra = transform(pair, forward_ref, mix_ref, twiddle_ref)
        rows = []
        for i in range(2):
            real, imag = spectra[i * n : (i + 1) * n, :n], spectra[i * n : (i + 1) * n, n:]
            gain_real = gain_ref[c + i, 0] + extra[0, c + i : c + i + 1, 10:11]
            gain_imag = gain_ref[c + i, 1]
            rows.append(
                jnp.concatenate(
                    [real * gain_real - imag * gain_imag, real * gain_imag + imag * gain_real], axis=1
                )
            )
        parts = right_dot(jnp.concatenate(rows, axis=0), mix_ref, transposed=True)
        columns = []
        for i in range(2):
            real, imag = parts[i * n : (i + 1) * n, :n], parts[i * n : (i + 1) * n, n:]
            columns.append(
                jnp.concatenate([real * cosine + imag * sine, imag * cosine - real * sine], axis=0)
            )
        times = left_dot(forward_ref, jnp.concatenate(columns, axis=1)) * (1.0 / (n * n))
        blocks = [times[:, i * n : (i + 1) * n].reshape(16, 8, n) for i in range(2)]
        out_ref[:, 8 * c : 8 * c + 16, :] = jnp.concatenate(blocks, axis=1).astype(BF16)


def piece_block(j, z, core):
    return (z + 4 - j % 4) % 4 * 2 + (core if j < 4 else 1 - core)


def project_kernel(index_ref, *refs):
    pieces, refs = refs[:8], refs[8:]
    gain_ref, weight_ref, short_ref, skip_ref, message_ref, gate_ref, projected_ref, stacked_ref, turned_ref = refs
    rows, width = pieces[0].shape
    z, core = index_ref[0] // 2, index_ref[0] % 2
    gains = []
    for j in range(8):
        block = piece_block(j, z, core)
        gains.append(gain_ref[pl.ds(block, 1), :])
        source = pl.ds(pl.multiple_of(block * width, width), width)
        for k in range(3):
            stacked_ref[j * width : (j + 1) * width, k * width : (k + 1) * width] = weight_ref[k, source, :]
    projected_ref[:HALO, :] = jnp.zeros((HALO, 3 * width), F32)
    step = 256
    for start in range(0, rows, step):
        parts = [piece[start : start + step, :].astype(F32) for piece in pieces]
        total = sum(part * part for part in parts)
        inv_rms = lax.rsqrt(jnp.sum(total, axis=1, keepdims=True) * (1.0 / (8 * width)) + 1e-05)
        normed = jnp.concatenate([(part * inv_rms * gain).astype(BF16) for part, gain in zip(parts, gains)], axis=1)
        projected_ref[HALO + start : HALO + start + step, :] = dot(normed, stacked_ref[...])
    taps = [[short_ref[i, j : j + 1, :] for j in range(3)] for i in range(3)]
    for block in range(rows // LANES):
        start = block * LANES
        mixes = []
        for j in range(3):
            columns = slice(j * width, (j + 1) * width)
            mixes.append(
                sum(
                    taps[i][j] * projected_ref[HALO + start - i : HALO + start - i + LANES, columns]
                    for i in range(3)
                )
            )
        turned_ref[pl.ds(block, LANES, stride=8), :] = (mixes[0] * mixes[1]).T
        gate_ref[start : start + LANES, :] = mixes[2]
        if block == 0:
            early = [mixes[0][:2], mixes[1][:2]]
    later = []
    for j in range(3):
        columns = slice(j * width, (j + 1) * width)
        last = projected_ref[HALO + rows - 1 : HALO + rows, columns]
        before = projected_ref[HALO + rows - 2 : HALO + rows - 1, columns]
        later.append(jnp.concatenate([taps[1][j] * last + taps[2][j] * before, taps[2][j] * last], axis=0))
    extra = jnp.concatenate(early + later + [skip_ref[...], jnp.zeros((LANES - 11, width), F32)], axis=0).T
    high = extra.astype(BF16).astype(F32)
    message_ref[:, :64, :] = turned_ref[...].reshape(16, 64, LANES).astype(BF16)
    message_ref[:, 64:, :] = jnp.concatenate(
        [high.reshape(16, 8, LANES), (extra - high).reshape(16, 8, LANES)], axis=1
    ).astype(BF16)


def gate_kernel(index_ref, conv_ref, gate_ref, weight_ref, *refs):
    columns_refs, (out_ref, mine_ref, theirs_ref, turned_ref) = refs[:3], refs[3:]
    z, core = index_ref[0] // 2, index_ref[0] % 2
    for k in range(4):
        for ref, c in ((mine_ref, core), (theirs_ref, 1 - core)):
            start = c * LANES if k else (2 * z + c) * LANES
            source = columns_refs[k - 1] if k else weight_ref
            ref[k * LANES : (k + 1) * LANES, :] = source[:, pl.ds(pl.multiple_of(start, LANES), LANES)]
    turned_ref[...] = conv_ref[:, :64, :].astype(F32).reshape(turned_ref.shape)
    extra_high, extra_low = channel_pair(conv_ref, 64)
    late = (extra_high + extra_low).reshape(LANES, LANES).T[8:10]
    for block in range(gate_ref.shape[0] // LANES):
        rows = slice(block * LANES, (block + 1) * LANES)
        conv = turned_ref[pl.ds(block, LANES, stride=8), :].T
        gate = gate_ref[rows, :]
        if block == 0:
            gate = jnp.concatenate([gate[:2] + late, gate[2:]], axis=0)
        out_ref[rows, :] = (gate * conv).astype(BF16)


def output_kernel(*refs):
    gated, mine_ref, theirs_ref, tokens_ref, out_ref = refs[:8], *refs[8:]
    weight = jnp.concatenate([mine_ref[...], theirs_ref[...]], axis=0)
    step = 256
    for start in range(0, out_ref.shape[0], step):
        piece = slice(start, start + step)
        product = dot(jnp.concatenate([ref[piece, :] for ref in gated], axis=1), weight)
        out_ref[piece, :] = tokens_ref[piece, :].astype(F32) + product


def around(value, steps):
    count = lax.axis_size("chan")
    return lax.ppermute(value, "chan", [(i, (i + 2 * steps) % count) for i in range(count)])


def across(value):
    return lax.ppermute(value, "chan", [(i, i ^ 1) for i in range(lax.axis_size("chan"))])


def gather(value):
    mine = [value] + [around(value, steps) for steps in (1, 2, 3)]
    return mine + [across(piece) for piece in mine]


def after(*values):
    return lax.optimization_barrier(values)


def call(kernel, shapes, *operands, scalars=0, scratch=(), cost=None):
    smem = pl.BlockSpec(memory_space=pltpu.SMEM)
    return pl.pallas_call(
        kernel,
        out_shape=shapes,
        in_specs=[smem] * scalars + [VMEM] * (len(operands) - scalars),
        out_specs=jax.tree.map(lambda _: VMEM, shapes),
        scratch_shapes=scratch,
        cost_estimate=cost,
        compiler_params=pltpu.CompilerParams(vmem_limit_bytes=VMEM_LIMIT),
    )(*operands)


def local(tokens, norm_gain, in_weight, short_kernel, filter_fwd, filter_bwd, skip_gain, out_weight):
    seq_count = lax.axis_size("seq")
    chan_index = lax.axis_index("chan").reshape(1)
    rows, width = tokens.shape
    table = {name: jnp.asarray(value) for name, value in tables().items()}
    shape = jax.ShapeDtypeStruct
    turned = pltpu.VMEM((rows, width), F32)

    pieces = [tokens] + [around(tokens, steps) for steps in (1, 2, 3)]
    spread, *columns = call(
        spread_kernel,
        [shape((seq_count, 128, width), BF16)] + [shape((width, 2 * width), BF16)] * 3,
        chan_index,
        filter_fwd,
        filter_bwd,
        out_weight,
        scalars=1,
        scratch=[turned],
    )
    pieces = pieces + [across(piece) for piece in pieces]
    filters = lax.all_to_all(spread, "seq", 0, 0)
    shared = [table[name] for name in ("forward", "mix", "twiddle")]
    gain = call(filter_kernel, shape((8, 2, LANES, LANES), F32), filters, *shared)

    message, gate = call(
        project_kernel,
        [shape((seq_count, 80, width), BF16), shape((rows, width), F32)],
        chan_index,
        *pieces,
        norm_gain.reshape(-1, width),
        in_weight,
        short_kernel,
        skip_gain.reshape(1, width),
        scalars=1,
        scratch=[
            pltpu.VMEM((rows + HALO, 3 * width), F32),
            pltpu.VMEM((8 * width, 3 * width), BF16),
            turned,
        ],
        cost=pl.CostEstimate(flops=int(PROJECT_FLOPS), bytes_accessed=1, transcendentals=0),
    )
    message, filters = after(message, filters)
    signal = lax.all_to_all(message, "seq", 0, 0)
    conv = call(conv_kernel, shape((seq_count, 80, width), BF16), signal, gain, *shared)
    conv, *columns = after(conv, *columns)
    conv = lax.all_to_all(conv, "seq", 0, 0)
    columns = [around(column, steps) for column, steps in zip(columns, (1, 2, 3))]
    conv, *columns = after(conv, *columns)
    gated, mine, theirs = call(
        gate_kernel,
        [shape((rows, width), BF16)] + [shape((4 * width, width), BF16)] * 2,
        chan_index,
        conv,
        gate,
        out_weight,
        *columns,
        scalars=1,
        scratch=[turned],
    )
    return call(output_kernel, shape((rows, width), F32), *gather(gated), mine, across(theirs), tokens)


def solution(mesh):
    return jax.shard_map(
        local,
        mesh=mesh,
        in_specs=(
            P("seq", "chan"),
            P(),
            P(None, None, "chan"),
            P(None, None, "chan"),
            P("seq", "chan"),
            P("seq", "chan"),
            P("chan"),
            P("chan", None),
        ),
        out_specs=P("seq", "chan"),
        check_vma=False,
    )
```

time: 90.2 us -> 75.8 us (0.84)
  the two profiles are of different devices: /device:TPU:3 before, /device:TPU:1 now
where the time goes in v3:
time: 75.8 us; the launch traced here: 75.3 us
  starting transfers between devices  45.5 us (60%)
  waiting for transfers between devices  14.7 us (19%)
  Pallas kernels  11.2 us (15%)
  local copies, waits for them, and re-layouts  3.71 us (5%)
    ppermute x9, starting transfers between devices, across(): lax.ppermute(value, 'chan', [(i, i ^ 1) for i in range(lax.axis_size('cha...  17.3 us
    pallas_call x6, Pallas kernels, call(): pl.pallas_call(kernel, out_shape=shapes, in_specs=[smem] * scalars + [VME...  11.2 us
    ppermute x9, starting transfers between devices, around(): lax.ppermute(value, 'chan', [(i, (i + 2 * steps) % count) for i in range(...  11.1 us
    all_to_all x1, starting transfers between devices, local(): filters = lax.all_to_all(spread, 'seq', 0, 0)  6.89 us
    all_to_all x1, waiting for transfers between devices, local(): signal = lax.all_to_all(message, 'seq', 0, 0)  6.3 us
    all_to_all x1, starting transfers between devices, local(): signal = lax.all_to_all(message, 'seq', 0, 0)  6.13 us
    all_to_all x1, starting transfers between devices, local(): conv = lax.all_to_all(conv, 'seq', 0, 0)  4.16 us
    unnamed x24, local copies, waits for them, and re-layouts  3.71 us
  transfers between devices with their start and end apart: 21, of which 9 were waited for; matrix products, arithmetic and copies ran while one was open for 0% of the time, Pallas kernels for 7%

profile of v3, /device:TPU:1, one launch (start us, length us, event | category | flops | bytes accessed | tf_op | source)
XLA Modules:
  0.0 75.3 jit_solution(6064010377196363442)
XLA Ops:
  0.0 4.6 %collective-permute-start.2 = (bf16[1024,128]{1,0:T(8,128)(2,1)}, bf16[1024,128]{1,0:T(8,128)(2,1)S(1)}, u32[]{:S(2)}, u32[]{:S(2)}) collective-permute-start(bf16[1024,128]{1,0:T(8,128)(2,1)} %refs_10_.3), channel_id=1, source_target_pairs={{0,6},{1,7},{2,0},{3,1},{4,2},{5,3},{6,4},{7,5},{8,14},{9,15},{10,... | collective-permute-start | bytes 786440 | tf_op jit(solution)/shard_map/ppermute | solution.py:254
  4.6 0.7 collective-permute-start
  5.3 0.9 %copy-done = bf16[128,1024]{1,0:T(8,128)(2,1)S(1)} copy-done((bf16[128,1024]{1,0:T(8,128)(2,1)S(1)}, bf16[128,1024]{1,0:T(8,128)(2,1)}, u32[]{:S(2)}) %copy-start) | copy-done | bytes 262168
  6.2 1.0 %copy-done.3 = f32[1024,128]{1,0:T(8,128)S(1)} copy-done((f32[1024,128]{1,0:T(8,128)S(1)}, f32[1024,128]{1,0:T(8,128)}, u32[]{:S(2)}) %copy-start.3) | copy-done | bytes 524312
  7.3 1.0 %copy-done.4 = f32[1024,128]{1,0:T(8,128)S(1)} copy-done((f32[1024,128]{1,0:T(8,128)S(1)}, f32[1024,128]{1,0:T(8,128)}, u32[]{:S(2)}) %copy-start.4) | copy-done | bytes 524312
  8.3 1.2 %shard_map.110 = (bf16[16,128,128]{2,1,0:T(8,128)(2,1)}, bf16[128,256]{1,0:T(8,128)(2,1)S(1)}, bf16[128,256]{1,0:T(8,128)(2,1)S(1)}, bf16[128,256]{1,0:T(8,128)(2,1)S(1)}) custom-call(s32[1]{0:T(128)} %bitcast.index_ref, f32[1024,128]{1,0:T(8,128)S(1)} %copy-done.3, f32[1024,128]{1,0:T(8,128)S(1)} %copy-done.4, bf16[128,1024]{1,0:T(8,128)(2,1)S(1)} %copy-done), custom_call_target="tpu_custom_call" | custom-call | tf_op jit(solution)/shard_map/pallas_call | solution.py:272
  9.5 6.9 %all-to-all-start = ((bf16[16,128,128]{2,1,0:T(8,128)(2,1)}), bf16[16,128,128]{2,1,0:T(8,128)(2,1)S(1)}, u32[]{:S(2)}, u32[]{:S(2)}) async-start(bf16[16,128,128]{2,1,0:T(8,128)(2,1)} %get-tuple-element.24), calls=%async_computation | async-start | bytes 1048576 | tf_op jit(solution)/shard_map/all_to_all | solution.py:303
  16.4 1.9 %collective-permute-start.3 = (bf16[1024,128]{1,0:T(8,128)(2,1)S(1)}, bf16[1024,128]{1,0:T(8,128)(2,1)S(1)}, u32[]{:S(2)}, u32[]{:S(2)}) collective-permute-start(bf16[1024,128]{1,0:T(8,128)(2,1)S(1)} %copy-done.7), channel_id=1, source_target_pairs={{0,1},{1,0},{2,3},{3,2},{4,5},{5,4},{6,7},{7,6},{8,9},{9,8},{10,11... | collective-permute-start | bytes 786440 | tf_op jit(solution)/shard_map/ppermute | solution.py:258
  18.8 0.7 collective-permute-done.refs_1_
  19.5 0.8 %collective-permute-start.4 = (bf16[1024,128]{1,0:T(8,128)(2,1)S(1)}, bf16[1024,128]{1,0:T(8,128)(2,1)S(1)}, u32[]{:S(2)}, u32[]{:S(2)}) collective-permute-start(bf16[1024,128]{1,0:T(8,128)(2,1)S(1)} %collective-permute-done.refs_1_), channel_id=1, source_target_pairs={{0,1},{1,0},{2,3},{3,2},{4,5},{5,4},{6,7},{7,6},{8,9},{9,8},{10,11... | collective-permute-start | bytes 786440 | tf_op jit(solution)/shard_map/ppermute | solution.py:258
  20.4 1.1 %collective-permute-done.4.refs_5_ = bf16[1024,128]{1,0:T(8,128)(2,1)S(1)} collective-permute-done((bf16[1024,128]{1,0:T(8,128)(2,1)S(1)}, bf16[1024,128]{1,0:T(8,128)(2,1)S(1)}, u32[]{:S(2)}, u32[]{:S(2)}) %collective-permute-start.4) | collective-permute-done | bytes 262176 | tf_op jit(solution)/shard_map/ppermute | solution.py:258
  22.2 2.6 %shard_map.109 = (bf16[16,80,128]{2,1,0:T(8,128)(2,1)}, f32[1024,128]{1,0:T(8,128)S(1)}) custom-call(s32[1]{0:T(128)} %bitcast.index_ref, bf16[1024,128]{1,0:T(8,128)(2,1)S(1)} %copy-done.7, bf16[1024,128]{1,0:T(8,128)(2,1)S(1)} %collective-permute-done.refs_1_, bf16[1024,128]{1,0:T(8,128)(2,1)S(1)} %collective-permute-done.1.refs_2_, ...), custom_call_target="tpu_custom_call" | custom-call | flops 1500000000 | bytes 1 | tf_op jit(solution)/shard_map/pallas_call | solution.py:272
  24.8 0.8 %all-to-all-done.filt_ref = bf16[16,128,128]{2,1,0:T(8,128)(2,1)S(1)} async-done(((bf16[16,128,128]{2,1,0:T(8,128)(2,1)}), bf16[16,128,128]{2,1,0:T(8,128)(2,1)S(1)}, u32[]{:S(2)}, u32[]{:S(2)}) %all-to-all-start) | async-done | bytes 524320 | tf_op jit(solution)/shard_map/all_to_all | solution.py:303
  25.6 6.1 %all-to-all-start.1 = ((bf16[16,80,128]{2,1,0:T(8,128)(2,1)}), bf16[16,80,128]{2,1,0:T(8,128)(2,1)S(1)}, u32[]{:S(2)}, u32[]{:S(2)}) async-start(bf16[16,80,128]{2,1,0:T(8,128)(2,1)} %get-tuple-element.25), calls=%async_computation.1 | async-start | bytes 655360 | tf_op jit(solution)/shard_map/all_to_all | solution.py:325
  31.8 1.5 %shard_map.111.gain_ref = f32[8,2,128,128]{3,2,1,0:T(8,128)S(1)} custom-call(bf16[16,128,128]{2,1,0:T(8,128)(2,1)S(1)} %all-to-all-done.filt_ref, bf16[256,256]{1,0:T(8,128)(2,1)S(1)} %copy-done.6, bf16[512,256]{1,0:T(8,128)(2,1)S(1)} %copy-done.2, f32[2,128,128]{2,1,0:T(8,128)S(1)} %copy-done.5), custom_call_target="tpu_custom_call" | custom-call | tf_op jit(solution)/shard_map/pallas_call | solution.py:272
  33.2 6.3 %all-to-all-done.1.sig_ref = bf16[16,80,128]{2,1,0:T(8,128)(2,1)S(1)} async-done(((bf16[16,80,128]{2,1,0:T(8,128)(2,1)}), bf16[16,80,128]{2,1,0:T(8,128)(2,1)S(1)}, u32[]{:S(2)}, u32[]{:S(2)}) %all-to-all-start.1) | async-done | bytes 327712 | tf_op jit(solution)/shard_map/all_to_all | solution.py:325
  39.5 4.1 %shard_map.112 = bf16[16,80,128]{2,1,0:T(8,128)(2,1)} custom-call(bf16[16,80,128]{2,1,0:T(8,128)(2,1)S(1)} %all-to-all-done.1.sig_ref, f32[8,2,128,128]{3,2,1,0:T(8,128)S(1)} %shard_map.111.gain_ref, bf16[256,256]{1,0:T(8,128)(2,1)S(1)} %copy-done.6, bf16[512,256]{1,0:T(8,128)(2,1)S(1)} %copy-done.2, f32[2,128,128]{2,1,0:T(8,128)S(1)} %copy-done.5), custom_call_target="tpu_custom_call" | custom-call | tf_op jit(solution)/shard_map/pallas_call | solution.py:272
  43.7 4.2 %all-to-all-start.2 = ((bf16[16,80,128]{2,1,0:T(8,128)(2,1)}), bf16[16,80,128]{2,1,0:T(8,128)(2,1)S(1)}, u32[]{:S(2)}, u32[]{:S(2)}) async-start(bf16[16,80,128]{2,1,0:T(8,128)(2,1)} %shard_map.112), calls=%async_computation.2 | async-start | bytes 655360 | tf_op jit(solution)/shard_map/all_to_all | solution.py:328
  47.9 0.8 %collective-permute-start.7 = (bf16[128,256]{1,0:T(8,128)(2,1)S(1)}, bf16[128,256]{1,0:T(8,128)(2,1)S(1)}, u32[]{:S(2)}, u32[]{:S(2)}) collective-permute-start(bf16[128,256]{1,0:T(8,128)(2,1)S(1)} %get-tuple-element.30), channel_id=1, source_target_pairs={{0,2},{1,3},{2,4},{3,5},{4,6},{5,7},{6,0},{7,1},{8,10},{9,11},{10,... | collective-permute-start | bytes 196616 | tf_op jit(solution)/shard_map/ppermute | solution.py:254
  48.6 0.9 %collective-permute-start.8 = (bf16[128,256]{1,0:T(8,128)(2,1)S(1)}, bf16[128,256]{1,0:T(8,128)(2,1)S(1)}, u32[]{:S(2)}, u32[]{:S(2)}) collective-permute-start(bf16[128,256]{1,0:T(8,128)(2,1)S(1)} %get-tuple-element.31), channel_id=1, source_target_pairs={{0,4},{1,5},{2,6},{3,7},{4,0},{5,1},{6,2},{7,3},{8,12},{9,13},{10,... | collective-permute-start | bytes 196616 | tf_op jit(solution)/shard_map/ppermute | solution.py:254
  49.6 1.6 %collective-permute-start.9 = (bf16[128,256]{1,0:T(8,128)(2,1)S(1)}, bf16[128,256]{1,0:T(8,128)(2,1)S(1)}, u32[]{:S(2)}, u32[]{:S(2)}) collective-permute-start(bf16[128,256]{1,0:T(8,128)(2,1)S(1)} %get-tuple-element.32), channel_id=1, source_target_pairs={{0,6},{1,7},{2,0},{3,1},{4,2},{5,3},{6,4},{7,5},{8,14},{9,15},{10,... | collective-permute-start | bytes 196616 | tf_op jit(solution)/shard_map/ppermute | solution.py:254
  51.1 1.1 %collective-permute-done.7.refs_0_ = bf16[128,256]{1,0:T(8,128)(2,1)S(1)} collective-permute-done((bf16[128,256]{1,0:T(8,128)(2,1)S(1)}, bf16[128,256]{1,0:T(8,128)(2,1)S(1)}, u32[]{:S(2)}, u32[]{:S(2)}) %collective-permute-start.7) | collective-permute-done | bytes 65568 | tf_op jit(solution)/shard_map/ppermute | solution.py:254
  52.3 1.0 %collective-permute-done.8.refs_1_ = bf16[128,256]{1,0:T(8,128)(2,1)S(1)} collective-permute-done((bf16[128,256]{1,0:T(8,128)(2,1)S(1)}, bf16[128,256]{1,0:T(8,128)(2,1)S(1)}, u32[]{:S(2)}, u32[]{:S(2)}) %collective-permute-start.8) | collective-permute-done | bytes 65568 | tf_op jit(solution)/shard_map/ppermute | solution.py:254
  53.8 1.8 %all-to-all-done.2.conv_ref = bf16[16,80,128]{2,1,0:T(8,128)(2,1)S(1)} async-done(((bf16[16,80,128]{2,1,0:T(8,128)(2,1)}), bf16[16,80,128]{2,1,0:T(8,128)(2,1)S(1)}, u32[]{:S(2)}, u32[]{:S(2)}) %all-to-all-start.2) | async-done | bytes 327712 | tf_op jit(solution)/shard_map/all_to_all | solution.py:328
  55.8 0.8 %collective-permute-start.12 = (bf16[1024,128]{1,0:T(8,128)(2,1)S(1)}, bf16[1024,128]{1,0:T(8,128)(2,1)S(1)}, u32[]{:S(2)}, u32[]{:S(2)}) collective-permute-start(bf16[1024,128]{1,0:T(8,128)(2,1)S(1)} %get-tuple-element.38.refs_0_), channel_id=1, source_target_pairs={{0,6},{1,7},{2,0},{3,1},{4,2},{5,3},{6,4},{7,5},{8,14},{9,15},{10,... | collective-permute-start | bytes 786440 | tf_op jit(solution)/shard_map/ppermute | solution.py:254
  56.5 1.8 %collective-permute-start.11 = (bf16[1024,128]{1,0:T(8,128)(2,1)S(1)}, bf16[1024,128]{1,0:T(8,128)(2,1)S(1)}, u32[]{:S(2)}, u32[]{:S(2)}) collective-permute-start(bf16[1024,128]{1,0:T(8,128)(2,1)S(1)} %get-tuple-element.38.refs_0_), channel_id=1, source_target_pairs={{0,4},{1,5},{2,6},{3,7},{4,0},{5,1},{6,2},{7,3},{8,12},{9,13},{10,... | collective-permute-start | bytes 786440 | tf_op jit(solution)/shard_map/ppermute | solution.py:254
  58.3 4.4 %collective-permute-start.13 = (bf16[1024,128]{1,0:T(8,128)(2,1)S(1)}, bf16[1024,128]{1,0:T(8,128)(2,1)S(1)}, u32[]{:S(2)}, u32[]{:S(2)}) collective-permute-start(bf16[1024,128]{1,0:T(8,128)(2,1)S(1)} %get-tuple-element.38.refs_0_), channel_id=1, source_target_pairs={{0,1},{1,0},{2,3},{3,2},{4,5},{5,4},{6,7},{7,6},{8,9},{9,8},{10,11... | collective-permute-start | bytes 786440 | tf_op jit(solution)/shard_map/ppermute | solution.py:258
  62.7 4.6 %collective-permute-start.16 = (bf16[1024,128]{1,0:T(8,128)(2,1)S(1)}, bf16[1024,128]{1,0:T(8,128)(2,1)S(1)}, u32[]{:S(2)}, u32[]{:S(2)}) collective-permute-start(bf16[1024,128]{1,0:T(8,128)(2,1)S(1)} %collective-permute-done.12.refs_3_), channel_id=1, source_target_pairs={{0,1},{1,0},{2,3},{3,2},{4,5},{5,4},{6,7},{7,6},{8,9},{9,8},{10,11... | collective-permute-start | bytes 786440 | tf_op jit(solution)/shard_map/ppermute | solution.py:258
  67.4 2.3 %collective-permute-start.15 = (bf16[1024,128]{1,0:T(8,128)(2,1)S(1)}, bf16[1024,128]{1,0:T(8,128)(2,1)S(1)}, u32[]{:S(2)}, u32[]{:S(2)}) collective-permute-start(bf16[1024,128]{1,0:T(8,128)(2,1)S(1)} %collective-permute-done.11.refs_2_), channel_id=1, source_target_pairs={{0,1},{1,0},{2,3},{3,2},{4,5},{5,4},{6,7},{7,6},{8,9},{9,8},{10,11... | collective-permute-start | bytes 786440 | tf_op jit(solution)/shard_map/ppermute | solution.py:258
  69.7 2.7 %collective-permute-start.14 = (bf16[1024,128]{1,0:T(8,128)(2,1)S(1)}, bf16[1024,128]{1,0:T(8,128)(2,1)S(1)}, u32[]{:S(2)}, u32[]{:S(2)}) collective-permute-start(bf16[1024,128]{1,0:T(8,128)(2,1)S(1)} %collective-permute-done.10.refs_1_), channel_id=1, source_target_pairs={{0,1},{1,0},{2,3},{3,2},{4,5},{5,4},{6,7},{7,6},{8,9},{9,8},{10,11... | collective-permute-start | bytes 786440 | tf_op jit(solution)/shard_map/ppermute | solution.py:258
  72.4 1.3 %collective-permute-done.17.refs_9_ = bf16[512,128]{1,0:T(8,128)(2,1)S(1)} collective-permute-done((bf16[512,128]{1,0:T(8,128)(2,1)S(1)}, bf16[512,128]{1,0:T(8,128)(2,1)S(1)}, u32[]{:S(2)}, u32[]{:S(2)}) %collective-permute-start.17) | collective-permute-done | bytes 131104 | tf_op jit(solution)/shard_map/ppermute | solution.py:258
  73.8 1.5 %shard_map.114 = f32[1024,128]{1,0:T(8,128)} custom-call(bf16[1024,128]{1,0:T(8,128)(2,1)S(1)} %get-tuple-element.38.refs_0_, bf16[1024,128]{1,0:T(8,128)(2,1)S(1)} %collective-permute-done.10.refs_1_, bf16[1024,128]{1,0:T(8,128)(2,1)S(1)} %collective-permute-done.11.refs_2_, bf16[1024,128]{1,0:T(8,128)(2,1)S(1)} %collective-permute-done.12.refs_3_, ...), custom_call_target="tpu_custom_call" | custom-call | tf_op jit(solution)/shard_map/pallas_call | solution.py:272
  (40 shorter events, 2.0 us)
Async XLA Ops:
  0.0 18.3 %collective-permute-start.2 = (bf16[1024,128]{1,0:T(8,128)(2,1)}, bf16[1024,128]{1,0:T(8,128)(2,1)S(1)}, u32[]{:S(2)}, u32[]{:S(2)}) collective-permute-start(bf16[1024,128]{1,0:T(8,128)(2,1)} %refs_10_.3), channel_id=1, source_target_pairs={{0,6},{1,7},{2,0},{3,1},{4,2},{5,3},{6,4},{7,5},{8,14},{9,15},{10,... | collective-permute-start | bytes 786440 | tf_op jit(solution)/shard_map/ppermute | solution.py:254
  4.6 13.8 %collective-permute-start.1 = (bf16[1024,128]{1,0:T(8,128)(2,1)}, bf16[1024,128]{1,0:T(8,128)(2,1)S(1)}, u32[]{:S(2)}, u32[]{:S(2)}) collective-permute-start(bf16[1024,128]{1,0:T(8,128)(2,1)} %refs_10_.3), channel_id=1, source_target_pairs={{0,4},{1,5},{2,6},{3,7},{4,0},{5,1},{6,2},{7,3},{8,12},{9,13},{10,... | collective-permute-start | bytes 786440 | tf_op jit(solution)/shard_map/ppermute | solution.py:254
  4.6 14.9 %collective-permute-start = (bf16[1024,128]{1,0:T(8,128)(2,1)}, bf16[1024,128]{1,0:T(8,128)(2,1)S(1)}, u32[]{:S(2)}, u32[]{:S(2)}) collective-permute-start(bf16[1024,128]{1,0:T(8,128)(2,1)} %refs_10_.3), channel_id=1, source_target_pairs={{0,2},{1,3},{2,4},{3,5},{4,6},{5,7},{6,0},{7,1},{8,10},{9,11},{10,... | collective-permute-start | bytes 786440 | tf_op jit(solution)/shard_map/ppermute | solution.py:254
  5.3 0.9 %copy-start = (bf16[128,1024]{1,0:T(8,128)(2,1)S(1)}, bf16[128,1024]{1,0:T(8,128)(2,1)}, u32[]{:S(2)}) copy-start(bf16[128,1024]{1,0:T(8,128)(2,1)} %weight_ref.3) | copy-start | bytes 786436
  6.2 1.0 %copy-start.3 = (f32[1024,128]{1,0:T(8,128)S(1)}, f32[1024,128]{1,0:T(8,128)}, u32[]{:S(2)}) copy-start(f32[1024,128]{1,0:T(8,128)} %fwd_ref.1) | copy-start | bytes 1572868
  7.3 1.0 %copy-start.4 = (f32[1024,128]{1,0:T(8,128)S(1)}, f32[1024,128]{1,0:T(8,128)}, u32[]{:S(2)}) copy-start(f32[1024,128]{1,0:T(8,128)} %bwd_ref.1) | copy-start | bytes 1572868
  8.3 13.2 %copy-start.9 = (f32[3,3,128]{2,1,0:T(4,128)S(1)}, f32[3,3,128]{2,1,0:T(4,128)}, u32[]{:S(2)}) copy-start(f32[3,3,128]{2,1,0:T(4,128)} %refs_10_.2) | copy-start | bytes 13828
  9.5 12.0 %copy-start.8 = (bf16[3,1024,128]{2,1,0:T(8,128)(2,1)S(1)}, bf16[3,1024,128]{2,1,0:T(8,128)(2,1)}, u32[]{:S(2)}) copy-start(bf16[3,1024,128]{2,1,0:T(8,128)(2,1)} %refs_9_.1) | copy-start | bytes 2359300
  9.5 6.9 %copy-start.7 = (bf16[1024,128]{1,0:T(8,128)(2,1)S(1)}, bf16[1024,128]{1,0:T(8,128)(2,1)}, u32[]{:S(2)}) copy-start(bf16[1024,128]{1,0:T(8,128)(2,1)} %refs_10_.3) | copy-start | bytes 786436
  9.5 12.0 %copy-start.10 = (f32[1024]{0:T(1024)S(1)}, f32[1024]{0:T(1024)}, u32[]{:S(2)}) copy-start(f32[1024]{0:T(1024)} %param.12) | copy-start | bytes 12292
  9.5 16.1 %all-to-all-start = ((bf16[16,128,128]{2,1,0:T(8,128)(2,1)}), bf16[16,128,128]{2,1,0:T(8,128)(2,1)S(1)}, u32[]{:S(2)}, u32[]{:S(2)}) async-start(bf16[16,128,128]{2,1,0:T(8,128)(2,1)} %get-tuple-element.24), calls=%async_computation | async-start | bytes 1048576 | tf_op jit(solution)/shard_map/all_to_all | solution.py:303
  16.4 3.9 %collective-permute-start.3 = (bf16[1024,128]{1,0:T(8,128)(2,1)S(1)}, bf16[1024,128]{1,0:T(8,128)(2,1)S(1)}, u32[]{:S(2)}, u32[]{:S(2)}) collective-permute-start(bf16[1024,128]{1,0:T(8,128)(2,1)S(1)} %copy-done.7), channel_id=1, source_target_pairs={{0,1},{1,0},{2,3},{3,2},{4,5},{5,4},{6,7},{7,6},{8,9},{9,8},{10,11... | collective-permute-start | bytes 786440 | tf_op jit(solution)/shard_map/ppermute | solution.py:258
  18.3 2.1 %collective-permute-start.6 = (bf16[1024,128]{1,0:T(8,128)(2,1)S(1)}, bf16[1024,128]{1,0:T(8,128)(2,1)S(1)}, u32[]{:S(2)}, u32[]{:S(2)}) collective-permute-start(bf16[1024,128]{1,0:T(8,128)(2,1)S(1)} %collective-permute-done.2.refs_3_), channel_id=1, source_target_pairs={{0,1},{1,0},{2,3},{3,2},{4,5},{5,4},{6,7},{7,6},{8,9},{9,8},{10,11... | collective-permute-start | bytes 786440 | tf_op jit(solution)/shard_map/ppermute | solution.py:258
  18.4 2.0 %collective-permute-start.5 = (bf16[1024,128]{1,0:T(8,128)(2,1)S(1)}, bf16[1024,128]{1,0:T(8,128)(2,1)S(1)}, u32[]{:S(2)}, u32[]{:S(2)}) collective-permute-start(bf16[1024,128]{1,0:T(8,128)(2,1)S(1)} %collective-permute-done.1.refs_2_), channel_id=1, source_target_pairs={{0,1},{1,0},{2,3},{3,2},{4,5},{5,4},{6,7},{7,6},{8,9},{9,8},{10,11... | collective-permute-start | bytes 786440 | tf_op jit(solution)/shard_map/ppermute | solution.py:258
  19.5 2.0 %collective-permute-start.4 = (bf16[1024,128]{1,0:T(8,128)(2,1)S(1)}, bf16[1024,128]{1,0:T(8,128)(2,1)S(1)}, u32[]{:S(2)}, u32[]{:S(2)}) collective-permute-start(bf16[1024,128]{1,0:T(8,128)(2,1)S(1)} %collective-permute-done.refs_1_), channel_id=1, source_target_pairs={{0,1},{1,0},{2,3},{3,2},{4,5},{5,4},{6,7},{7,6},{8,9},{9,8},{10,11... | collective-permute-start | bytes 786440 | tf_op jit(solution)/shard_map/ppermute | solution.py:258
  25.6 6.1 %copy-start.2 = (bf16[512,256]{1,0:T(8,128)(2,1)S(1)}, bf16[512,256]{1,0:T(8,128)(2,1)}, u32[]{:S(2)}) copy-start(bf16[512,256]{1,0:T(8,128)(2,1)} %constant.11.clone.mix_ref) | copy-start | bytes 786436
  25.6 6.2 %copy-start.5 = (f32[2,128,128]{2,1,0:T(8,128)S(1)}, f32[2,128,128]{2,1,0:T(8,128)}, u32[]{:S(2)}) copy-start(f32[2,128,128]{2,1,0:T(8,128)} %constant.12.clone.twiddle_ref) | copy-start | bytes 393220
  25.6 6.2 %copy-start.6 = (bf16[256,256]{1,0:T(8,128)(2,1)S(1)}, bf16[256,256]{1,0:T(8,128)(2,1)}, u32[]{:S(2)}) copy-start(bf16[256,256]{1,0:T(8,128)(2,1)} %constant.10.clone.forward_ref) | copy-start | bytes 393220
  25.6 14.0 %all-to-all-start.1 = ((bf16[16,80,128]{2,1,0:T(8,128)(2,1)}), bf16[16,80,128]{2,1,0:T(8,128)(2,1)S(1)}, u32[]{:S(2)}, u32[]{:S(2)}) async-start(bf16[16,80,128]{2,1,0:T(8,128)(2,1)} %get-tuple-element.25), calls=%async_computation.1 | async-start | bytes 655360 | tf_op jit(solution)/shard_map/all_to_all | solution.py:325
  43.7 11.8 %copy-start.1 = (bf16[128,1024]{1,0:T(8,128)(2,1)S(1)}, bf16[128,1024]{1,0:T(8,128)(2,1)}, u32[]{:S(2)}) copy-start(bf16[128,1024]{1,0:T(8,128)(2,1)} %weight_ref.3) | copy-start | bytes 786436
  43.7 11.8 %all-to-all-start.2 = ((bf16[16,80,128]{2,1,0:T(8,128)(2,1)}), bf16[16,80,128]{2,1,0:T(8,128)(2,1)S(1)}, u32[]{:S(2)}, u32[]{:S(2)}) async-start(bf16[16,80,128]{2,1,0:T(8,128)(2,1)} %shard_map.112), calls=%async_computation.2 | async-start | bytes 655360 | tf_op jit(solution)/shard_map/all_to_all | solution.py:328
  47.9 4.4 %collective-permute-start.7 = (bf16[128,256]{1,0:T(8,128)(2,1)S(1)}, bf16[128,256]{1,0:T(8,128)(2,1)S(1)}, u32[]{:S(2)}, u32[]{:S(2)}) collective-permute-start(bf16[128,256]{1,0:T(8,128)(2,1)S(1)} %get-tuple-element.30), channel_id=1, source_target_pairs={{0,2},{1,3},{2,4},{3,5},{4,6},{5,7},{6,0},{7,1},{8,10},{9,11},{10,... | collective-permute-start | bytes 196616 | tf_op jit(solution)/shard_map/ppermute | solution.py:254
  48.6 4.6 %collective-permute-start.8 = (bf16[128,256]{1,0:T(8,128)(2,1)S(1)}, bf16[128,256]{1,0:T(8,128)(2,1)S(1)}, u32[]{:S(2)}, u32[]{:S(2)}) collective-permute-start(bf16[128,256]{1,0:T(8,128)(2,1)S(1)} %get-tuple-element.31), channel_id=1, source_target_pairs={{0,4},{1,5},{2,6},{3,7},{4,0},{5,1},{6,2},{7,3},{8,12},{9,13},{10,... | collective-permute-start | bytes 196616 | tf_op jit(solution)/shard_map/ppermute | solution.py:254
  49.6 4.2 %collective-permute-start.9 = (bf16[128,256]{1,0:T(8,128)(2,1)S(1)}, bf16[128,256]{1,0:T(8,128)(2,1)S(1)}, u32[]{:S(2)}, u32[]{:S(2)}) collective-permute-start(bf16[128,256]{1,0:T(8,128)(2,1)S(1)} %get-tuple-element.32), channel_id=1, source_target_pairs={{0,6},{1,7},{2,0},{3,1},{4,2},{5,3},{6,4},{7,5},{8,14},{9,15},{10,... | collective-permute-start | bytes 196616 | tf_op jit(solution)/shard_map/ppermute | solution.py:254
  55.8 7.0 %collective-permute-start.12 = (bf16[1024,128]{1,0:T(8,128)(2,1)S(1)}, bf16[1024,128]{1,0:T(8,128)(2,1)S(1)}, u32[]{:S(2)}, u32[]{:S(2)}) collective-permute-start(bf16[1024,128]{1,0:T(8,128)(2,1)S(1)} %get-tuple-element.38.refs_0_), channel_id=1, source_target_pairs={{0,6},{1,7},{2,0},{3,1},{4,2},{5,3},{6,4},{7,5},{8,14},{9,15},{10,... | collective-permute-start | bytes 786440 | tf_op jit(solution)/shard_map/ppermute | solution.py:254
  56.5 10.8 %collective-permute-start.11 = (bf16[1024,128]{1,0:T(8,128)(2,1)S(1)}, bf16[1024,128]{1,0:T(8,128)(2,1)S(1)}, u32[]{:S(2)}, u32[]{:S(2)}) collective-permute-start(bf16[1024,128]{1,0:T(8,128)(2,1)S(1)} %get-tuple-element.38.refs_0_), channel_id=1, source_target_pairs={{0,4},{1,5},{2,6},{3,7},{4,0},{5,1},{6,2},{7,3},{8,12},{9,13},{10,... | collective-permute-start | bytes 786440 | tf_op jit(solution)/shard_map/ppermute | solution.py:254
  58.3 11.4 %collective-permute-start.10 = (bf16[1024,128]{1,0:T(8,128)(2,1)S(1)}, bf16[1024,128]{1,0:T(8,128)(2,1)S(1)}, u32[]{:S(2)}, u32[]{:S(2)}) collective-permute-start(bf16[1024,128]{1,0:T(8,128)(2,1)S(1)} %get-tuple-element.38.refs_0_), channel_id=1, source_target_pairs={{0,2},{1,3},{2,4},{3,5},{4,6},{5,7},{6,0},{7,1},{8,10},{9,11},{10,... | collective-permute-start | bytes 786440 | tf_op jit(solution)/shard_map/ppermute | solution.py:254
  58.3 15.4 %collective-permute-start.13 = (bf16[1024,128]{1,0:T(8,128)(2,1)S(1)}, bf16[1024,128]{1,0:T(8,128)(2,1)S(1)}, u32[]{:S(2)}, u32[]{:S(2)}) collective-permute-start(bf16[1024,128]{1,0:T(8,128)(2,1)S(1)} %get-tuple-element.38.refs_0_), channel_id=1, source_target_pairs={{0,1},{1,0},{2,3},{3,2},{4,5},{5,4},{6,7},{7,6},{8,9},{9,8},{10,11... | collective-permute-start | bytes 786440 | tf_op jit(solution)/shard_map/ppermute | solution.py:258
  62.7 11.0 %collective-permute-start.16 = (bf16[1024,128]{1,0:T(8,128)(2,1)S(1)}, bf16[1024,128]{1,0:T(8,128)(2,1)S(1)}, u32[]{:S(2)}, u32[]{:S(2)}) collective-permute-start(bf16[1024,128]{1,0:T(8,128)(2,1)S(1)} %collective-permute-done.12.refs_3_), channel_id=1, source_target_pairs={{0,1},{1,0},{2,3},{3,2},{4,5},{5,4},{6,7},{7,6},{8,9},{9,8},{10,11... | collective-permute-start | bytes 786440 | tf_op jit(solution)/shard_map/ppermute | solution.py:258
  67.4 6.4 %collective-permute-start.15 = (bf16[1024,128]{1,0:T(8,128)(2,1)S(1)}, bf16[1024,128]{1,0:T(8,128)(2,1)S(1)}, u32[]{:S(2)}, u32[]{:S(2)}) collective-permute-start(bf16[1024,128]{1,0:T(8,128)(2,1)S(1)} %collective-permute-done.11.refs_2_), channel_id=1, source_target_pairs={{0,1},{1,0},{2,3},{3,2},{4,5},{5,4},{6,7},{7,6},{8,9},{9,8},{10,11... | collective-permute-start | bytes 786440 | tf_op jit(solution)/shard_map/ppermute | solution.py:258
  69.7 4.1 %collective-permute-start.14 = (bf16[1024,128]{1,0:T(8,128)(2,1)S(1)}, bf16[1024,128]{1,0:T(8,128)(2,1)S(1)}, u32[]{:S(2)}, u32[]{:S(2)}) collective-permute-start(bf16[1024,128]{1,0:T(8,128)(2,1)S(1)} %collective-permute-done.10.refs_1_), channel_id=1, source_target_pairs={{0,1},{1,0},{2,3},{3,2},{4,5},{5,4},{6,7},{7,6},{8,9},{9,8},{10,11... | collective-permute-start | bytes 786440 | tf_op jit(solution)/shard_map/ppermute | solution.py:258
  72.4 1.3 %collective-permute-start.17 = (bf16[512,128]{1,0:T(8,128)(2,1)S(1)}, bf16[512,128]{1,0:T(8,128)(2,1)S(1)}, u32[]{:S(2)}, u32[]{:S(2)}) collective-permute-start(bf16[512,128]{1,0:T(8,128)(2,1)S(1)} %get-tuple-element.40), channel_id=1, source_target_pairs={{0,1},{1,0},{2,3},{3,2},{4,5},{5,4},{6,7},{7,6},{8,9},{9,8},{10,11... | collective-permute-start | bytes 393224 | tf_op jit(solution)/shard_map/ppermute | solution.py:258
  (1 other events, 0.7 us)

commit v4 on v3

--- a/solution.py
+++ b/solution.py
@@ -56,21 +56,16 @@
 
 def left_dot(table_ref, value):
     high, low = halves(value)
-    table_hi, table_lo = [table_ref[:, i * LANES : (i + 1) * LANES].T for i in range(2)]
-    return dot(
-        jnp.concatenate([table_hi, table_lo, table_hi], axis=1), jnp.concatenate([high, high, low], axis=0)
-    )
-
-
-def right_dot(value, table_ref, transposed=False):
+    depth = value.shape[0]
+    table_hi, table_lo = table_ref[:, :depth], table_ref[:, depth:]
+    return dot(jnp.concatenate([table_hi, table_lo, table_hi], axis=1), jnp.concatenate([high, high, low], axis=0))
+
+
+def right_dot(value, table_ref):
     high, low = halves(value)
     depth = value.shape[1]
     table_hi, table_lo = table_ref[:depth], table_ref[depth:]
-    left = jnp.concatenate([high, low, high], axis=1)
-    if transposed:
-        right = jnp.concatenate([table_hi, table_hi, table_lo], axis=1)
-        return lax.dot_general(left, right, (((1,), (1,)), ((), ())), preferred_element_type=F32)
-    return dot(left, jnp.concatenate([table_hi, table_hi, table_lo], axis=0))
+    return dot(jnp.concatenate([high, low, high], axis=1), jnp.concatenate([table_hi, table_hi, table_lo], axis=0))
 
 
 def transform(sequences, forward_ref, mix_ref, twiddle_ref):
@@ -86,16 +81,41 @@
     return right_dot(jnp.concatenate(rows, axis=0), mix_ref)
 
 
+def fetch(pairs, sems):
+    copies = [pltpu.make_async_copy(source, target, sems.at[i]) for i, (source, target) in enumerate(pairs)]
+    for copy in copies:
+        copy.start()
+    return copies
+
+
 def spread_kernel(index_ref, fwd_ref, bwd_ref, weight_ref, out_ref, *refs):
-    columns_refs, turned_ref = refs[:3], refs[3]
+    columns_refs, (held_ref, turned_ref, sems, column_sems) = refs[:3], refs[3:]
+    step = 2 * LANES
+    places = [(which, start) for which in range(2) for start in range(0, fwd_ref.shape[0], step)]
+    copies = fetch(
+        [
+            ((fwd_ref, bwd_ref)[which].at[pl.ds(start, step), :], held_ref.at[which, pl.ds(start, step), :])
+            for which, start in places
+        ],
+        sems,
+    )
     z = index_ref[0] // 2
-    for steps, columns_ref in enumerate(columns_refs):
-        start = pl.multiple_of((z + steps + 1) % 4 * 2 * LANES, 2 * LANES)
-        columns_ref[...] = weight_ref[:, pl.ds(start, 2 * LANES)]
-    for which, source in enumerate((fwd_ref, bwd_ref)):
-        for block in range(source.shape[0] // LANES):
-            turned_ref[pl.ds(block, LANES, stride=8), :] = source[block * LANES : (block + 1) * LANES, :].T
-        out_ref[:, which * 64 : (which + 1) * 64, :] = turned_ref[...].reshape(16, 64, LANES).astype(BF16)
+    columns = fetch(
+        [
+            (weight_ref.at[:, pl.ds(pl.multiple_of((z + steps) % 4 * 2 * LANES, 2 * LANES), 2 * LANES)], columns_ref)
+            for steps, columns_ref in zip((1, 2, 3), columns_refs)
+        ],
+        column_sems,
+    )
+    for copy, (which, start) in zip(copies, places):
+        copy.wait()
+        for block in range(start // LANES, (start + step) // LANES):
+            turned = held_ref[which, block * LANES : (block + 1) * LANES, :].T
+            turned_ref[which, pl.ds(block, LANES, stride=8), :] = turned
+        if start + step == fwd_ref.shape[0]:
+            out_ref[:, which * 64 : (which + 1) * 64, :] = turned_ref[which].reshape(16, 64, LANES).astype(BF16)
+    for copy in columns:
+        copy.wait()
 
 
 def channel_pair(ref, start):
@@ -103,8 +123,11 @@
     return both[:, :8], both[:, 8:]
 
 
-def filter_kernel(filt_ref, forward_ref, mix_ref, twiddle_ref, gain_ref):
+def filter_kernel(index_ref, skip_ref, filt_ref, forward_ref, mix_ref, twiddle_ref, gain_ref, backward_ref):
     n = LANES
+    first_channel = index_ref[0] * 8
+    for half in range(2):
+        backward_ref[:, 2 * n * half : 2 * n * (half + 1)] = forward_ref[:, n * half : n * (half + 1)].astype(F32).T.astype(BF16)
     row = mix_ref[:8, :].astype(F32) + mix_ref[2 * n : 2 * n + 8, :].astype(F32)
     row_real, row_imag = row[1:2, :n], -row[1:2, n:]
     column_real, column_imag = twiddle_ref[0, :, 1:2], -twiddle_ref[1, :, 1:2]
@@ -119,11 +142,11 @@
             forth_rows = slice(i * n, (i + 1) * n)
             back_rows = slice((2 + i) * n, (3 + i) * n)
             back_real, back_imag = spectra[back_rows, :n], -spectra[back_rows, n:]
-            gain_ref[c + i, 0] = spectra[forth_rows, :n] + (back_real * cosine - back_imag * sine)
+            gain_ref[c + i, 0] = spectra[forth_rows, :n] + (back_real * cosine - back_imag * sine) + skip_ref[first_channel + c + i]
             gain_ref[c + i, 1] = spectra[forth_rows, n:] + (back_real * sine + back_imag * cosine)
 
 
-def conv_kernel(sig_ref, gain_ref, forward_ref, mix_ref, twiddle_ref, out_ref):
+def conv_kernel(sig_ref, gain_ref, forward_ref, mix_ref, twiddle_ref, backward_ref, out_ref):
     n = LANES
     extra_high, extra_low = channel_pair(sig_ref, 64)
     extra = extra_high + extra_low
@@ -137,32 +160,26 @@
         lax.broadcasted_iota(jnp.int32, (16, 8, n), 1) == 0, lax.broadcasted_iota(jnp.int32, (16, 8, n), 2) < 2
     )
     cosine, sine = twiddle_ref[0], twiddle_ref[1]
+    sequences = []
     for c in range(0, 8, 2):
-        pair = [
-            jnp.where(at_first, first[:, c + i : c + i + 1, :], part).reshape(n, n).astype(BF16)
-            for i, part in enumerate(channel_pair(sig_ref, 8 * c))
-        ]
-        spectra = transform(pair, forward_ref, mix_ref, twiddle_ref)
-        rows = []
-        for i in range(2):
-            real, imag = spectra[i * n : (i + 1) * n, :n], spectra[i * n : (i + 1) * n, n:]
-            gain_real = gain_ref[c + i, 0] + extra[0, c + i : c + i + 1, 10:11]
-            gain_imag = gain_ref[c + i, 1]
-            rows.append(
-                jnp.concatenate(
-                    [real * gain_real - imag * gain_imag, real * gain_imag + imag * gain_real], axis=1
-                )
-            )
-        parts = right_dot(jnp.concatenate(rows, axis=0), mix_ref, transposed=True)
-        columns = []
-        for i in range(2):
-            real, imag = parts[i * n : (i + 1) * n, :n], parts[i * n : (i + 1) * n, n:]
-            columns.append(
-                jnp.concatenate([real * cosine + imag * sine, imag * cosine - real * sine], axis=0)
-            )
-        times = left_dot(forward_ref, jnp.concatenate(columns, axis=1)) * (1.0 / (n * n))
-        blocks = [times[:, i * n : (i + 1) * n].reshape(16, 8, n) for i in range(2)]
-        out_ref[:, 8 * c : 8 * c + 16, :] = jnp.concatenate(blocks, axis=1).astype(BF16)
+        for i, part in enumerate(channel_pair(sig_ref, 8 * c)):
+            sequences.append(jnp.where(at_first, first[:, c + i : c + i + 1, :], part).reshape(n, n).astype(BF16))
+    spectra = transform(sequences, forward_ref, mix_ref, twiddle_ref)
+    rows = []
+    for c in range(8):
+        real, imag = spectra[c * n : (c + 1) * n, :n], spectra[c * n : (c + 1) * n, n:]
+        gain_real, gain_imag = gain_ref[c, 0], gain_ref[c, 1]
+        rows.append(
+            jnp.concatenate([real * gain_real - imag * gain_imag, -(real * gain_imag + imag * gain_real)], axis=1)
+        )
+    parts = right_dot(jnp.concatenate(rows, axis=0), mix_ref)
+    columns = []
+    for c in range(8):
+        real, imag = parts[c * n : (c + 1) * n, :n], parts[c * n : (c + 1) * n, n:]
+        columns.append(jnp.concatenate([real * cosine - imag * sine, -(real * sine + imag * cosine)], axis=0))
+    times = left_dot(backward_ref, jnp.concatenate(columns, axis=1)) * (1.0 / (n * n))
+    blocks = [times[:, c * n : (c + 1) * n].reshape(16, 8, n) for c in range(8)]
+    out_ref[:, :64, :] = jnp.concatenate(blocks, axis=1).astype(BF16)
 
 
 def piece_block(j, z, core):
@@ -171,7 +188,7 @@
 
 def project_kernel(index_ref, *refs):
     pieces, refs = refs[:8], refs[8:]
-    gain_ref, weight_ref, short_ref, skip_ref, message_ref, gate_ref, projected_ref, stacked_ref, turned_ref = refs
+    gain_ref, weight_ref, short_ref, message_ref, gate_ref, projected_ref, stacked_ref, turned_ref = refs
     rows, width = pieces[0].shape
     z, core = index_ref[0] // 2, index_ref[0] % 2
     gains = []
@@ -182,7 +199,7 @@
         for k in range(3):
             stacked_ref[j * width : (j + 1) * width, k * width : (k + 1) * width] = weight_ref[k, source, :]
     projected_ref[:HALO, :] = jnp.zeros((HALO, 3 * width), F32)
-    step = 256
+    step = 512
     for start in range(0, rows, step):
         parts = [piece[start : start + step, :].astype(F32) for piece in pieces]
         total = sum(part * part for part in parts)
@@ -211,7 +228,7 @@
         last = projected_ref[HALO + rows - 1 : HALO + rows, columns]
         before = projected_ref[HALO + rows - 2 : HALO + rows - 1, columns]
         later.append(jnp.concatenate([taps[1][j] * last + taps[2][j] * before, taps[2][j] * last], axis=0))
-    extra = jnp.concatenate(early + later + [skip_ref[...], jnp.zeros((LANES - 11, width), F32)], axis=0).T
+    extra = jnp.concatenate(early + later + [jnp.zeros((LANES - 10, width), F32)], axis=0).T
     high = extra.astype(BF16).astype(F32)
     message_ref[:, :64, :] = turned_ref[...].reshape(16, 64, LANES).astype(BF16)
     message_ref[:, 64:, :] = jnp.concatenate(
@@ -267,12 +284,16 @@
     return lax.optimization_barrier(values)
 
 
-def call(kernel, shapes, *operands, scalars=0, scratch=(), cost=None):
-    smem = pl.BlockSpec(memory_space=pltpu.SMEM)
+def call(kernel, shapes, *operands, scalars=0, outside=(), scratch=(), cost=None):
+    spaces = [pltpu.SMEM if i < scalars else pltpu.HBM if i in outside else pltpu.VMEM for i in range(len(operands))]
+    operands = [
+        pltpu.with_memory_space_constraint(operand, space) if space is pltpu.HBM else operand
+        for operand, space in zip(operands, spaces)
+    ]
     return pl.pallas_call(
         kernel,
         out_shape=shapes,
-        in_specs=[smem] * scalars + [VMEM] * (len(operands) - scalars),
+        in_specs=[pl.BlockSpec(memory_space=space) for space in spaces],
         out_specs=jax.tree.map(lambda _: VMEM, shapes),
         scratch_shapes=scratch,
         cost_estimate=cost,
@@ -284,11 +305,9 @@
     seq_count = lax.axis_size("seq")
     chan_index = lax.axis_index("chan").reshape(1)
     rows, width = tokens.shape
-    table = {name: jnp.asarray(value) for name, value in tables().items()}
     shape = jax.ShapeDtypeStruct
     turned = pltpu.VMEM((rows, width), F32)
 
-    pieces = [tokens] + [around(tokens, steps) for steps in (1, 2, 3)]
     spread, *columns = call(
         spread_kernel,
         [shape((seq_count, 128, width), BF16)] + [shape((width, 2 * width), BF16)] * 3,
@@ -297,12 +316,25 @@
         filter_bwd,
         out_weight,
         scalars=1,
-        scratch=[turned],
-    )
+        outside=(1, 2, 3),
+        scratch=[pltpu.VMEM((2, rows, width), F32)] * 2
+        + [pltpu.SemaphoreType.DMA((8,)), pltpu.SemaphoreType.DMA((3,))],
+    )
+    pieces = [tokens] + [around(tokens, steps) for steps in (1, 2, 3)]
     pieces = pieces + [across(piece) for piece in pieces]
     filters = lax.all_to_all(spread, "seq", 0, 0)
-    shared = [table[name] for name in ("forward", "mix", "twiddle")]
-    gain = call(filter_kernel, shape((8, 2, LANES, LANES), F32), filters, *shared)
+    forward, mix, twiddle = [jnp.asarray(tables()[name]) for name in ("forward", "mix", "twiddle")]
+    gain, backward = call(
+        filter_kernel,
+        [shape((8, 2, LANES, LANES), F32), shape((LANES, 4 * LANES), BF16)],
+        lax.axis_index("seq").reshape(1),
+        skip_gain,
+        filters,
+        forward,
+        mix,
+        twiddle,
+        scalars=2,
+    )
 
     message, gate = call(
         project_kernel,
@@ -312,7 +344,6 @@
         norm_gain.reshape(-1, width),
         in_weight,
         short_kernel,
-        skip_gain.reshape(1, width),
         scalars=1,
         scratch=[
             pltpu.VMEM((rows + HALO, 3 * width), F32),
@@ -323,11 +354,12 @@
     )
     message, filters = after(message, filters)
     signal = lax.all_to_all(message, "seq", 0, 0)
-    conv = call(conv_kernel, shape((seq_count, 80, width), BF16), signal, gain, *shared)
+    conv = call(
+        conv_kernel, shape((seq_count, 80, width), BF16), signal, gain, forward, mix, twiddle, backward
+    )
+    columns = [around(column, steps) for column, steps in zip(columns, (1, 2, 3))]
     conv, *columns = after(conv, *columns)
     conv = lax.all_to_all(conv, "seq", 0, 0)
-    columns = [around(column, steps) for column, steps in zip(columns, (1, 2, 3))]
-    conv, *columns = after(conv, *columns)
     gated, mine, theirs = call(
         gate_kernel,
         [shape((rows, width), BF16)] + [shape((4 * width, width), BF16)] * 2,

time: 75.8 us -> 73.2 us (0.966)
  blocking collectives: 0 us -> 11.8 us
  waiting for transfers between devices: 14.7 us -> 7.19 us
  starting transfers between devices: 45.5 us -> 41.5 us
  local copies, waits for them, and re-layouts: 3.71 us -> 0.68 us
    all_to_all x0 -> x1, blocking collectives: none -> 11.8 us  [local(): conv = lax.all_to_all(conv, 'seq', 0, 0)]
    all_to_all x1 -> x0, starting transfers between devices: 4.16 us -> none  [local(): conv = lax.all_to_all(conv, 'seq', 0, 0)]
    all_to_all x1, waiting for transfers between devices: 6.3 us -> 2.5 us  [local(): signal = lax.all_to_all(message, 'seq', 0, 0)]
    unnamed x24 -> x18, local copies, waits for them, and re-layouts: 3.71 us -> 0.68 us
    all_to_all x1 -> x0, waiting for transfers between devices: 1.76 us -> none  [local(): conv = lax.all_to_all(conv, 'seq', 0, 0)]
    ppermute x9, waiting for transfers between devices: 3.36 us -> 2.17 us  [around(): lax.ppermute(value, 'chan', [(i, (i + 2 * steps) % count) for i in range(...]
    all_to_all x1, starting transfers between devices: 6.13 us -> 6.91 us  [local(): signal = lax.all_to_all(message, 'seq', 0, 0)]
    all_to_all x1, waiting for transfers between devices: 0.77 us -> 0.01 us  [local(): filters = lax.all_to_all(spread, 'seq', 0, 0)]
  transfers between devices with their start and end apart: 21 -> 20, of which waited for: 9 -> 4; matrix products, arithmetic and copies ran while one was open for 0% -> 0% of each run, Pallas kernels for 7% -> 13%
where the time goes in v4:
time: 73.2 us; the launch traced here: 72.8 us
  starting transfers between devices  41.5 us (57%)
  blocking collectives  11.8 us (16%)
  Pallas kernels  11.4 us (16%)
  waiting for transfers between devices  7.19 us (10%)
    ppermute x9, starting transfers between devices, across(): lax.ppermute(value, 'chan', [(i, i ^ 1) for i in range(lax.axis_size('cha...  16.5 us
    all_to_all x1, blocking collectives, local(): conv = lax.all_to_all(conv, 'seq', 0, 0)  11.8 us
    pallas_call x6, Pallas kernels, call(): pl.pallas_call(kernel, out_shape=shapes, in_specs=[pl.BlockSpec(memory_sp...  11.4 us
    ppermute x9, starting transfers between devices, around(): lax.ppermute(value, 'chan', [(i, (i + 2 * steps) % count) for i in range(...  11.2 us
    all_to_all x1, starting transfers between devices, local(): signal = lax.all_to_all(message, 'seq', 0, 0)  6.91 us
    all_to_all x1, starting transfers between devices, local(): filters = lax.all_to_all(spread, 'seq', 0, 0)  6.9 us
    ppermute x9, waiting for transfers between devices, across(): lax.ppermute(value, 'chan', [(i, i ^ 1) for i in range(lax.axis_size('cha...  2.51 us
    all_to_all x1, waiting for transfers between devices, local(): signal = lax.all_to_all(message, 'seq', 0, 0)  2.5 us
  transfers between devices with their start and end apart: 20, of which 4 were waited for; matrix products, arithmetic and copies ran while one was open for 0% of the time, Pallas kernels for 13%

profile of v4, /device:TPU:1, one launch (start us, length us, event | category | flops | bytes accessed | tf_op | source)
XLA Modules:
  0.0 72.8 jit_solution(3760648591518189742)
XLA Ops:
  0.0 4.6 %collective-permute-start.2 = (bf16[1024,128]{1,0:T(8,128)(2,1)}, bf16[1024,128]{1,0:T(8,128)(2,1)S(1)}, u32[]{:S(2)}, u32[]{:S(2)}) collective-permute-start(bf16[1024,128]{1,0:T(8,128)(2,1)} %refs_10_.3), channel_id=1, source_target_pairs={{0,6},{1,7},{2,0},{3,1},{4,2},{5,3},{6,4},{7,5},{8,14},{9,15},{10,... | collective-permute-start | bytes 786440 | tf_op jit(solution)/shard_map/ppermute | solution.py:271
  4.6 0.7 collective-permute-start
  5.3 2.7 %shard_map.110 = (bf16[16,128,128]{2,1,0:T(8,128)(2,1)}, bf16[128,256]{1,0:T(8,128)(2,1)}, bf16[128,256]{1,0:T(8,128)(2,1)}, bf16[128,256]{1,0:T(8,128)(2,1)}) custom-call(s32[1]{0:T(128)} %bitcast.index_ref, f32[1024,128]{1,0:T(8,128)} %fwd_ref.1, f32[1024,128]{1,0:T(8,128)} %bwd_ref.1, bf16[128,1024]{1,0:T(8,128)(2,1)} %weight_ref.3), custom_call_target="tpu_custom_call" | custom-call | tf_op jit(solution)/shard_map/pallas_call | solution.py:293
  8.0 0.0 copy-start.6
  8.1 6.9 %all-to-all-start = ((bf16[16,128,128]{2,1,0:T(8,128)(2,1)}), bf16[16,128,128]{2,1,0:T(8,128)(2,1)S(1)}, u32[]{:S(2)}, u32[]{:S(2)}) async-start(bf16[16,128,128]{2,1,0:T(8,128)(2,1)} %get-tuple-element.22), calls=%async_computation | async-start | bytes 1048576 | tf_op jit(solution)/shard_map/all_to_all | solution.py:325
  15.0 1.9 %collective-permute-start.3 = (bf16[1024,128]{1,0:T(8,128)(2,1)S(1)}, bf16[1024,128]{1,0:T(8,128)(2,1)S(1)}, u32[]{:S(2)}, u32[]{:S(2)}) collective-permute-start(bf16[1024,128]{1,0:T(8,128)(2,1)S(1)} %copy-done.4), channel_id=1, source_target_pairs={{0,1},{1,0},{2,3},{3,2},{4,5},{5,4},{6,7},{7,6},{8,9},{9,8},{10,11... | collective-permute-start | bytes 786440 | tf_op jit(solution)/shard_map/ppermute | solution.py:275
  16.9 0.2 collective-permute-start.6
  17.0 0.3 collective-permute-start.5
  17.4 2.1 %collective-permute-done.refs_1_ = bf16[1024,128]{1,0:T(8,128)(2,1)S(1)} collective-permute-done((bf16[1024,128]{1,0:T(8,128)(2,1)}, bf16[1024,128]{1,0:T(8,128)(2,1)S(1)}, u32[]{:S(2)}, u32[]{:S(2)}) %collective-permute-start) | collective-permute-done | bytes 262176 | tf_op jit(solution)/shard_map/ppermute | solution.py:271
  19.5 0.8 %collective-permute-start.4 = (bf16[1024,128]{1,0:T(8,128)(2,1)S(1)}, bf16[1024,128]{1,0:T(8,128)(2,1)S(1)}, u32[]{:S(2)}, u32[]{:S(2)}) collective-permute-start(bf16[1024,128]{1,0:T(8,128)(2,1)S(1)} %collective-permute-done.refs_1_), channel_id=1, source_target_pairs={{0,1},{1,0},{2,3},{3,2},{4,5},{5,4},{6,7},{7,6},{8,9},{9,8},{10,11... | collective-permute-start | bytes 786440 | tf_op jit(solution)/shard_map/ppermute | solution.py:275
  20.4 1.1 %collective-permute-done.4.refs_5_ = bf16[1024,128]{1,0:T(8,128)(2,1)S(1)} collective-permute-done((bf16[1024,128]{1,0:T(8,128)(2,1)S(1)}, bf16[1024,128]{1,0:T(8,128)(2,1)S(1)}, u32[]{:S(2)}, u32[]{:S(2)}) %collective-permute-start.4) | collective-permute-done | bytes 262176 | tf_op jit(solution)/shard_map/ppermute | solution.py:275
  21.5 2.7 %shard_map.109 = (bf16[16,80,128]{2,1,0:T(8,128)(2,1)}, f32[1024,128]{1,0:T(8,128)S(1)}) custom-call(s32[1]{0:T(128)} %bitcast.index_ref, bf16[1024,128]{1,0:T(8,128)(2,1)S(1)} %copy-done.4, bf16[1024,128]{1,0:T(8,128)(2,1)S(1)} %collective-permute-done.refs_1_, bf16[1024,128]{1,0:T(8,128)(2,1)S(1)} %collective-permute-done.1.refs_2_, ...), custom_call_target="tpu_custom_call" | custom-call | flops 1500000000 | bytes 1 | tf_op jit(solution)/shard_map/pallas_call | solution.py:293
  24.2 6.9 %all-to-all-start.1 = ((bf16[16,80,128]{2,1,0:T(8,128)(2,1)}), bf16[16,80,128]{2,1,0:T(8,128)(2,1)S(1)}, u32[]{:S(2)}, u32[]{:S(2)}) async-start(bf16[16,80,128]{2,1,0:T(8,128)(2,1)} %get-tuple-element.23), calls=%async_computation.1 | async-start | bytes 655360 | tf_op jit(solution)/shard_map/all_to_all | solution.py:356
  31.1 0.1 collective-permute-start.7
  31.2 1.9 %collective-permute-start.8 = (bf16[128,256]{1,0:T(8,128)(2,1)}, bf16[128,256]{1,0:T(8,128)(2,1)S(1)}, u32[]{:S(2)}, u32[]{:S(2)}) collective-permute-start(bf16[128,256]{1,0:T(8,128)(2,1)} %get-tuple-element.27), channel_id=1, source_target_pairs={{0,4},{1,5},{2,6},{3,7},{4,0},{5,1},{6,2},{7,3},{8,12},{9,13},{10,... | collective-permute-start | bytes 196616 | tf_op jit(solution)/shard_map/ppermute | solution.py:271
  33.1 0.8 %collective-permute-start.9 = (bf16[128,256]{1,0:T(8,128)(2,1)}, bf16[128,256]{1,0:T(8,128)(2,1)S(1)}, u32[]{:S(2)}, u32[]{:S(2)}) collective-permute-start(bf16[128,256]{1,0:T(8,128)(2,1)} %get-tuple-element.28), channel_id=1, source_target_pairs={{0,6},{1,7},{2,0},{3,1},{4,2},{5,3},{6,4},{7,5},{8,14},{9,15},{10,... | collective-permute-start | bytes 196616 | tf_op jit(solution)/shard_map/ppermute | solution.py:271
  33.9 0.6 copy-done.5
  34.5 2.0 %shard_map.111 = (f32[8,2,128,128]{3,2,1,0:T(8,128)S(1)}, bf16[128,512]{1,0:T(8,128)(2,1)S(1)}) custom-call(s32[1]{0:T(128)} %bitcast.2.index_ref, f32[128]{0:T(128)S(1)} %copy-done.5, bf16[16,128,128]{2,1,0:T(8,128)(2,1)S(1)} %all-to-all-done.filt_ref, bf16[256,256]{1,0:T(8,128)(2,1)S(1)} %copy-done.3, bf16[512,256]{1,0:T(8,128)(2,1)S(1)} %copy-done.1, ...), custom_call_target="tpu_custom_call" | custom-call | tf_op jit(solution)/shard_map/pallas_call | solution.py:293
  36.5 2.5 %all-to-all-done.1.sig_ref = bf16[16,80,128]{2,1,0:T(8,128)(2,1)S(1)} async-done(((bf16[16,80,128]{2,1,0:T(8,128)(2,1)}), bf16[16,80,128]{2,1,0:T(8,128)(2,1)S(1)}, u32[]{:S(2)}, u32[]{:S(2)}) %all-to-all-start.1) | async-done | bytes 327712 | tf_op jit(solution)/shard_map/all_to_all | solution.py:356
  39.1 2.3 %shard_map.112 = bf16[16,80,128]{2,1,0:T(8,128)(2,1)S(1)} custom-call(bf16[16,80,128]{2,1,0:T(8,128)(2,1)S(1)} %all-to-all-done.1.sig_ref, f32[8,2,128,128]{3,2,1,0:T(8,128)S(1)} %get-tuple-element.24.gain_ref, bf16[256,256]{1,0:T(8,128)(2,1)S(1)} %copy-done.3, bf16[512,256]{1,0:T(8,128)(2,1)S(1)} %copy-done.1, f32[2,128,128]{2,1,0:T(8,128)S(1)} %copy-done.2, ...), custom_call_target="tpu_custom_call" | custom-call | tf_op jit(solution)/shard_map/pallas_call | solution.py:293
  41.3 0.0 copy-start
  41.4 11.8 %all_to_all.15.conv_ref = bf16[16,80,128]{2,1,0:T(8,128)(2,1)S(1)} all-to-all(bf16[16,80,128]{2,1,0:T(8,128)(2,1)S(1)} %shard_map.112), channel_id=1, replica_groups=mesh['seq'=16,'chan'=8] {'seq'}, dimensions={0} | all-to-all | bytes 655360 | tf_op jit(solution)/shard_map/all_to_all | solution.py:362
  53.2 0.3 shard_map.113
  53.4 0.7 collective-permute-start.12
  54.1 1.9 %collective-permute-start.11 = (bf16[1024,128]{1,0:T(8,128)(2,1)S(1)}, bf16[1024,128]{1,0:T(8,128)(2,1)S(1)}, u32[]{:S(2)}, u32[]{:S(2)}) collective-permute-start(bf16[1024,128]{1,0:T(8,128)(2,1)S(1)} %get-tuple-element.34.refs_0_), channel_id=1, source_target_pairs={{0,4},{1,5},{2,6},{3,7},{4,0},{5,1},{6,2},{7,3},{8,12},{9,13},{10,... | collective-permute-start | bytes 786440 | tf_op jit(solution)/shard_map/ppermute | solution.py:271
  56.0 0.6 collective-permute-start.10
  56.6 4.0 %collective-permute-start.13 = (bf16[1024,128]{1,0:T(8,128)(2,1)S(1)}, bf16[1024,128]{1,0:T(8,128)(2,1)S(1)}, u32[]{:S(2)}, u32[]{:S(2)}) collective-permute-start(bf16[1024,128]{1,0:T(8,128)(2,1)S(1)} %get-tuple-element.34.refs_0_), channel_id=1, source_target_pairs={{0,1},{1,0},{2,3},{3,2},{4,5},{5,4},{6,7},{7,6},{8,9},{9,8},{10,11... | collective-permute-start | bytes 786440 | tf_op jit(solution)/shard_map/ppermute | solution.py:275
  60.7 4.4 %collective-permute-start.16 = (bf16[1024,128]{1,0:T(8,128)(2,1)S(1)}, bf16[1024,128]{1,0:T(8,128)(2,1)S(1)}, u32[]{:S(2)}, u32[]{:S(2)}) collective-permute-start(bf16[1024,128]{1,0:T(8,128)(2,1)S(1)} %collective-permute-done.12.refs_3_), channel_id=1, source_target_pairs={{0,1},{1,0},{2,3},{3,2},{4,5},{5,4},{6,7},{7,6},{8,9},{9,8},{10,11... | collective-permute-start | bytes 786440 | tf_op jit(solution)/shard_map/ppermute | solution.py:275
  65.0 2.2 %collective-permute-start.15 = (bf16[1024,128]{1,0:T(8,128)(2,1)S(1)}, bf16[1024,128]{1,0:T(8,128)(2,1)S(1)}, u32[]{:S(2)}, u32[]{:S(2)}) collective-permute-start(bf16[1024,128]{1,0:T(8,128)(2,1)S(1)} %collective-permute-done.11.refs_2_), channel_id=1, source_target_pairs={{0,1},{1,0},{2,3},{3,2},{4,5},{5,4},{6,7},{7,6},{8,9},{9,8},{10,11... | collective-permute-start | bytes 786440 | tf_op jit(solution)/shard_map/ppermute | solution.py:275
  67.2 2.7 %collective-permute-start.14 = (bf16[1024,128]{1,0:T(8,128)(2,1)S(1)}, bf16[1024,128]{1,0:T(8,128)(2,1)S(1)}, u32[]{:S(2)}, u32[]{:S(2)}) collective-permute-start(bf16[1024,128]{1,0:T(8,128)(2,1)S(1)} %collective-permute-done.10.refs_1_), channel_id=1, source_target_pairs={{0,1},{1,0},{2,3},{3,2},{4,5},{5,4},{6,7},{7,6},{8,9},{9,8},{10,11... | collective-permute-start | bytes 786440 | tf_op jit(solution)/shard_map/ppermute | solution.py:275
  69.9 1.3 %collective-permute-done.17.refs_9_ = bf16[512,128]{1,0:T(8,128)(2,1)S(1)} collective-permute-done((bf16[512,128]{1,0:T(8,128)(2,1)S(1)}, bf16[512,128]{1,0:T(8,128)(2,1)S(1)}, u32[]{:S(2)}, u32[]{:S(2)}) %collective-permute-start.17) | collective-permute-done | bytes 131104 | tf_op jit(solution)/shard_map/ppermute | solution.py:275
  71.3 1.5 %shard_map.114 = f32[1024,128]{1,0:T(8,128)} custom-call(bf16[1024,128]{1,0:T(8,128)(2,1)S(1)} %get-tuple-element.34.refs_0_, bf16[1024,128]{1,0:T(8,128)(2,1)S(1)} %collective-permute-done.10.refs_1_, bf16[1024,128]{1,0:T(8,128)(2,1)S(1)} %collective-permute-done.11.refs_2_, bf16[1024,128]{1,0:T(8,128)(2,1)S(1)} %collective-permute-done.12.refs_3_, ...), custom_call_target="tpu_custom_call" | custom-call | tf_op jit(solution)/shard_map/pallas_call | solution.py:293
  (33 shorter events, 0.1 us)
Async XLA Ops:
  0.0 16.9 %collective-permute-start.2 = (bf16[1024,128]{1,0:T(8,128)(2,1)}, bf16[1024,128]{1,0:T(8,128)(2,1)S(1)}, u32[]{:S(2)}, u32[]{:S(2)}) collective-permute-start(bf16[1024,128]{1,0:T(8,128)(2,1)} %refs_10_.3), channel_id=1, source_target_pairs={{0,6},{1,7},{2,0},{3,1},{4,2},{5,3},{6,4},{7,5},{8,14},{9,15},{10,... | collective-permute-start | bytes 786440 | tf_op jit(solution)/shard_map/ppermute | solution.py:271
  4.6 12.5 %collective-permute-start.1 = (bf16[1024,128]{1,0:T(8,128)(2,1)}, bf16[1024,128]{1,0:T(8,128)(2,1)S(1)}, u32[]{:S(2)}, u32[]{:S(2)}) collective-permute-start(bf16[1024,128]{1,0:T(8,128)(2,1)} %refs_10_.3), channel_id=1, source_target_pairs={{0,4},{1,5},{2,6},{3,7},{4,0},{5,1},{6,2},{7,3},{8,12},{9,13},{10,... | collective-permute-start | bytes 786440 | tf_op jit(solution)/shard_map/ppermute | solution.py:271
  4.6 14.9 %collective-permute-start = (bf16[1024,128]{1,0:T(8,128)(2,1)}, bf16[1024,128]{1,0:T(8,128)(2,1)S(1)}, u32[]{:S(2)}, u32[]{:S(2)}) collective-permute-start(bf16[1024,128]{1,0:T(8,128)(2,1)} %refs_10_.3), channel_id=1, source_target_pairs={{0,2},{1,3},{2,4},{3,5},{4,6},{5,7},{6,0},{7,1},{8,10},{9,11},{10,... | collective-permute-start | bytes 786440 | tf_op jit(solution)/shard_map/ppermute | solution.py:271
  5.3 16.2 %copy-start.7 = (f32[3,3,128]{2,1,0:T(4,128)S(1)}, f32[3,3,128]{2,1,0:T(4,128)}, u32[]{:S(2)}) copy-start(f32[3,3,128]{2,1,0:T(4,128)} %refs_10_.2) | copy-start | bytes 13828
  5.3 16.2 %copy-start.8 = (f32[1024]{0:T(1024)S(1)}, f32[1024]{0:T(1024)}, u32[]{:S(2)}) copy-start(f32[1024]{0:T(1024)} %param.12) | copy-start | bytes 12292
  8.0 13.5 %copy-start.6 = (bf16[3,1024,128]{2,1,0:T(8,128)(2,1)S(1)}, bf16[3,1024,128]{2,1,0:T(8,128)(2,1)}, u32[]{:S(2)}) copy-start(bf16[3,1024,128]{2,1,0:T(8,128)(2,1)} %refs_9_.1) | copy-start | bytes 2359300
  8.0 6.9 %copy-start.4 = (bf16[1024,128]{1,0:T(8,128)(2,1)S(1)}, bf16[1024,128]{1,0:T(8,128)(2,1)}, u32[]{:S(2)}) copy-start(bf16[1024,128]{1,0:T(8,128)(2,1)} %refs_10_.3) | copy-start | bytes 786436
  8.1 16.1 %all-to-all-start = ((bf16[16,128,128]{2,1,0:T(8,128)(2,1)}), bf16[16,128,128]{2,1,0:T(8,128)(2,1)S(1)}, u32[]{:S(2)}, u32[]{:S(2)}) async-start(bf16[16,128,128]{2,1,0:T(8,128)(2,1)} %get-tuple-element.22), calls=%async_computation | async-start | bytes 1048576 | tf_op jit(solution)/shard_map/all_to_all | solution.py:325
  15.0 5.4 %collective-permute-start.3 = (bf16[1024,128]{1,0:T(8,128)(2,1)S(1)}, bf16[1024,128]{1,0:T(8,128)(2,1)S(1)}, u32[]{:S(2)}, u32[]{:S(2)}) collective-permute-start(bf16[1024,128]{1,0:T(8,128)(2,1)S(1)} %copy-done.4), channel_id=1, source_target_pairs={{0,1},{1,0},{2,3},{3,2},{4,5},{5,4},{6,7},{7,6},{8,9},{9,8},{10,11... | collective-permute-start | bytes 786440 | tf_op jit(solution)/shard_map/ppermute | solution.py:275
  16.9 3.5 %collective-permute-start.6 = (bf16[1024,128]{1,0:T(8,128)(2,1)S(1)}, bf16[1024,128]{1,0:T(8,128)(2,1)S(1)}, u32[]{:S(2)}, u32[]{:S(2)}) collective-permute-start(bf16[1024,128]{1,0:T(8,128)(2,1)S(1)} %collective-permute-done.2.refs_3_), channel_id=1, source_target_pairs={{0,1},{1,0},{2,3},{3,2},{4,5},{5,4},{6,7},{7,6},{8,9},{9,8},{10,11... | collective-permute-start | bytes 786440 | tf_op jit(solution)/shard_map/ppermute | solution.py:275
  17.0 3.3 %collective-permute-start.5 = (bf16[1024,128]{1,0:T(8,128)(2,1)S(1)}, bf16[1024,128]{1,0:T(8,128)(2,1)S(1)}, u32[]{:S(2)}, u32[]{:S(2)}) collective-permute-start(bf16[1024,128]{1,0:T(8,128)(2,1)S(1)} %collective-permute-done.1.refs_2_), channel_id=1, source_target_pairs={{0,1},{1,0},{2,3},{3,2},{4,5},{5,4},{6,7},{7,6},{8,9},{9,8},{10,11... | collective-permute-start | bytes 786440 | tf_op jit(solution)/shard_map/ppermute | solution.py:275
  19.5 2.0 %collective-permute-start.4 = (bf16[1024,128]{1,0:T(8,128)(2,1)S(1)}, bf16[1024,128]{1,0:T(8,128)(2,1)S(1)}, u32[]{:S(2)}, u32[]{:S(2)}) collective-permute-start(bf16[1024,128]{1,0:T(8,128)(2,1)S(1)} %collective-permute-done.refs_1_), channel_id=1, source_target_pairs={{0,1},{1,0},{2,3},{3,2},{4,5},{5,4},{6,7},{7,6},{8,9},{9,8},{10,11... | collective-permute-start | bytes 786440 | tf_op jit(solution)/shard_map/ppermute | solution.py:275
  24.2 9.7 %copy-start.1 = (bf16[512,256]{1,0:T(8,128)(2,1)S(1)}, bf16[512,256]{1,0:T(8,128)(2,1)}, u32[]{:S(2)}) copy-start(bf16[512,256]{1,0:T(8,128)(2,1)} %constant.16.clone.mix_ref) | copy-start | bytes 786436
  24.2 9.7 %copy-start.2 = (f32[2,128,128]{2,1,0:T(8,128)S(1)}, f32[2,128,128]{2,1,0:T(8,128)}, u32[]{:S(2)}) copy-start(f32[2,128,128]{2,1,0:T(8,128)} %constant.17.clone.twiddle_ref) | copy-start | bytes 393220
  24.2 9.7 %copy-start.3 = (bf16[256,256]{1,0:T(8,128)(2,1)S(1)}, bf16[256,256]{1,0:T(8,128)(2,1)}, u32[]{:S(2)}) copy-start(bf16[256,256]{1,0:T(8,128)(2,1)} %constant.15.clone.forward_ref) | copy-start | bytes 393220
  24.2 14.9 %all-to-all-start.1 = ((bf16[16,80,128]{2,1,0:T(8,128)(2,1)}), bf16[16,80,128]{2,1,0:T(8,128)(2,1)S(1)}, u32[]{:S(2)}, u32[]{:S(2)}) async-start(bf16[16,80,128]{2,1,0:T(8,128)(2,1)} %get-tuple-element.23), calls=%async_computation.1 | async-start | bytes 655360 | tf_op jit(solution)/shard_map/all_to_all | solution.py:356
  31.1 10.2 %collective-permute-start.7 = (bf16[128,256]{1,0:T(8,128)(2,1)}, bf16[128,256]{1,0:T(8,128)(2,1)S(1)}, u32[]{:S(2)}, u32[]{:S(2)}) collective-permute-start(bf16[128,256]{1,0:T(8,128)(2,1)} %get-tuple-element.26), channel_id=1, source_target_pairs={{0,2},{1,3},{2,4},{3,5},{4,6},{5,7},{6,0},{7,1},{8,10},{9,11},{10,... | collective-permute-start | bytes 196616 | tf_op jit(solution)/shard_map/ppermute | solution.py:271
  31.2 10.1 %collective-permute-start.8 = (bf16[128,256]{1,0:T(8,128)(2,1)}, bf16[128,256]{1,0:T(8,128)(2,1)S(1)}, u32[]{:S(2)}, u32[]{:S(2)}) collective-permute-start(bf16[128,256]{1,0:T(8,128)(2,1)} %get-tuple-element.27), channel_id=1, source_target_pairs={{0,4},{1,5},{2,6},{3,7},{4,0},{5,1},{6,2},{7,3},{8,12},{9,13},{10,... | collective-permute-start | bytes 196616 | tf_op jit(solution)/shard_map/ppermute | solution.py:271
  33.1 8.2 %collective-permute-start.9 = (bf16[128,256]{1,0:T(8,128)(2,1)}, bf16[128,256]{1,0:T(8,128)(2,1)S(1)}, u32[]{:S(2)}, u32[]{:S(2)}) collective-permute-start(bf16[128,256]{1,0:T(8,128)(2,1)} %get-tuple-element.28), channel_id=1, source_target_pairs={{0,6},{1,7},{2,0},{3,1},{4,2},{5,3},{6,4},{7,5},{8,14},{9,15},{10,... | collective-permute-start | bytes 196616 | tf_op jit(solution)/shard_map/ppermute | solution.py:271
  33.9 0.7 copy-start.5
  41.3 11.8 %copy-start = (bf16[128,1024]{1,0:T(8,128)(2,1)S(1)}, bf16[128,1024]{1,0:T(8,128)(2,1)}, u32[]{:S(2)}) copy-start(bf16[128,1024]{1,0:T(8,128)(2,1)} %weight_ref.3) | copy-start | bytes 786436
  53.4 7.2 %collective-permute-start.12 = (bf16[1024,128]{1,0:T(8,128)(2,1)S(1)}, bf16[1024,128]{1,0:T(8,128)(2,1)S(1)}, u32[]{:S(2)}, u32[]{:S(2)}) collective-permute-start(bf16[1024,128]{1,0:T(8,128)(2,1)S(1)} %get-tuple-element.34.refs_0_), channel_id=1, source_target_pairs={{0,6},{1,7},{2,0},{3,1},{4,2},{5,3},{6,4},{7,5},{8,14},{9,15},{10,... | collective-permute-start | bytes 786440 | tf_op jit(solution)/shard_map/ppermute | solution.py:271
  54.1 10.9 %collective-permute-start.11 = (bf16[1024,128]{1,0:T(8,128)(2,1)S(1)}, bf16[1024,128]{1,0:T(8,128)(2,1)S(1)}, u32[]{:S(2)}, u32[]{:S(2)}) collective-permute-start(bf16[1024,128]{1,0:T(8,128)(2,1)S(1)} %get-tuple-element.34.refs_0_), channel_id=1, source_target_pairs={{0,4},{1,5},{2,6},{3,7},{4,0},{5,1},{6,2},{7,3},{8,12},{9,13},{10,... | collective-permute-start | bytes 786440 | tf_op jit(solution)/shard_map/ppermute | solution.py:271
  56.0 11.3 %collective-permute-start.10 = (bf16[1024,128]{1,0:T(8,128)(2,1)S(1)}, bf16[1024,128]{1,0:T(8,128)(2,1)S(1)}, u32[]{:S(2)}, u32[]{:S(2)}) collective-permute-start(bf16[1024,128]{1,0:T(8,128)(2,1)S(1)} %get-tuple-element.34.refs_0_), channel_id=1, source_target_pairs={{0,2},{1,3},{2,4},{3,5},{4,6},{5,7},{6,0},{7,1},{8,10},{9,11},{10,... | collective-permute-start | bytes 786440 | tf_op jit(solution)/shard_map/ppermute | solution.py:271
  56.6 14.7 %collective-permute-start.13 = (bf16[1024,128]{1,0:T(8,128)(2,1)S(1)}, bf16[1024,128]{1,0:T(8,128)(2,1)S(1)}, u32[]{:S(2)}, u32[]{:S(2)}) collective-permute-start(bf16[1024,128]{1,0:T(8,128)(2,1)S(1)} %get-tuple-element.34.refs_0_), channel_id=1, source_target_pairs={{0,1},{1,0},{2,3},{3,2},{4,5},{5,4},{6,7},{7,6},{8,9},{9,8},{10,11... | collective-permute-start | bytes 786440 | tf_op jit(solution)/shard_map/ppermute | solution.py:275
  60.7 10.6 %collective-permute-start.16 = (bf16[1024,128]{1,0:T(8,128)(2,1)S(1)}, bf16[1024,128]{1,0:T(8,128)(2,1)S(1)}, u32[]{:S(2)}, u32[]{:S(2)}) collective-permute-start(bf16[1024,128]{1,0:T(8,128)(2,1)S(1)} %collective-permute-done.12.refs_3_), channel_id=1, source_target_pairs={{0,1},{1,0},{2,3},{3,2},{4,5},{5,4},{6,7},{7,6},{8,9},{9,8},{10,11... | collective-permute-start | bytes 786440 | tf_op jit(solution)/shard_map/ppermute | solution.py:275
  65.0 6.3 %collective-permute-start.15 = (bf16[1024,128]{1,0:T(8,128)(2,1)S(1)}, bf16[1024,128]{1,0:T(8,128)(2,1)S(1)}, u32[]{:S(2)}, u32[]{:S(2)}) collective-permute-start(bf16[1024,128]{1,0:T(8,128)(2,1)S(1)} %collective-permute-done.11.refs_2_), channel_id=1, source_target_pairs={{0,1},{1,0},{2,3},{3,2},{4,5},{5,4},{6,7},{7,6},{8,9},{9,8},{10,11... | collective-permute-start | bytes 786440 | tf_op jit(solution)/shard_map/ppermute | solution.py:275
  67.2 4.1 %collective-permute-start.14 = (bf16[1024,128]{1,0:T(8,128)(2,1)S(1)}, bf16[1024,128]{1,0:T(8,128)(2,1)S(1)}, u32[]{:S(2)}, u32[]{:S(2)}) collective-permute-start(bf16[1024,128]{1,0:T(8,128)(2,1)S(1)} %collective-permute-done.10.refs_1_), channel_id=1, source_target_pairs={{0,1},{1,0},{2,3},{3,2},{4,5},{5,4},{6,7},{7,6},{8,9},{9,8},{10,11... | collective-permute-start | bytes 786440 | tf_op jit(solution)/shard_map/ppermute | solution.py:275
  69.9 1.3 %collective-permute-start.17 = (bf16[512,128]{1,0:T(8,128)(2,1)S(1)}, bf16[512,128]{1,0:T(8,128)(2,1)S(1)}, u32[]{:S(2)}, u32[]{:S(2)}) collective-permute-start(bf16[512,128]{1,0:T(8,128)(2,1)S(1)} %get-tuple-element.36), channel_id=1, source_target_pairs={{0,1},{1,0},{2,3},{3,2},{4,5},{5,4},{6,7},{7,6},{8,9},{9,8},{10,11... | collective-permute-start | bytes 393224 | tf_op jit(solution)/shard_map/ppermute | solution.py:275

commit v5 on v4

--- a/solution.py
+++ b/solution.py
@@ -113,13 +113,21 @@
             turned = held_ref[which, block * LANES : (block + 1) * LANES, :].T
             turned_ref[which, pl.ds(block, LANES, stride=8), :] = turned
         if start + step == fwd_ref.shape[0]:
-            out_ref[:, which * 64 : (which + 1) * 64, :] = turned_ref[which].reshape(16, 64, LANES).astype(BF16)
+            out_ref[:, which * 64 : (which + 1) * 64, :] = turned_round(turned_ref[which].reshape(16, 64, LANES)).astype(BF16)
     for copy in columns:
         copy.wait()
 
 
+def turned_round(value):
+    return jnp.concatenate([value[15 - j : 16 - j] for j in range(16)], axis=0)
+
+
+def exchange(value):
+    return lax.all_to_all(value, "seq", 0, 0, axis_index_groups=[list(range(15, -1, -1))])
+
+
 def channel_pair(ref, start):
-    both = ref[:, start : start + 16, :].astype(F32)
+    both = turned_round(ref[:, start : start + 16, :].astype(F32))
     return both[:, :8], both[:, 8:]
 
 
@@ -152,7 +160,7 @@
     extra = extra_high + extra_low
     before = jnp.concatenate([jnp.zeros((1, 8, n), F32), extra[:-1]], axis=0)
     high = before.astype(BF16).astype(F32)
-    out_ref[:, 64:, :] = jnp.concatenate([high, before - high], axis=1).astype(BF16)
+    out_ref[:, 64:, :] = turned_round(jnp.concatenate([high, before - high], axis=1)).astype(BF16)
     before = before.reshape(n, n)
     mixes = extra.reshape(n, n) + pltpu.roll(before, n - 4, 1)
     first = (mixes * pltpu.roll(mixes, n - 2, 1)).reshape(16, 8, n)
@@ -179,7 +187,7 @@
         columns.append(jnp.concatenate([real * cosine - imag * sine, -(real * sine + imag * cosine)], axis=0))
     times = left_dot(backward_ref, jnp.concatenate(columns, axis=1)) * (1.0 / (n * n))
     blocks = [times[:, c * n : (c + 1) * n].reshape(16, 8, n) for c in range(8)]
-    out_ref[:, :64, :] = jnp.concatenate(blocks, axis=1).astype(BF16)
+    out_ref[:, :64, :] = turned_round(jnp.concatenate(blocks, axis=1)).astype(BF16)
 
 
 def piece_block(j, z, core):
@@ -230,9 +238,9 @@
         later.append(jnp.concatenate([taps[1][j] * last + taps[2][j] * before, taps[2][j] * last], axis=0))
     extra = jnp.concatenate(early + later + [jnp.zeros((LANES - 10, width), F32)], axis=0).T
     high = extra.astype(BF16).astype(F32)
-    message_ref[:, :64, :] = turned_ref[...].reshape(16, 64, LANES).astype(BF16)
-    message_ref[:, 64:, :] = jnp.concatenate(
-        [high.reshape(16, 8, LANES), (extra - high).reshape(16, 8, LANES)], axis=1
+    message_ref[:, :64, :] = turned_round(turned_ref[...].reshape(16, 64, LANES)).astype(BF16)
+    message_ref[:, 64:, :] = turned_round(
+        jnp.concatenate([high.reshape(16, 8, LANES), (extra - high).reshape(16, 8, LANES)], axis=1)
     ).astype(BF16)
 
 
@@ -244,7 +252,7 @@
             start = c * LANES if k else (2 * z + c) * LANES
             source = columns_refs[k - 1] if k else weight_ref
             ref[k * LANES : (k + 1) * LANES, :] = source[:, pl.ds(pl.multiple_of(start, LANES), LANES)]
-    turned_ref[...] = conv_ref[:, :64, :].astype(F32).reshape(turned_ref.shape)
+    turned_ref[...] = turned_round(conv_ref[:, :64, :].astype(F32)).reshape(turned_ref.shape)
     extra_high, extra_low = channel_pair(conv_ref, 64)
     late = (extra_high + extra_low).reshape(LANES, LANES).T[8:10]
     for block in range(gate_ref.shape[0] // LANES):
@@ -322,7 +330,7 @@
     )
     pieces = [tokens] + [around(tokens, steps) for steps in (1, 2, 3)]
     pieces = pieces + [across(piece) for piece in pieces]
-    filters = lax.all_to_all(spread, "seq", 0, 0)
+    filters = exchange(spread)
     forward, mix, twiddle = [jnp.asarray(tables()[name]) for name in ("forward", "mix", "twiddle")]
     gain, backward = call(
         filter_kernel,
@@ -353,13 +361,13 @@
         cost=pl.CostEstimate(flops=int(PROJECT_FLOPS), bytes_accessed=1, transcendentals=0),
     )
     message, filters = after(message, filters)
-    signal = lax.all_to_all(message, "seq", 0, 0)
+    signal = exchange(message)
     conv = call(
         conv_kernel, shape((seq_count, 80, width), BF16), signal, gain, forward, mix, twiddle, backward
     )
     columns = [around(column, steps) for column, steps in zip(columns, (1, 2, 3))]
     conv, *columns = after(conv, *columns)
-    conv = lax.all_to_all(conv, "seq", 0, 0)
+    conv = exchange(conv)
     gated, mine, theirs = call(
         gate_kernel,
         [shape((rows, width), BF16)] + [shape((4 * width, width), BF16)] * 2,
@@ -371,7 +379,10 @@
         scalars=1,
         scratch=[turned],
     )
-    return call(output_kernel, shape((rows, width), F32), *gather(gated), mine, across(theirs), tokens)
+    pieces = [gated] + [around(gated, steps) for steps in (1, 2, 3)]
+    theirs, pieces[3] = after(across(theirs), pieces[3])
+    pieces = pieces + [across(piece) for piece in pieces]
+    return call(output_kernel, shape((rows, width), F32), *pieces, mine, theirs, tokens)
 
 
 def solution(mesh):

time: 73.2 us -> 70.8 us (0.967)
  waiting for transfers between devices: 7.19 us -> 3.94 us
  starting transfers between devices: 41.5 us -> 43.5 us
  blocking collectives: 11.8 us -> 10.8 us
    all_to_all x2, starting transfers between devices: 13.8 us -> 17 us  [exchange(): lax.all_to_all(value, 'seq', 0, 0, axis_index_groups=[list(range(15, -1,...]
    all_to_all x2, waiting for transfers between devices: 2.51 us -> 0.1 us  [exchange(): lax.all_to_all(value, 'seq', 0, 0, axis_index_groups=[list(range(15, -1,...]
    ppermute x9, waiting for transfers between devices: 2.17 us -> 0.55 us  [around(): lax.ppermute(value, 'chan', [(i, (i + 2 * steps) % count) for i in range(...]
    all_to_all x1, blocking collectives: 11.8 us -> 10.8 us  [exchange(): lax.all_to_all(value, 'seq', 0, 0, axis_index_groups=[list(range(15, -1,...]
    ppermute x9, starting transfers between devices: 16.5 us -> 15.5 us  [across(): lax.ppermute(value, 'chan', [(i, i ^ 1) for i in range(lax.axis_size('cha...]
    ppermute x9, waiting for transfers between devices: 2.51 us -> 3.3 us  [across(): lax.ppermute(value, 'chan', [(i, i ^ 1) for i in range(lax.axis_size('cha...]
  transfers between devices with their start and end apart: 20 -> 20, of which waited for: 4 -> 5; matrix products, arithmetic and copies ran while one was open for 0% -> 0% of each run, Pallas kernels for 13% -> 14%
where the time goes in v5:
time: 70.8 us; the launch traced here: 70.4 us
  starting transfers between devices  43.5 us (61%)
  Pallas kernels  11.4 us (16%)
  blocking collectives  10.8 us (15%)
  waiting for transfers between devices  3.94 us (6%)
    all_to_all x2, starting transfers between devices, exchange(): lax.all_to_all(value, 'seq', 0, 0, axis_index_groups=[list(range(15, -1,...  17 us
    ppermute x9, starting transfers between devices, across(): lax.ppermute(value, 'chan', [(i, i ^ 1) for i in range(lax.axis_size('cha...  15.5 us
    pallas_call x6, Pallas kernels, call(): pl.pallas_call(kernel, out_shape=shapes, in_specs=[pl.BlockSpec(memory_sp...  11.4 us
    ppermute x9, starting transfers between devices, around(): lax.ppermute(value, 'chan', [(i, (i + 2 * steps) % count) for i in range(...  11 us
    all_to_all x1, blocking collectives, exchange(): lax.all_to_all(value, 'seq', 0, 0, axis_index_groups=[list(range(15, -1,...  10.8 us
    ppermute x9, waiting for transfers between devices, across(): lax.ppermute(value, 'chan', [(i, i ^ 1) for i in range(lax.axis_size('cha...  3.3 us
  transfers between devices with their start and end apart: 20, of which 5 were waited for; matrix products, arithmetic and copies ran while one was open for 0% of the time, Pallas kernels for 14%

profile of v5, /device:TPU:1, one launch (start us, length us, event | category | flops | bytes accessed | tf_op | source)
XLA Modules:
  0.0 70.4 jit_solution(6159632892183751594)
XLA Ops:
  0.0 4.6 %collective-permute-start.2 = (bf16[1024,128]{1,0:T(8,128)(2,1)}, bf16[1024,128]{1,0:T(8,128)(2,1)S(1)}, u32[]{:S(2)}, u32[]{:S(2)}) collective-permute-start(bf16[1024,128]{1,0:T(8,128)(2,1)} %refs_10_.3), channel_id=1, source_target_pairs={{0,6},{1,7},{2,0},{3,1},{4,2},{5,3},{6,4},{7,5},{8,14},{9,15},{10,... | collective-permute-start | bytes 786440 | tf_op jit(solution)/shard_map/ppermute | solution.py:279
  4.6 0.7 collective-permute-start
  5.3 2.7 %shard_map.110 = (bf16[16,128,128]{2,1,0:T(8,128)(2,1)}, bf16[128,256]{1,0:T(8,128)(2,1)}, bf16[128,256]{1,0:T(8,128)(2,1)}, bf16[128,256]{1,0:T(8,128)(2,1)}) custom-call(s32[1]{0:T(128)} %bitcast.index_ref, f32[1024,128]{1,0:T(8,128)} %fwd_ref.1, f32[1024,128]{1,0:T(8,128)} %bwd_ref.1, bf16[128,1024]{1,0:T(8,128)(2,1)} %weight_ref.3), custom_call_target="tpu_custom_call" | custom-call | tf_op jit(solution)/shard_map/pallas_call | solution.py:301
  8.0 0.0 copy-start.6
  8.1 8.5 %all-to-all-start = ((bf16[16,128,128]{2,1,0:T(8,128)(2,1)}), bf16[16,128,128]{2,1,0:T(8,128)(2,1)S(1)}, u32[]{:S(2)}, u32[]{:S(2)}) async-start(bf16[16,128,128]{2,1,0:T(8,128)(2,1)} %get-tuple-element.24), calls=%async_computation | async-start | bytes 1048576 | tf_op jit(solution)/shard_map/all_to_all | solution.py:126
  16.6 1.9 %collective-permute-start.3 = (bf16[1024,128]{1,0:T(8,128)(2,1)S(1)}, bf16[1024,128]{1,0:T(8,128)(2,1)S(1)}, u32[]{:S(2)}, u32[]{:S(2)}) collective-permute-start(bf16[1024,128]{1,0:T(8,128)(2,1)S(1)} %copy-done.4), channel_id=1, source_target_pairs={{0,1},{1,0},{2,3},{3,2},{4,5},{5,4},{6,7},{7,6},{8,9},{9,8},{10,11... | collective-permute-start | bytes 786440 | tf_op jit(solution)/shard_map/ppermute | solution.py:283
  18.5 0.1 collective-permute-start.6
  18.6 0.4 collective-permute-start.5
  19.0 0.5 collective-permute-done.refs_1_
  19.5 0.8 %collective-permute-start.4 = (bf16[1024,128]{1,0:T(8,128)(2,1)S(1)}, bf16[1024,128]{1,0:T(8,128)(2,1)S(1)}, u32[]{:S(2)}, u32[]{:S(2)}) collective-permute-start(bf16[1024,128]{1,0:T(8,128)(2,1)S(1)} %collective-permute-done.refs_1_), channel_id=1, source_target_pairs={{0,1},{1,0},{2,3},{3,2},{4,5},{5,4},{6,7},{7,6},{8,9},{9,8},{10,11... | collective-permute-start | bytes 786440 | tf_op jit(solution)/shard_map/ppermute | solution.py:283
  20.4 0.0 collective-permute-done.5.refs_6_
  20.4 1.1 %collective-permute-done.4.refs_5_ = bf16[1024,128]{1,0:T(8,128)(2,1)S(1)} collective-permute-done((bf16[1024,128]{1,0:T(8,128)(2,1)S(1)}, bf16[1024,128]{1,0:T(8,128)(2,1)S(1)}, u32[]{:S(2)}, u32[]{:S(2)}) %collective-permute-start.4) | collective-permute-done | bytes 262176 | tf_op jit(solution)/shard_map/ppermute | solution.py:283
  21.5 2.7 %shard_map.109 = (bf16[16,80,128]{2,1,0:T(8,128)(2,1)}, f32[1024,128]{1,0:T(8,128)S(1)}) custom-call(s32[1]{0:T(128)} %bitcast.index_ref, bf16[1024,128]{1,0:T(8,128)(2,1)S(1)} %copy-done.4, bf16[1024,128]{1,0:T(8,128)(2,1)S(1)} %collective-permute-done.refs_1_, bf16[1024,128]{1,0:T(8,128)(2,1)S(1)} %collective-permute-done.1.refs_2_, ...), custom_call_target="tpu_custom_call" | custom-call | flops 1500000000 | bytes 1 | tf_op jit(solution)/shard_map/pallas_call | solution.py:301
  24.2 8.5 %all-to-all-start.1 = ((bf16[16,80,128]{2,1,0:T(8,128)(2,1)}), bf16[16,80,128]{2,1,0:T(8,128)(2,1)S(1)}, u32[]{:S(2)}, u32[]{:S(2)}) async-start(bf16[16,80,128]{2,1,0:T(8,128)(2,1)} %get-tuple-element.25), calls=%async_computation.1 | async-start | bytes 655360 | tf_op jit(solution)/shard_map/all_to_all | solution.py:126
  32.7 1.9 %collective-permute-start.8 = (bf16[128,256]{1,0:T(8,128)(2,1)}, bf16[128,256]{1,0:T(8,128)(2,1)S(1)}, u32[]{:S(2)}, u32[]{:S(2)}) collective-permute-start(bf16[128,256]{1,0:T(8,128)(2,1)} %get-tuple-element.29), channel_id=1, source_target_pairs={{0,4},{1,5},{2,6},{3,7},{4,0},{5,1},{6,2},{7,3},{8,12},{9,13},{10,... | collective-permute-start | bytes 196616 | tf_op jit(solution)/shard_map/ppermute | solution.py:279
  34.6 0.7 %collective-permute-start.9 = (bf16[128,256]{1,0:T(8,128)(2,1)}, bf16[128,256]{1,0:T(8,128)(2,1)S(1)}, u32[]{:S(2)}, u32[]{:S(2)}) collective-permute-start(bf16[128,256]{1,0:T(8,128)(2,1)} %get-tuple-element.30), channel_id=1, source_target_pairs={{0,6},{1,7},{2,0},{3,1},{4,2},{5,3},{6,4},{7,5},{8,14},{9,15},{10,... | collective-permute-start | bytes 196616 | tf_op jit(solution)/shard_map/ppermute | solution.py:279
  35.4 0.6 copy-done.5
  36.0 2.0 %shard_map.111 = (f32[8,2,128,128]{3,2,1,0:T(8,128)S(1)}, bf16[128,512]{1,0:T(8,128)(2,1)S(1)}) custom-call(s32[1]{0:T(128)} %bitcast.2.index_ref, f32[128]{0:T(128)S(1)} %copy-done.5, bf16[16,128,128]{2,1,0:T(8,128)(2,1)S(1)} %all-to-all-done.filt_ref, bf16[256,256]{1,0:T(8,128)(2,1)S(1)} %copy-done.3, bf16[512,256]{1,0:T(8,128)(2,1)S(1)} %copy-done.1, ...), custom_call_target="tpu_custom_call" | custom-call | tf_op jit(solution)/shard_map/pallas_call | solution.py:301
  38.1 0.1 all-to-all-done.1.sig_ref
  38.2 2.3 %shard_map.112 = bf16[16,80,128]{2,1,0:T(8,128)(2,1)S(1)} custom-call(bf16[16,80,128]{2,1,0:T(8,128)(2,1)S(1)} %all-to-all-done.1.sig_ref, f32[8,2,128,128]{3,2,1,0:T(8,128)S(1)} %get-tuple-element.26.gain_ref, bf16[256,256]{1,0:T(8,128)(2,1)S(1)} %copy-done.3, bf16[512,256]{1,0:T(8,128)(2,1)S(1)} %copy-done.1, f32[2,128,128]{2,1,0:T(8,128)S(1)} %copy-done.2, ...), custom_call_target="tpu_custom_call" | custom-call | tf_op jit(solution)/shard_map/pallas_call | solution.py:301
  40.5 10.8 %all_to_all.15.conv_ref = bf16[16,80,128]{2,1,0:T(8,128)(2,1)S(1)} all-to-all(bf16[16,80,128]{2,1,0:T(8,128)(2,1)S(1)} %shard_map.112), channel_id=1, replica_groups={{120,112,104,96,88,80,72,64,56,48,40,32,24,16,8,0},{121,113,105,97,89,8..., dimensions={0} | all-to-all | bytes 655360 | tf_op jit(solution)/shard_map/all_to_all | solution.py:126
  51.2 0.2 shard_map.113
  51.5 0.4 collective-permute-start.13
  51.9 1.9 %collective-permute-start.11 = (bf16[1024,128]{1,0:T(8,128)(2,1)S(1)}, bf16[1024,128]{1,0:T(8,128)(2,1)S(1)}, u32[]{:S(2)}, u32[]{:S(2)}) collective-permute-start(bf16[1024,128]{1,0:T(8,128)(2,1)S(1)} %get-tuple-element.36.refs_0_), channel_id=1, source_target_pairs={{0,4},{1,5},{2,6},{3,7},{4,0},{5,1},{6,2},{7,3},{8,12},{9,13},{10,... | collective-permute-start | bytes 786440 | tf_op jit(solution)/shard_map/ppermute | solution.py:279
  53.8 0.7 %collective-permute-start.10 = (bf16[1024,128]{1,0:T(8,128)(2,1)S(1)}, bf16[1024,128]{1,0:T(8,128)(2,1)S(1)}, u32[]{:S(2)}, u32[]{:S(2)}) collective-permute-start(bf16[1024,128]{1,0:T(8,128)(2,1)S(1)} %get-tuple-element.36.refs_0_), channel_id=1, source_target_pairs={{0,2},{1,3},{2,4},{3,5},{4,6},{5,7},{6,0},{7,1},{8,10},{9,11},{10,... | collective-permute-start | bytes 786440 | tf_op jit(solution)/shard_map/ppermute | solution.py:279
  54.5 3.8 %collective-permute-start.12 = (bf16[512,128]{1,0:T(8,128)(2,1)S(1)}, bf16[512,128]{1,0:T(8,128)(2,1)S(1)}, u32[]{:S(2)}, u32[]{:S(2)}) collective-permute-start(bf16[512,128]{1,0:T(8,128)(2,1)S(1)} %get-tuple-element.37), channel_id=1, source_target_pairs={{0,1},{1,0},{2,3},{3,2},{4,5},{5,4},{6,7},{7,6},{8,9},{9,8},{10,11... | collective-permute-start | bytes 393224 | tf_op jit(solution)/shard_map/ppermute | solution.py:283
  58.2 1.0 %collective-permute-done.12.refs_9_ = bf16[512,128]{1,0:T(8,128)(2,1)S(1)} collective-permute-done((bf16[512,128]{1,0:T(8,128)(2,1)S(1)}, bf16[512,128]{1,0:T(8,128)(2,1)S(1)}, u32[]{:S(2)}, u32[]{:S(2)}) %collective-permute-start.12) | collective-permute-done | bytes 131104 | tf_op jit(solution)/shard_map/ppermute | solution.py:283
  59.2 3.8 %collective-permute-start.17 = (bf16[1024,128]{1,0:T(8,128)(2,1)S(1)}, bf16[1024,128]{1,0:T(8,128)(2,1)S(1)}, u32[]{:S(2)}, u32[]{:S(2)}) collective-permute-start(bf16[1024,128]{1,0:T(8,128)(2,1)S(1)} %collective-permute-done.13.refs_3_), channel_id=1, source_target_pairs={{0,1},{1,0},{2,3},{3,2},{4,5},{5,4},{6,7},{7,6},{8,9},{9,8},{10,11... | collective-permute-start | bytes 786440 | tf_op jit(solution)/shard_map/ppermute | solution.py:283
  63.1 2.0 %collective-permute-start.16 = (bf16[1024,128]{1,0:T(8,128)(2,1)S(1)}, bf16[1024,128]{1,0:T(8,128)(2,1)S(1)}, u32[]{:S(2)}, u32[]{:S(2)}) collective-permute-start(bf16[1024,128]{1,0:T(8,128)(2,1)S(1)} %collective-permute-done.11.refs_2_), channel_id=1, source_target_pairs={{0,1},{1,0},{2,3},{3,2},{4,5},{5,4},{6,7},{7,6},{8,9},{9,8},{10,11... | collective-permute-start | bytes 786440 | tf_op jit(solution)/shard_map/ppermute | solution.py:283
  65.1 2.7 %collective-permute-start.15 = (bf16[1024,128]{1,0:T(8,128)(2,1)S(1)}, bf16[1024,128]{1,0:T(8,128)(2,1)S(1)}, u32[]{:S(2)}, u32[]{:S(2)}) collective-permute-start(bf16[1024,128]{1,0:T(8,128)(2,1)S(1)} %collective-permute-done.10.refs_1_), channel_id=1, source_target_pairs={{0,1},{1,0},{2,3},{3,2},{4,5},{5,4},{6,7},{7,6},{8,9},{9,8},{10,11... | collective-permute-start | bytes 786440 | tf_op jit(solution)/shard_map/ppermute | solution.py:283
  67.8 1.1 %collective-permute-done.15.refs_5_ = bf16[1024,128]{1,0:T(8,128)(2,1)S(1)} collective-permute-done((bf16[1024,128]{1,0:T(8,128)(2,1)S(1)}, bf16[1024,128]{1,0:T(8,128)(2,1)S(1)}, u32[]{:S(2)}, u32[]{:S(2)}) %collective-permute-start.15) | collective-permute-done | bytes 262176 | tf_op jit(solution)/shard_map/ppermute | solution.py:283
  68.9 1.5 %shard_map.114 = f32[1024,128]{1,0:T(8,128)} custom-call(bf16[1024,128]{1,0:T(8,128)(2,1)S(1)} %get-tuple-element.36.refs_0_, bf16[1024,128]{1,0:T(8,128)(2,1)S(1)} %collective-permute-done.10.refs_1_, bf16[1024,128]{1,0:T(8,128)(2,1)S(1)} %collective-permute-done.11.refs_2_, bf16[1024,128]{1,0:T(8,128)(2,1)S(1)} %collective-permute-done.13.refs_3_, ...), custom_call_target="tpu_custom_call" | custom-call | tf_op jit(solution)/shard_map/pallas_call | solution.py:301
  (33 shorter events, 0.1 us)
Async XLA Ops:
  0.0 18.5 %collective-permute-start.2 = (bf16[1024,128]{1,0:T(8,128)(2,1)}, bf16[1024,128]{1,0:T(8,128)(2,1)S(1)}, u32[]{:S(2)}, u32[]{:S(2)}) collective-permute-start(bf16[1024,128]{1,0:T(8,128)(2,1)} %refs_10_.3), channel_id=1, source_target_pairs={{0,6},{1,7},{2,0},{3,1},{4,2},{5,3},{6,4},{7,5},{8,14},{9,15},{10,... | collective-permute-start | bytes 786440 | tf_op jit(solution)/shard_map/ppermute | solution.py:279
  4.6 14.0 %collective-permute-start.1 = (bf16[1024,128]{1,0:T(8,128)(2,1)}, bf16[1024,128]{1,0:T(8,128)(2,1)S(1)}, u32[]{:S(2)}, u32[]{:S(2)}) collective-permute-start(bf16[1024,128]{1,0:T(8,128)(2,1)} %refs_10_.3), channel_id=1, source_target_pairs={{0,4},{1,5},{2,6},{3,7},{4,0},{5,1},{6,2},{7,3},{8,12},{9,13},{10,... | collective-permute-start | bytes 786440 | tf_op jit(solution)/shard_map/ppermute | solution.py:279
  4.6 14.9 %collective-permute-start = (bf16[1024,128]{1,0:T(8,128)(2,1)}, bf16[1024,128]{1,0:T(8,128)(2,1)S(1)}, u32[]{:S(2)}, u32[]{:S(2)}) collective-permute-start(bf16[1024,128]{1,0:T(8,128)(2,1)} %refs_10_.3), channel_id=1, source_target_pairs={{0,2},{1,3},{2,4},{3,5},{4,6},{5,7},{6,0},{7,1},{8,10},{9,11},{10,... | collective-permute-start | bytes 786440 | tf_op jit(solution)/shard_map/ppermute | solution.py:279
  5.3 16.2 %copy-start.7 = (f32[3,3,128]{2,1,0:T(4,128)S(1)}, f32[3,3,128]{2,1,0:T(4,128)}, u32[]{:S(2)}) copy-start(f32[3,3,128]{2,1,0:T(4,128)} %refs_10_.2) | copy-start | bytes 13828
  5.3 16.2 %copy-start.8 = (f32[1024]{0:T(1024)S(1)}, f32[1024]{0:T(1024)}, u32[]{:S(2)}) copy-start(f32[1024]{0:T(1024)} %param.12) | copy-start | bytes 12292
  8.0 13.5 %copy-start.6 = (bf16[3,1024,128]{2,1,0:T(8,128)(2,1)S(1)}, bf16[3,1024,128]{2,1,0:T(8,128)(2,1)}, u32[]{:S(2)}) copy-start(bf16[3,1024,128]{2,1,0:T(8,128)(2,1)} %refs_9_.1) | copy-start | bytes 2359300
  8.0 8.5 %copy-start.4 = (bf16[1024,128]{1,0:T(8,128)(2,1)S(1)}, bf16[1024,128]{1,0:T(8,128)(2,1)}, u32[]{:S(2)}) copy-start(bf16[1024,128]{1,0:T(8,128)(2,1)} %refs_10_.3) | copy-start | bytes 786436
  8.1 16.1 %all-to-all-start = ((bf16[16,128,128]{2,1,0:T(8,128)(2,1)}), bf16[16,128,128]{2,1,0:T(8,128)(2,1)S(1)}, u32[]{:S(2)}, u32[]{:S(2)}) async-start(bf16[16,128,128]{2,1,0:T(8,128)(2,1)} %get-tuple-element.24), calls=%async_computation | async-start | bytes 1048576 | tf_op jit(solution)/shard_map/all_to_all | solution.py:126
  16.6 3.8 %collective-permute-start.3 = (bf16[1024,128]{1,0:T(8,128)(2,1)S(1)}, bf16[1024,128]{1,0:T(8,128)(2,1)S(1)}, u32[]{:S(2)}, u32[]{:S(2)}) collective-permute-start(bf16[1024,128]{1,0:T(8,128)(2,1)S(1)} %copy-done.4), channel_id=1, source_target_pairs={{0,1},{1,0},{2,3},{3,2},{4,5},{5,4},{6,7},{7,6},{8,9},{9,8},{10,11... | collective-permute-start | bytes 786440 | tf_op jit(solution)/shard_map/ppermute | solution.py:283
  18.5 1.9 %collective-permute-start.6 = (bf16[1024,128]{1,0:T(8,128)(2,1)S(1)}, bf16[1024,128]{1,0:T(8,128)(2,1)S(1)}, u32[]{:S(2)}, u32[]{:S(2)}) collective-permute-start(bf16[1024,128]{1,0:T(8,128)(2,1)S(1)} %collective-permute-done.2.refs_3_), channel_id=1, source_target_pairs={{0,1},{1,0},{2,3},{3,2},{4,5},{5,4},{6,7},{7,6},{8,9},{9,8},{10,11... | collective-permute-start | bytes 786440 | tf_op jit(solution)/shard_map/ppermute | solution.py:283
  18.6 1.8 %collective-permute-start.5 = (bf16[1024,128]{1,0:T(8,128)(2,1)S(1)}, bf16[1024,128]{1,0:T(8,128)(2,1)S(1)}, u32[]{:S(2)}, u32[]{:S(2)}) collective-permute-start(bf16[1024,128]{1,0:T(8,128)(2,1)S(1)} %collective-permute-done.1.refs_2_), channel_id=1, source_target_pairs={{0,1},{1,0},{2,3},{3,2},{4,5},{5,4},{6,7},{7,6},{8,9},{9,8},{10,11... | collective-permute-start | bytes 786440 | tf_op jit(solution)/shard_map/ppermute | solution.py:283
  19.5 2.0 %collective-permute-start.4 = (bf16[1024,128]{1,0:T(8,128)(2,1)S(1)}, bf16[1024,128]{1,0:T(8,128)(2,1)S(1)}, u32[]{:S(2)}, u32[]{:S(2)}) collective-permute-start(bf16[1024,128]{1,0:T(8,128)(2,1)S(1)} %collective-permute-done.refs_1_), channel_id=1, source_target_pairs={{0,1},{1,0},{2,3},{3,2},{4,5},{5,4},{6,7},{7,6},{8,9},{9,8},{10,11... | collective-permute-start | bytes 786440 | tf_op jit(solution)/shard_map/ppermute | solution.py:283
  24.2 11.2 %copy-start.1 = (bf16[512,256]{1,0:T(8,128)(2,1)S(1)}, bf16[512,256]{1,0:T(8,128)(2,1)}, u32[]{:S(2)}) copy-start(bf16[512,256]{1,0:T(8,128)(2,1)} %constant.16.clone.mix_ref) | copy-start | bytes 786436
  24.2 11.2 %copy-start.2 = (f32[2,128,128]{2,1,0:T(8,128)S(1)}, f32[2,128,128]{2,1,0:T(8,128)}, u32[]{:S(2)}) copy-start(f32[2,128,128]{2,1,0:T(8,128)} %constant.17.clone.twiddle_ref) | copy-start | bytes 393220
  24.2 11.2 %copy-start.3 = (bf16[256,256]{1,0:T(8,128)(2,1)S(1)}, bf16[256,256]{1,0:T(8,128)(2,1)}, u32[]{:S(2)}) copy-start(bf16[256,256]{1,0:T(8,128)(2,1)} %constant.15.clone.forward_ref) | copy-start | bytes 393220
  24.2 14.0 %all-to-all-start.1 = ((bf16[16,80,128]{2,1,0:T(8,128)(2,1)}), bf16[16,80,128]{2,1,0:T(8,128)(2,1)S(1)}, u32[]{:S(2)}, u32[]{:S(2)}) async-start(bf16[16,80,128]{2,1,0:T(8,128)(2,1)} %get-tuple-element.25), calls=%async_computation.1 | async-start | bytes 655360 | tf_op jit(solution)/shard_map/all_to_all | solution.py:126
  32.7 7.7 %collective-permute-start.7 = (bf16[128,256]{1,0:T(8,128)(2,1)}, bf16[128,256]{1,0:T(8,128)(2,1)S(1)}, u32[]{:S(2)}, u32[]{:S(2)}) collective-permute-start(bf16[128,256]{1,0:T(8,128)(2,1)} %get-tuple-element.28), channel_id=1, source_target_pairs={{0,2},{1,3},{2,4},{3,5},{4,6},{5,7},{6,0},{7,1},{8,10},{9,11},{10,... | collective-permute-start | bytes 196616 | tf_op jit(solution)/shard_map/ppermute | solution.py:279
  32.7 7.7 %collective-permute-start.8 = (bf16[128,256]{1,0:T(8,128)(2,1)}, bf16[128,256]{1,0:T(8,128)(2,1)S(1)}, u32[]{:S(2)}, u32[]{:S(2)}) collective-permute-start(bf16[128,256]{1,0:T(8,128)(2,1)} %get-tuple-element.29), channel_id=1, source_target_pairs={{0,4},{1,5},{2,6},{3,7},{4,0},{5,1},{6,2},{7,3},{8,12},{9,13},{10,... | collective-permute-start | bytes 196616 | tf_op jit(solution)/shard_map/ppermute | solution.py:279
  34.6 5.8 %collective-permute-start.9 = (bf16[128,256]{1,0:T(8,128)(2,1)}, bf16[128,256]{1,0:T(8,128)(2,1)S(1)}, u32[]{:S(2)}, u32[]{:S(2)}) collective-permute-start(bf16[128,256]{1,0:T(8,128)(2,1)} %get-tuple-element.30), channel_id=1, source_target_pairs={{0,6},{1,7},{2,0},{3,1},{4,2},{5,3},{6,4},{7,5},{8,14},{9,15},{10,... | collective-permute-start | bytes 196616 | tf_op jit(solution)/shard_map/ppermute | solution.py:279
  35.4 0.7 copy-start.5
  40.4 10.8 %copy-start = (bf16[128,1024]{1,0:T(8,128)(2,1)S(1)}, bf16[128,1024]{1,0:T(8,128)(2,1)}, u32[]{:S(2)}) copy-start(bf16[128,1024]{1,0:T(8,128)(2,1)} %weight_ref.3) | copy-start | bytes 786436
  51.5 7.8 %collective-permute-start.13 = (bf16[1024,128]{1,0:T(8,128)(2,1)S(1)}, bf16[1024,128]{1,0:T(8,128)(2,1)S(1)}, u32[]{:S(2)}, u32[]{:S(2)}) collective-permute-start(bf16[1024,128]{1,0:T(8,128)(2,1)S(1)} %get-tuple-element.36.refs_0_), channel_id=1, source_target_pairs={{0,6},{1,7},{2,0},{3,1},{4,2},{5,3},{6,4},{7,5},{8,14},{9,15},{10,... | collective-permute-start | bytes 786440 | tf_op jit(solution)/shard_map/ppermute | solution.py:279
  51.9 11.2 %collective-permute-start.11 = (bf16[1024,128]{1,0:T(8,128)(2,1)S(1)}, bf16[1024,128]{1,0:T(8,128)(2,1)S(1)}, u32[]{:S(2)}, u32[]{:S(2)}) collective-permute-start(bf16[1024,128]{1,0:T(8,128)(2,1)S(1)} %get-tuple-element.36.refs_0_), channel_id=1, source_target_pairs={{0,4},{1,5},{2,6},{3,7},{4,0},{5,1},{6,2},{7,3},{8,12},{9,13},{10,... | collective-permute-start | bytes 786440 | tf_op jit(solution)/shard_map/ppermute | solution.py:279
  53.8 11.3 %collective-permute-start.10 = (bf16[1024,128]{1,0:T(8,128)(2,1)S(1)}, bf16[1024,128]{1,0:T(8,128)(2,1)S(1)}, u32[]{:S(2)}, u32[]{:S(2)}) collective-permute-start(bf16[1024,128]{1,0:T(8,128)(2,1)S(1)} %get-tuple-element.36.refs_0_), channel_id=1, source_target_pairs={{0,2},{1,3},{2,4},{3,5},{4,6},{5,7},{6,0},{7,1},{8,10},{9,11},{10,... | collective-permute-start | bytes 786440 | tf_op jit(solution)/shard_map/ppermute | solution.py:279
  54.5 4.7 %collective-permute-start.12 = (bf16[512,128]{1,0:T(8,128)(2,1)S(1)}, bf16[512,128]{1,0:T(8,128)(2,1)S(1)}, u32[]{:S(2)}, u32[]{:S(2)}) collective-permute-start(bf16[512,128]{1,0:T(8,128)(2,1)S(1)} %get-tuple-element.37), channel_id=1, source_target_pairs={{0,1},{1,0},{2,3},{3,2},{4,5},{5,4},{6,7},{7,6},{8,9},{9,8},{10,11... | collective-permute-start | bytes 393224 | tf_op jit(solution)/shard_map/ppermute | solution.py:283
  58.2 9.5 %collective-permute-start.14 = (bf16[1024,128]{1,0:T(8,128)(2,1)S(1)}, bf16[1024,128]{1,0:T(8,128)(2,1)S(1)}, u32[]{:S(2)}, u32[]{:S(2)}) collective-permute-start(bf16[1024,128]{1,0:T(8,128)(2,1)S(1)} %get-tuple-element.36.refs_0_), channel_id=1, source_target_pairs={{0,1},{1,0},{2,3},{3,2},{4,5},{5,4},{6,7},{7,6},{8,9},{9,8},{10,11... | collective-permute-start | bytes 786440 | tf_op jit(solution)/shard_map/ppermute | solution.py:283
  59.2 8.5 %collective-permute-start.17 = (bf16[1024,128]{1,0:T(8,128)(2,1)S(1)}, bf16[1024,128]{1,0:T(8,128)(2,1)S(1)}, u32[]{:S(2)}, u32[]{:S(2)}) collective-permute-start(bf16[1024,128]{1,0:T(8,128)(2,1)S(1)} %collective-permute-done.13.refs_3_), channel_id=1, source_target_pairs={{0,1},{1,0},{2,3},{3,2},{4,5},{5,4},{6,7},{7,6},{8,9},{9,8},{10,11... | collective-permute-start | bytes 786440 | tf_op jit(solution)/shard_map/ppermute | solution.py:283
  63.1 4.7 %collective-permute-start.16 = (bf16[1024,128]{1,0:T(8,128)(2,1)S(1)}, bf16[1024,128]{1,0:T(8,128)(2,1)S(1)}, u32[]{:S(2)}, u32[]{:S(2)}) collective-permute-start(bf16[1024,128]{1,0:T(8,128)(2,1)S(1)} %collective-permute-done.11.refs_2_), channel_id=1, source_target_pairs={{0,1},{1,0},{2,3},{3,2},{4,5},{5,4},{6,7},{7,6},{8,9},{9,8},{10,11... | collective-permute-start | bytes 786440 | tf_op jit(solution)/shard_map/ppermute | solution.py:283
  65.1 3.9 %collective-permute-start.15 = (bf16[1024,128]{1,0:T(8,128)(2,1)S(1)}, bf16[1024,128]{1,0:T(8,128)(2,1)S(1)}, u32[]{:S(2)}, u32[]{:S(2)}) collective-permute-start(bf16[1024,128]{1,0:T(8,128)(2,1)S(1)} %collective-permute-done.10.refs_1_), channel_id=1, source_target_pairs={{0,1},{1,0},{2,3},{3,2},{4,5},{5,4},{6,7},{7,6},{8,9},{9,8},{10,11... | collective-permute-start | bytes 786440 | tf_op jit(solution)/shard_map/ppermute | solution.py:283

commit v6 on v5

--- a/solution.py
+++ b/solution.py
@@ -265,13 +265,19 @@
 
 
 def output_kernel(*refs):
-    gated, mine_ref, theirs_ref, tokens_ref, out_ref = refs[:8], *refs[8:]
+    gated, (mine_ref, theirs_ref, tokens_ref, out_ref, total_ref, sems) = refs[:8], refs[8:]
     weight = jnp.concatenate([mine_ref[...], theirs_ref[...]], axis=0)
     step = 256
-    for start in range(0, out_ref.shape[0], step):
+    copies = []
+    for start in range(0, total_ref.shape[0], step):
         piece = slice(start, start + step)
         product = dot(jnp.concatenate([ref[piece, :] for ref in gated], axis=1), weight)
-        out_ref[piece, :] = tokens_ref[piece, :].astype(F32) + product
+        total_ref[piece, :] = tokens_ref[piece, :].astype(F32) + product
+        part = pl.ds(start, step)
+        copies.append(pltpu.make_async_copy(total_ref.at[part, :], out_ref.at[part, :], sems.at[start // step]))
+        copies[-1].start()
+    for copy in copies:
+        copy.wait()
 
 
 def around(value, steps):
@@ -292,7 +298,7 @@
     return lax.optimization_barrier(values)
 
 
-def call(kernel, shapes, *operands, scalars=0, outside=(), scratch=(), cost=None):
+def call(kernel, shapes, *operands, scalars=0, outside=(), written=(), scratch=(), cost=None):
     spaces = [pltpu.SMEM if i < scalars else pltpu.HBM if i in outside else pltpu.VMEM for i in range(len(operands))]
     operands = [
         pltpu.with_memory_space_constraint(operand, space) if space is pltpu.HBM else operand
@@ -300,9 +306,9 @@
     ]
     return pl.pallas_call(
         kernel,
-        out_shape=shapes,
+        out_shape=list(shapes),
         in_specs=[pl.BlockSpec(memory_space=space) for space in spaces],
-        out_specs=jax.tree.map(lambda _: VMEM, shapes),
+        out_specs=[pl.BlockSpec(memory_space=pl.ANY) if i in written else VMEM for i in range(len(shapes))],
         scratch_shapes=scratch,
         cost_estimate=cost,
         compiler_params=pltpu.CompilerParams(vmem_limit_bytes=VMEM_LIMIT),
@@ -362,8 +368,8 @@
     )
     message, filters = after(message, filters)
     signal = exchange(message)
-    conv = call(
-        conv_kernel, shape((seq_count, 80, width), BF16), signal, gain, forward, mix, twiddle, backward
+    (conv,) = call(
+        conv_kernel, [shape((seq_count, 80, width), BF16)], signal, gain, forward, mix, twiddle, backward
     )
     columns = [around(column, steps) for column, steps in zip(columns, (1, 2, 3))]
     conv, *columns = after(conv, *columns)
@@ -382,7 +388,17 @@
     pieces = [gated] + [around(gated, steps) for steps in (1, 2, 3)]
     theirs, pieces[3] = after(across(theirs), pieces[3])
     pieces = pieces + [across(piece) for piece in pieces]
-    return call(output_kernel, shape((rows, width), F32), *pieces, mine, theirs, tokens)
+    (result,) = call(
+        output_kernel,
+        [shape((rows, width), F32)],
+        *pieces,
+        mine,
+        theirs,
+        tokens,
+        written=(0,),
+        scratch=[turned, pltpu.SemaphoreType.DMA((rows // 256,))],
+    )
+    return result
 
 
 def solution(mesh):

time: 70.8 us -> 70.7 us (level)
  no operation moved by 1% of the time
where the time goes in v6:
time: 70.7 us; the launch traced here: 70.3 us
  starting transfers between devices  43.5 us (62%)
  Pallas kernels  11.3 us (16%)
  blocking collectives  10.8 us (15%)
  waiting for transfers between devices  3.94 us (6%)
    all_to_all x2, starting transfers between devices, exchange(): lax.all_to_all(value, 'seq', 0, 0, axis_index_groups=[list(range(15, -1,...  17 us
    ppermute x9, starting transfers between devices, across(): lax.ppermute(value, 'chan', [(i, i ^ 1) for i in range(lax.axis_size('cha...  15.5 us
    pallas_call x6, Pallas kernels, call(): pl.pallas_call(kernel, out_shape=list(shapes), in_specs=[pl.BlockSpec(mem...  11.3 us
    ppermute x9, starting transfers between devices, around(): lax.ppermute(value, 'chan', [(i, (i + 2 * steps) % count) for i in range(...  11 us
    all_to_all x1, blocking collectives, exchange(): lax.all_to_all(value, 'seq', 0, 0, axis_index_groups=[list(range(15, -1,...  10.8 us
    ppermute x9, waiting for transfers between devices, across(): lax.ppermute(value, 'chan', [(i, i ^ 1) for i in range(lax.axis_size('cha...  3.3 us
  transfers between devices with their start and end apart: 20, of which 5 were waited for; matrix products, arithmetic and copies ran while one was open for 0% of the time, Pallas kernels for 14%

profile of v6, /device:TPU:1, one launch (start us, length us, event | category | flops | bytes accessed | tf_op | source)
XLA Modules:
  0.0 70.3 jit_solution(11436284410626128931)
XLA Ops:
  0.0 4.6 %collective-permute-start.2 = (bf16[1024,128]{1,0:T(8,128)(2,1)}, bf16[1024,128]{1,0:T(8,128)(2,1)S(1)}, u32[]{:S(2)}, u32[]{:S(2)}) collective-permute-start(bf16[1024,128]{1,0:T(8,128)(2,1)} %refs_10_.3), channel_id=1, source_target_pairs={{0,6},{1,7},{2,0},{3,1},{4,2},{5,3},{6,4},{7,5},{8,14},{9,15},{10,... | collective-permute-start | bytes 786440 | tf_op jit(solution)/shard_map/ppermute | solution.py:285
  4.6 0.7 collective-permute-start
  5.3 2.7 %shard_map.110 = (bf16[16,128,128]{2,1,0:T(8,128)(2,1)}, bf16[128,256]{1,0:T(8,128)(2,1)}, bf16[128,256]{1,0:T(8,128)(2,1)}, bf16[128,256]{1,0:T(8,128)(2,1)}) custom-call(s32[1]{0:T(128)} %bitcast.index_ref, f32[1024,128]{1,0:T(8,128)} %fwd_ref.1, f32[1024,128]{1,0:T(8,128)} %bwd_ref.1, bf16[128,1024]{1,0:T(8,128)(2,1)} %weight_ref.3), custom_call_target="tpu_custom_call" | custom-call | tf_op jit(solution)/shard_map/pallas_call | solution.py:307
  8.0 0.0 copy-start.6
  8.1 8.5 %all-to-all-start = ((bf16[16,128,128]{2,1,0:T(8,128)(2,1)}), bf16[16,128,128]{2,1,0:T(8,128)(2,1)S(1)}, u32[]{:S(2)}, u32[]{:S(2)}) async-start(bf16[16,128,128]{2,1,0:T(8,128)(2,1)} %get-tuple-element.24), calls=%async_computation | async-start | bytes 1048576 | tf_op jit(solution)/shard_map/all_to_all | solution.py:126
  16.6 1.9 %collective-permute-start.3 = (bf16[1024,128]{1,0:T(8,128)(2,1)S(1)}, bf16[1024,128]{1,0:T(8,128)(2,1)S(1)}, u32[]{:S(2)}, u32[]{:S(2)}) collective-permute-start(bf16[1024,128]{1,0:T(8,128)(2,1)S(1)} %copy-done.4), channel_id=1, source_target_pairs={{0,1},{1,0},{2,3},{3,2},{4,5},{5,4},{6,7},{7,6},{8,9},{9,8},{10,11... | collective-permute-start | bytes 786440 | tf_op jit(solution)/shard_map/ppermute | solution.py:289
  18.5 0.1 collective-permute-start.6
  18.6 0.4 collective-permute-start.5
  19.0 0.5 collective-permute-done.refs_1_
  19.5 0.8 %collective-permute-start.4 = (bf16[1024,128]{1,0:T(8,128)(2,1)S(1)}, bf16[1024,128]{1,0:T(8,128)(2,1)S(1)}, u32[]{:S(2)}, u32[]{:S(2)}) collective-permute-start(bf16[1024,128]{1,0:T(8,128)(2,1)S(1)} %collective-permute-done.refs_1_), channel_id=1, source_target_pairs={{0,1},{1,0},{2,3},{3,2},{4,5},{5,4},{6,7},{7,6},{8,9},{9,8},{10,11... | collective-permute-start | bytes 786440 | tf_op jit(solution)/shard_map/ppermute | solution.py:289
  20.4 0.0 collective-permute-done.5.refs_6_
  20.4 1.1 %collective-permute-done.4.refs_5_ = bf16[1024,128]{1,0:T(8,128)(2,1)S(1)} collective-permute-done((bf16[1024,128]{1,0:T(8,128)(2,1)S(1)}, bf16[1024,128]{1,0:T(8,128)(2,1)S(1)}, u32[]{:S(2)}, u32[]{:S(2)}) %collective-permute-start.4) | collective-permute-done | bytes 262176 | tf_op jit(solution)/shard_map/ppermute | solution.py:289
  21.5 2.7 %shard_map.109 = (bf16[16,80,128]{2,1,0:T(8,128)(2,1)}, f32[1024,128]{1,0:T(8,128)S(1)}) custom-call(s32[1]{0:T(128)} %bitcast.index_ref, bf16[1024,128]{1,0:T(8,128)(2,1)S(1)} %copy-done.4, bf16[1024,128]{1,0:T(8,128)(2,1)S(1)} %collective-permute-done.refs_1_, bf16[1024,128]{1,0:T(8,128)(2,1)S(1)} %collective-permute-done.1.refs_2_, ...), custom_call_target="tpu_custom_call" | custom-call | flops 1500000000 | bytes 1 | tf_op jit(solution)/shard_map/pallas_call | solution.py:307
  24.2 8.5 %all-to-all-start.1 = ((bf16[16,80,128]{2,1,0:T(8,128)(2,1)}), bf16[16,80,128]{2,1,0:T(8,128)(2,1)S(1)}, u32[]{:S(2)}, u32[]{:S(2)}) async-start(bf16[16,80,128]{2,1,0:T(8,128)(2,1)} %get-tuple-element.25), calls=%async_computation.1 | async-start | bytes 655360 | tf_op jit(solution)/shard_map/all_to_all | solution.py:126
  32.7 1.9 %collective-permute-start.8 = (bf16[128,256]{1,0:T(8,128)(2,1)}, bf16[128,256]{1,0:T(8,128)(2,1)S(1)}, u32[]{:S(2)}, u32[]{:S(2)}) collective-permute-start(bf16[128,256]{1,0:T(8,128)(2,1)} %get-tuple-element.29), channel_id=1, source_target_pairs={{0,4},{1,5},{2,6},{3,7},{4,0},{5,1},{6,2},{7,3},{8,12},{9,13},{10,... | collective-permute-start | bytes 196616 | tf_op jit(solution)/shard_map/ppermute | solution.py:285
  34.6 0.7 %collective-permute-start.9 = (bf16[128,256]{1,0:T(8,128)(2,1)}, bf16[128,256]{1,0:T(8,128)(2,1)S(1)}, u32[]{:S(2)}, u32[]{:S(2)}) collective-permute-start(bf16[128,256]{1,0:T(8,128)(2,1)} %get-tuple-element.30), channel_id=1, source_target_pairs={{0,6},{1,7},{2,0},{3,1},{4,2},{5,3},{6,4},{7,5},{8,14},{9,15},{10,... | collective-permute-start | bytes 196616 | tf_op jit(solution)/shard_map/ppermute | solution.py:285
  35.4 0.6 copy-done.5
  36.0 2.0 %shard_map.111 = (f32[8,2,128,128]{3,2,1,0:T(8,128)S(1)}, bf16[128,512]{1,0:T(8,128)(2,1)S(1)}) custom-call(s32[1]{0:T(128)} %bitcast.2.index_ref, f32[128]{0:T(128)S(1)} %copy-done.5, bf16[16,128,128]{2,1,0:T(8,128)(2,1)S(1)} %all-to-all-done.filt_ref, bf16[256,256]{1,0:T(8,128)(2,1)S(1)} %copy-done.3, bf16[512,256]{1,0:T(8,128)(2,1)S(1)} %copy-done.1, ...), custom_call_target="tpu_custom_call" | custom-call | tf_op jit(solution)/shard_map/pallas_call | solution.py:307
  38.1 0.1 all-to-all-done.1.sig_ref
  38.2 2.3 %shard_map.112 = bf16[16,80,128]{2,1,0:T(8,128)(2,1)S(1)} custom-call(bf16[16,80,128]{2,1,0:T(8,128)(2,1)S(1)} %all-to-all-done.1.sig_ref, f32[8,2,128,128]{3,2,1,0:T(8,128)S(1)} %get-tuple-element.26.gain_ref, bf16[256,256]{1,0:T(8,128)(2,1)S(1)} %copy-done.3, bf16[512,256]{1,0:T(8,128)(2,1)S(1)} %copy-done.1, f32[2,128,128]{2,1,0:T(8,128)S(1)} %copy-done.2, ...), custom_call_target="tpu_custom_call" | custom-call | tf_op jit(solution)/shard_map/pallas_call | solution.py:307
  40.5 10.8 %all_to_all.15.conv_ref = bf16[16,80,128]{2,1,0:T(8,128)(2,1)S(1)} all-to-all(bf16[16,80,128]{2,1,0:T(8,128)(2,1)S(1)} %shard_map.112), channel_id=1, replica_groups={{120,112,104,96,88,80,72,64,56,48,40,32,24,16,8,0},{121,113,105,97,89,8..., dimensions={0} | all-to-all | bytes 655360 | tf_op jit(solution)/shard_map/all_to_all | solution.py:126
  51.2 0.2 shard_map.113
  51.5 0.4 collective-permute-start.13
  51.9 1.9 %collective-permute-start.11 = (bf16[1024,128]{1,0:T(8,128)(2,1)S(1)}, bf16[1024,128]{1,0:T(8,128)(2,1)S(1)}, u32[]{:S(2)}, u32[]{:S(2)}) collective-permute-start(bf16[1024,128]{1,0:T(8,128)(2,1)S(1)} %get-tuple-element.36.refs_0_), channel_id=1, source_target_pairs={{0,4},{1,5},{2,6},{3,7},{4,0},{5,1},{6,2},{7,3},{8,12},{9,13},{10,... | collective-permute-start | bytes 786440 | tf_op jit(solution)/shard_map/ppermute | solution.py:285
  53.8 0.7 %collective-permute-start.10 = (bf16[1024,128]{1,0:T(8,128)(2,1)S(1)}, bf16[1024,128]{1,0:T(8,128)(2,1)S(1)}, u32[]{:S(2)}, u32[]{:S(2)}) collective-permute-start(bf16[1024,128]{1,0:T(8,128)(2,1)S(1)} %get-tuple-element.36.refs_0_), channel_id=1, source_target_pairs={{0,2},{1,3},{2,4},{3,5},{4,6},{5,7},{6,0},{7,1},{8,10},{9,11},{10,... | collective-permute-start | bytes 786440 | tf_op jit(solution)/shard_map/ppermute | solution.py:285
  54.5 3.8 %collective-permute-start.12 = (bf16[512,128]{1,0:T(8,128)(2,1)S(1)}, bf16[512,128]{1,0:T(8,128)(2,1)S(1)}, u32[]{:S(2)}, u32[]{:S(2)}) collective-permute-start(bf16[512,128]{1,0:T(8,128)(2,1)S(1)} %get-tuple-element.37), channel_id=1, source_target_pairs={{0,1},{1,0},{2,3},{3,2},{4,5},{5,4},{6,7},{7,6},{8,9},{9,8},{10,11... | collective-permute-start | bytes 393224 | tf_op jit(solution)/shard_map/ppermute | solution.py:289
  58.2 1.0 %collective-permute-done.12.refs_9_ = bf16[512,128]{1,0:T(8,128)(2,1)S(1)} collective-permute-done((bf16[512,128]{1,0:T(8,128)(2,1)S(1)}, bf16[512,128]{1,0:T(8,128)(2,1)S(1)}, u32[]{:S(2)}, u32[]{:S(2)}) %collective-permute-start.12) | collective-permute-done | bytes 131104 | tf_op jit(solution)/shard_map/ppermute | solution.py:289
  59.2 3.8 %collective-permute-start.17 = (bf16[1024,128]{1,0:T(8,128)(2,1)S(1)}, bf16[1024,128]{1,0:T(8,128)(2,1)S(1)}, u32[]{:S(2)}, u32[]{:S(2)}) collective-permute-start(bf16[1024,128]{1,0:T(8,128)(2,1)S(1)} %collective-permute-done.13.refs_3_), channel_id=1, source_target_pairs={{0,1},{1,0},{2,3},{3,2},{4,5},{5,4},{6,7},{7,6},{8,9},{9,8},{10,11... | collective-permute-start | bytes 786440 | tf_op jit(solution)/shard_map/ppermute | solution.py:289
  63.1 2.0 %collective-permute-start.16 = (bf16[1024,128]{1,0:T(8,128)(2,1)S(1)}, bf16[1024,128]{1,0:T(8,128)(2,1)S(1)}, u32[]{:S(2)}, u32[]{:S(2)}) collective-permute-start(bf16[1024,128]{1,0:T(8,128)(2,1)S(1)} %collective-permute-done.11.refs_2_), channel_id=1, source_target_pairs={{0,1},{1,0},{2,3},{3,2},{4,5},{5,4},{6,7},{7,6},{8,9},{9,8},{10,11... | collective-permute-start | bytes 786440 | tf_op jit(solution)/shard_map/ppermute | solution.py:289
  65.1 2.7 %collective-permute-start.15 = (bf16[1024,128]{1,0:T(8,128)(2,1)S(1)}, bf16[1024,128]{1,0:T(8,128)(2,1)S(1)}, u32[]{:S(2)}, u32[]{:S(2)}) collective-permute-start(bf16[1024,128]{1,0:T(8,128)(2,1)S(1)} %collective-permute-done.10.refs_1_), channel_id=1, source_target_pairs={{0,1},{1,0},{2,3},{3,2},{4,5},{5,4},{6,7},{7,6},{8,9},{9,8},{10,11... | collective-permute-start | bytes 786440 | tf_op jit(solution)/shard_map/ppermute | solution.py:289
  67.8 1.1 %collective-permute-done.15.refs_5_ = bf16[1024,128]{1,0:T(8,128)(2,1)S(1)} collective-permute-done((bf16[1024,128]{1,0:T(8,128)(2,1)S(1)}, bf16[1024,128]{1,0:T(8,128)(2,1)S(1)}, u32[]{:S(2)}, u32[]{:S(2)}) %collective-permute-start.15) | collective-permute-done | bytes 262176 | tf_op jit(solution)/shard_map/ppermute | solution.py:289
  68.9 1.4 %shard_map.114 = f32[1024,128]{1,0:T(8,128)} custom-call(bf16[1024,128]{1,0:T(8,128)(2,1)S(1)} %get-tuple-element.36.refs_0_, bf16[1024,128]{1,0:T(8,128)(2,1)S(1)} %collective-permute-done.10.refs_1_, bf16[1024,128]{1,0:T(8,128)(2,1)S(1)} %collective-permute-done.11.refs_2_, bf16[1024,128]{1,0:T(8,128)(2,1)S(1)} %collective-permute-done.13.refs_3_, ...), custom_call_target="tpu_custom_call" | custom-call | tf_op jit(solution)/shard_map/pallas_call | solution.py:307
  (33 shorter events, 0.1 us)
Async XLA Ops:
  0.0 18.5 %collective-permute-start.2 = (bf16[1024,128]{1,0:T(8,128)(2,1)}, bf16[1024,128]{1,0:T(8,128)(2,1)S(1)}, u32[]{:S(2)}, u32[]{:S(2)}) collective-permute-start(bf16[1024,128]{1,0:T(8,128)(2,1)} %refs_10_.3), channel_id=1, source_target_pairs={{0,6},{1,7},{2,0},{3,1},{4,2},{5,3},{6,4},{7,5},{8,14},{9,15},{10,... | collective-permute-start | bytes 786440 | tf_op jit(solution)/shard_map/ppermute | solution.py:285
  4.6 14.0 %collective-permute-start.1 = (bf16[1024,128]{1,0:T(8,128)(2,1)}, bf16[1024,128]{1,0:T(8,128)(2,1)S(1)}, u32[]{:S(2)}, u32[]{:S(2)}) collective-permute-start(bf16[1024,128]{1,0:T(8,128)(2,1)} %refs_10_.3), channel_id=1, source_target_pairs={{0,4},{1,5},{2,6},{3,7},{4,0},{5,1},{6,2},{7,3},{8,12},{9,13},{10,... | collective-permute-start | bytes 786440 | tf_op jit(solution)/shard_map/ppermute | solution.py:285
  4.6 14.9 %collective-permute-start = (bf16[1024,128]{1,0:T(8,128)(2,1)}, bf16[1024,128]{1,0:T(8,128)(2,1)S(1)}, u32[]{:S(2)}, u32[]{:S(2)}) collective-permute-start(bf16[1024,128]{1,0:T(8,128)(2,1)} %refs_10_.3), channel_id=1, source_target_pairs={{0,2},{1,3},{2,4},{3,5},{4,6},{5,7},{6,0},{7,1},{8,10},{9,11},{10,... | collective-permute-start | bytes 786440 | tf_op jit(solution)/shard_map/ppermute | solution.py:285
  5.3 16.2 %copy-start.7 = (f32[3,3,128]{2,1,0:T(4,128)S(1)}, f32[3,3,128]{2,1,0:T(4,128)}, u32[]{:S(2)}) copy-start(f32[3,3,128]{2,1,0:T(4,128)} %refs_10_.2) | copy-start | bytes 13828
  5.3 16.2 %copy-start.8 = (f32[1024]{0:T(1024)S(1)}, f32[1024]{0:T(1024)}, u32[]{:S(2)}) copy-start(f32[1024]{0:T(1024)} %param.12) | copy-start | bytes 12292
  8.0 13.5 %copy-start.6 = (bf16[3,1024,128]{2,1,0:T(8,128)(2,1)S(1)}, bf16[3,1024,128]{2,1,0:T(8,128)(2,1)}, u32[]{:S(2)}) copy-start(bf16[3,1024,128]{2,1,0:T(8,128)(2,1)} %refs_9_.1) | copy-start | bytes 2359300
  8.0 8.5 %copy-start.4 = (bf16[1024,128]{1,0:T(8,128)(2,1)S(1)}, bf16[1024,128]{1,0:T(8,128)(2,1)}, u32[]{:S(2)}) copy-start(bf16[1024,128]{1,0:T(8,128)(2,1)} %refs_10_.3) | copy-start | bytes 786436
  8.1 16.1 %all-to-all-start = ((bf16[16,128,128]{2,1,0:T(8,128)(2,1)}), bf16[16,128,128]{2,1,0:T(8,128)(2,1)S(1)}, u32[]{:S(2)}, u32[]{:S(2)}) async-start(bf16[16,128,128]{2,1,0:T(8,128)(2,1)} %get-tuple-element.24), calls=%async_computation | async-start | bytes 1048576 | tf_op jit(solution)/shard_map/all_to_all | solution.py:126
  16.6 3.8 %collective-permute-start.3 = (bf16[1024,128]{1,0:T(8,128)(2,1)S(1)}, bf16[1024,128]{1,0:T(8,128)(2,1)S(1)}, u32[]{:S(2)}, u32[]{:S(2)}) collective-permute-start(bf16[1024,128]{1,0:T(8,128)(2,1)S(1)} %copy-done.4), channel_id=1, source_target_pairs={{0,1},{1,0},{2,3},{3,2},{4,5},{5,4},{6,7},{7,6},{8,9},{9,8},{10,11... | collective-permute-start | bytes 786440 | tf_op jit(solution)/shard_map/ppermute | solution.py:289
  18.5 1.9 %collective-permute-start.6 = (bf16[1024,128]{1,0:T(8,128)(2,1)S(1)}, bf16[1024,128]{1,0:T(8,128)(2,1)S(1)}, u32[]{:S(2)}, u32[]{:S(2)}) collective-permute-start(bf16[1024,128]{1,0:T(8,128)(2,1)S(1)} %collective-permute-done.2.refs_3_), channel_id=1, source_target_pairs={{0,1},{1,0},{2,3},{3,2},{4,5},{5,4},{6,7},{7,6},{8,9},{9,8},{10,11... | collective-permute-start | bytes 786440 | tf_op jit(solution)/shard_map/ppermute | solution.py:289
  18.6 1.8 %collective-permute-start.5 = (bf16[1024,128]{1,0:T(8,128)(2,1)S(1)}, bf16[1024,128]{1,0:T(8,128)(2,1)S(1)}, u32[]{:S(2)}, u32[]{:S(2)}) collective-permute-start(bf16[1024,128]{1,0:T(8,128)(2,1)S(1)} %collective-permute-done.1.refs_2_), channel_id=1, source_target_pairs={{0,1},{1,0},{2,3},{3,2},{4,5},{5,4},{6,7},{7,6},{8,9},{9,8},{10,11... | collective-permute-start | bytes 786440 | tf_op jit(solution)/shard_map/ppermute | solution.py:289
  19.5 2.0 %collective-permute-start.4 = (bf16[1024,128]{1,0:T(8,128)(2,1)S(1)}, bf16[1024,128]{1,0:T(8,128)(2,1)S(1)}, u32[]{:S(2)}, u32[]{:S(2)}) collective-permute-start(bf16[1024,128]{1,0:T(8,128)(2,1)S(1)} %collective-permute-done.refs_1_), channel_id=1, source_target_pairs={{0,1},{1,0},{2,3},{3,2},{4,5},{5,4},{6,7},{7,6},{8,9},{9,8},{10,11... | collective-permute-start | bytes 786440 | tf_op jit(solution)/shard_map/ppermute | solution.py:289
  24.2 11.2 %copy-start.1 = (bf16[512,256]{1,0:T(8,128)(2,1)S(1)}, bf16[512,256]{1,0:T(8,128)(2,1)}, u32[]{:S(2)}) copy-start(bf16[512,256]{1,0:T(8,128)(2,1)} %constant.16.clone.mix_ref) | copy-start | bytes 786436
  24.2 11.2 %copy-start.2 = (f32[2,128,128]{2,1,0:T(8,128)S(1)}, f32[2,128,128]{2,1,0:T(8,128)}, u32[]{:S(2)}) copy-start(f32[2,128,128]{2,1,0:T(8,128)} %constant.17.clone.twiddle_ref) | copy-start | bytes 393220
  24.2 11.2 %copy-start.3 = (bf16[256,256]{1,0:T(8,128)(2,1)S(1)}, bf16[256,256]{1,0:T(8,128)(2,1)}, u32[]{:S(2)}) copy-start(bf16[256,256]{1,0:T(8,128)(2,1)} %constant.15.clone.forward_ref) | copy-start | bytes 393220
  24.2 14.0 %all-to-all-start.1 = ((bf16[16,80,128]{2,1,0:T(8,128)(2,1)}), bf16[16,80,128]{2,1,0:T(8,128)(2,1)S(1)}, u32[]{:S(2)}, u32[]{:S(2)}) async-start(bf16[16,80,128]{2,1,0:T(8,128)(2,1)} %get-tuple-element.25), calls=%async_computation.1 | async-start | bytes 655360 | tf_op jit(solution)/shard_map/all_to_all | solution.py:126
  32.7 7.7 %collective-permute-start.7 = (bf16[128,256]{1,0:T(8,128)(2,1)}, bf16[128,256]{1,0:T(8,128)(2,1)S(1)}, u32[]{:S(2)}, u32[]{:S(2)}) collective-permute-start(bf16[128,256]{1,0:T(8,128)(2,1)} %get-tuple-element.28), channel_id=1, source_target_pairs={{0,2},{1,3},{2,4},{3,5},{4,6},{5,7},{6,0},{7,1},{8,10},{9,11},{10,... | collective-permute-start | bytes 196616 | tf_op jit(solution)/shard_map/ppermute | solution.py:285
  32.7 7.7 %collective-permute-start.8 = (bf16[128,256]{1,0:T(8,128)(2,1)}, bf16[128,256]{1,0:T(8,128)(2,1)S(1)}, u32[]{:S(2)}, u32[]{:S(2)}) collective-permute-start(bf16[128,256]{1,0:T(8,128)(2,1)} %get-tuple-element.29), channel_id=1, source_target_pairs={{0,4},{1,5},{2,6},{3,7},{4,0},{5,1},{6,2},{7,3},{8,12},{9,13},{10,... | collective-permute-start | bytes 196616 | tf_op jit(solution)/shard_map/ppermute | solution.py:285
  34.6 5.8 %collective-permute-start.9 = (bf16[128,256]{1,0:T(8,128)(2,1)}, bf16[128,256]{1,0:T(8,128)(2,1)S(1)}, u32[]{:S(2)}, u32[]{:S(2)}) collective-permute-start(bf16[128,256]{1,0:T(8,128)(2,1)} %get-tuple-element.30), channel_id=1, source_target_pairs={{0,6},{1,7},{2,0},{3,1},{4,2},{5,3},{6,4},{7,5},{8,14},{9,15},{10,... | collective-permute-start | bytes 196616 | tf_op jit(solution)/shard_map/ppermute | solution.py:285
  35.4 0.7 copy-start.5
  40.4 10.8 %copy-start = (bf16[128,1024]{1,0:T(8,128)(2,1)S(1)}, bf16[128,1024]{1,0:T(8,128)(2,1)}, u32[]{:S(2)}) copy-start(bf16[128,1024]{1,0:T(8,128)(2,1)} %weight_ref.3) | copy-start | bytes 786436
  51.5 7.8 %collective-permute-start.13 = (bf16[1024,128]{1,0:T(8,128)(2,1)S(1)}, bf16[1024,128]{1,0:T(8,128)(2,1)S(1)}, u32[]{:S(2)}, u32[]{:S(2)}) collective-permute-start(bf16[1024,128]{1,0:T(8,128)(2,1)S(1)} %get-tuple-element.36.refs_0_), channel_id=1, source_target_pairs={{0,6},{1,7},{2,0},{3,1},{4,2},{5,3},{6,4},{7,5},{8,14},{9,15},{10,... | collective-permute-start | bytes 786440 | tf_op jit(solution)/shard_map/ppermute | solution.py:285
  51.9 11.2 %collective-permute-start.11 = (bf16[1024,128]{1,0:T(8,128)(2,1)S(1)}, bf16[1024,128]{1,0:T(8,128)(2,1)S(1)}, u32[]{:S(2)}, u32[]{:S(2)}) collective-permute-start(bf16[1024,128]{1,0:T(8,128)(2,1)S(1)} %get-tuple-element.36.refs_0_), channel_id=1, source_target_pairs={{0,4},{1,5},{2,6},{3,7},{4,0},{5,1},{6,2},{7,3},{8,12},{9,13},{10,... | collective-permute-start | bytes 786440 | tf_op jit(solution)/shard_map/ppermute | solution.py:285
  53.8 11.3 %collective-permute-start.10 = (bf16[1024,128]{1,0:T(8,128)(2,1)S(1)}, bf16[1024,128]{1,0:T(8,128)(2,1)S(1)}, u32[]{:S(2)}, u32[]{:S(2)}) collective-permute-start(bf16[1024,128]{1,0:T(8,128)(2,1)S(1)} %get-tuple-element.36.refs_0_), channel_id=1, source_target_pairs={{0,2},{1,3},{2,4},{3,5},{4,6},{5,7},{6,0},{7,1},{8,10},{9,11},{10,... | collective-permute-start | bytes 786440 | tf_op jit(solution)/shard_map/ppermute | solution.py:285
  54.5 4.7 %collective-permute-start.12 = (bf16[512,128]{1,0:T(8,128)(2,1)S(1)}, bf16[512,128]{1,0:T(8,128)(2,1)S(1)}, u32[]{:S(2)}, u32[]{:S(2)}) collective-permute-start(bf16[512,128]{1,0:T(8,128)(2,1)S(1)} %get-tuple-element.37), channel_id=1, source_target_pairs={{0,1},{1,0},{2,3},{3,2},{4,5},{5,4},{6,7},{7,6},{8,9},{9,8},{10,11... | collective-permute-start | bytes 393224 | tf_op jit(solution)/shard_map/ppermute | solution.py:289
  58.2 9.5 %collective-permute-start.14 = (bf16[1024,128]{1,0:T(8,128)(2,1)S(1)}, bf16[1024,128]{1,0:T(8,128)(2,1)S(1)}, u32[]{:S(2)}, u32[]{:S(2)}) collective-permute-start(bf16[1024,128]{1,0:T(8,128)(2,1)S(1)} %get-tuple-element.36.refs_0_), channel_id=1, source_target_pairs={{0,1},{1,0},{2,3},{3,2},{4,5},{5,4},{6,7},{7,6},{8,9},{9,8},{10,11... | collective-permute-start | bytes 786440 | tf_op jit(solution)/shard_map/ppermute | solution.py:289
  59.2 8.5 %collective-permute-start.17 = (bf16[1024,128]{1,0:T(8,128)(2,1)S(1)}, bf16[1024,128]{1,0:T(8,128)(2,1)S(1)}, u32[]{:S(2)}, u32[]{:S(2)}) collective-permute-start(bf16[1024,128]{1,0:T(8,128)(2,1)S(1)} %collective-permute-done.13.refs_3_), channel_id=1, source_target_pairs={{0,1},{1,0},{2,3},{3,2},{4,5},{5,4},{6,7},{7,6},{8,9},{9,8},{10,11... | collective-permute-start | bytes 786440 | tf_op jit(solution)/shard_map/ppermute | solution.py:289
  63.1 4.7 %collective-permute-start.16 = (bf16[1024,128]{1,0:T(8,128)(2,1)S(1)}, bf16[1024,128]{1,0:T(8,128)(2,1)S(1)}, u32[]{:S(2)}, u32[]{:S(2)}) collective-permute-start(bf16[1024,128]{1,0:T(8,128)(2,1)S(1)} %collective-permute-done.11.refs_2_), channel_id=1, source_target_pairs={{0,1},{1,0},{2,3},{3,2},{4,5},{5,4},{6,7},{7,6},{8,9},{9,8},{10,11... | collective-permute-start | bytes 786440 | tf_op jit(solution)/shard_map/ppermute | solution.py:289
  65.1 3.9 %collective-permute-start.15 = (bf16[1024,128]{1,0:T(8,128)(2,1)S(1)}, bf16[1024,128]{1,0:T(8,128)(2,1)S(1)}, u32[]{:S(2)}, u32[]{:S(2)}) collective-permute-start(bf16[1024,128]{1,0:T(8,128)(2,1)S(1)} %collective-permute-done.10.refs_1_), channel_id=1, source_target_pairs={{0,1},{1,0},{2,3},{3,2},{4,5},{5,4},{6,7},{7,6},{8,9},{9,8},{10,11... | collective-permute-start | bytes 786440 | tf_op jit(solution)/shard_map/ppermute | solution.py:289

commit v7 on v6

--- a/solution.py
+++ b/solution.py
@@ -385,7 +385,8 @@
         scalars=1,
         scratch=[turned],
     )
-    pieces = [gated] + [around(gated, steps) for steps in (1, 2, 3)]
+    moved = {steps: around(gated, steps) for steps in (1, 3, 2)}
+    pieces = [gated] + [moved[steps] for steps in (1, 2, 3)]
     theirs, pieces[3] = after(across(theirs), pieces[3])
     pieces = pieces + [across(piece) for piece in pieces]
     (result,) = call(

time: 70.7 us -> 70.7 us (level)
  no operation moved by 1% of the time
where the time goes in v7:
time: 70.7 us; the launch traced here: 70.3 us
  starting transfers between devices  43.5 us (62%)
  Pallas kernels  11.3 us (16%)
  blocking collectives  10.8 us (15%)
  waiting for transfers between devices  3.94 us (6%)
    all_to_all x2, starting transfers between devices, exchange(): lax.all_to_all(value, 'seq', 0, 0, axis_index_groups=[list(range(15, -1,...  17 us
    ppermute x9, starting transfers between devices, across(): lax.ppermute(value, 'chan', [(i, i ^ 1) for i in range(lax.axis_size('cha...  15.5 us
    pallas_call x6, Pallas kernels, call(): pl.pallas_call(kernel, out_shape=list(shapes), in_specs=[pl.BlockSpec(mem...  11.3 us
    ppermute x9, starting transfers between devices, around(): lax.ppermute(value, 'chan', [(i, (i + 2 * steps) % count) for i in range(...  11 us
    all_to_all x1, blocking collectives, exchange(): lax.all_to_all(value, 'seq', 0, 0, axis_index_groups=[list(range(15, -1,...  10.8 us
    ppermute x9, waiting for transfers between devices, across(): lax.ppermute(value, 'chan', [(i, i ^ 1) for i in range(lax.axis_size('cha...  3.3 us
  transfers between devices with their start and end apart: 20, of which 5 were waited for; matrix products, arithmetic and copies ran while one was open for 0% of the time, Pallas kernels for 14%

profile of v7, /device:TPU:1, one launch (start us, length us, event | category | flops | bytes accessed | tf_op | source)
XLA Modules:
  0.0 70.3 jit_solution(11436284410626128931)
XLA Ops:
  0.0 4.6 %collective-permute-start.2 = (bf16[1024,128]{1,0:T(8,128)(2,1)}, bf16[1024,128]{1,0:T(8,128)(2,1)S(1)}, u32[]{:S(2)}, u32[]{:S(2)}) collective-permute-start(bf16[1024,128]{1,0:T(8,128)(2,1)} %refs_10_.3), channel_id=1, source_target_pairs={{0,6},{1,7},{2,0},{3,1},{4,2},{5,3},{6,4},{7,5},{8,14},{9,15},{10,... | collective-permute-start | bytes 786440 | tf_op jit(solution)/shard_map/ppermute | solution.py:285
  4.6 0.7 collective-permute-start
  5.3 2.7 %shard_map.110 = (bf16[16,128,128]{2,1,0:T(8,128)(2,1)}, bf16[128,256]{1,0:T(8,128)(2,1)}, bf16[128,256]{1,0:T(8,128)(2,1)}, bf16[128,256]{1,0:T(8,128)(2,1)}) custom-call(s32[1]{0:T(128)} %bitcast.index_ref, f32[1024,128]{1,0:T(8,128)} %fwd_ref.1, f32[1024,128]{1,0:T(8,128)} %bwd_ref.1, bf16[128,1024]{1,0:T(8,128)(2,1)} %weight_ref.3), custom_call_target="tpu_custom_call" | custom-call | tf_op jit(solution)/shard_map/pallas_call | solution.py:307
  8.0 0.0 copy-start.6
  8.1 8.5 %all-to-all-start = ((bf16[16,128,128]{2,1,0:T(8,128)(2,1)}), bf16[16,128,128]{2,1,0:T(8,128)(2,1)S(1)}, u32[]{:S(2)}, u32[]{:S(2)}) async-start(bf16[16,128,128]{2,1,0:T(8,128)(2,1)} %get-tuple-element.24), calls=%async_computation | async-start | bytes 1048576 | tf_op jit(solution)/shard_map/all_to_all | solution.py:126
  16.6 1.9 %collective-permute-start.3 = (bf16[1024,128]{1,0:T(8,128)(2,1)S(1)}, bf16[1024,128]{1,0:T(8,128)(2,1)S(1)}, u32[]{:S(2)}, u32[]{:S(2)}) collective-permute-start(bf16[1024,128]{1,0:T(8,128)(2,1)S(1)} %copy-done.4), channel_id=1, source_target_pairs={{0,1},{1,0},{2,3},{3,2},{4,5},{5,4},{6,7},{7,6},{8,9},{9,8},{10,11... | collective-permute-start | bytes 786440 | tf_op jit(solution)/shard_map/ppermute | solution.py:289
  18.5 0.1 collective-permute-start.6
  18.6 0.4 collective-permute-start.5
  19.0 0.5 collective-permute-done.refs_1_
  19.5 0.8 %collective-permute-start.4 = (bf16[1024,128]{1,0:T(8,128)(2,1)S(1)}, bf16[1024,128]{1,0:T(8,128)(2,1)S(1)}, u32[]{:S(2)}, u32[]{:S(2)}) collective-permute-start(bf16[1024,128]{1,0:T(8,128)(2,1)S(1)} %collective-permute-done.refs_1_), channel_id=1, source_target_pairs={{0,1},{1,0},{2,3},{3,2},{4,5},{5,4},{6,7},{7,6},{8,9},{9,8},{10,11... | collective-permute-start | bytes 786440 | tf_op jit(solution)/shard_map/ppermute | solution.py:289
  20.4 0.0 collective-permute-done.5.refs_6_
  20.4 1.1 %collective-permute-done.4.refs_5_ = bf16[1024,128]{1,0:T(8,128)(2,1)S(1)} collective-permute-done((bf16[1024,128]{1,0:T(8,128)(2,1)S(1)}, bf16[1024,128]{1,0:T(8,128)(2,1)S(1)}, u32[]{:S(2)}, u32[]{:S(2)}) %collective-permute-start.4) | collective-permute-done | bytes 262176 | tf_op jit(solution)/shard_map/ppermute | solution.py:289
  21.5 2.7 %shard_map.109 = (bf16[16,80,128]{2,1,0:T(8,128)(2,1)}, f32[1024,128]{1,0:T(8,128)S(1)}) custom-call(s32[1]{0:T(128)} %bitcast.index_ref, bf16[1024,128]{1,0:T(8,128)(2,1)S(1)} %copy-done.4, bf16[1024,128]{1,0:T(8,128)(2,1)S(1)} %collective-permute-done.refs_1_, bf16[1024,128]{1,0:T(8,128)(2,1)S(1)} %collective-permute-done.1.refs_2_, ...), custom_call_target="tpu_custom_call" | custom-call | flops 1500000000 | bytes 1 | tf_op jit(solution)/shard_map/pallas_call | solution.py:307
  24.2 8.5 %all-to-all-start.1 = ((bf16[16,80,128]{2,1,0:T(8,128)(2,1)}), bf16[16,80,128]{2,1,0:T(8,128)(2,1)S(1)}, u32[]{:S(2)}, u32[]{:S(2)}) async-start(bf16[16,80,128]{2,1,0:T(8,128)(2,1)} %get-tuple-element.25), calls=%async_computation.1 | async-start | bytes 655360 | tf_op jit(solution)/shard_map/all_to_all | solution.py:126
  32.7 1.9 %collective-permute-start.8 = (bf16[128,256]{1,0:T(8,128)(2,1)}, bf16[128,256]{1,0:T(8,128)(2,1)S(1)}, u32[]{:S(2)}, u32[]{:S(2)}) collective-permute-start(bf16[128,256]{1,0:T(8,128)(2,1)} %get-tuple-element.29), channel_id=1, source_target_pairs={{0,4},{1,5},{2,6},{3,7},{4,0},{5,1},{6,2},{7,3},{8,12},{9,13},{10,... | collective-permute-start | bytes 196616 | tf_op jit(solution)/shard_map/ppermute | solution.py:285
  34.6 0.7 %collective-permute-start.9 = (bf16[128,256]{1,0:T(8,128)(2,1)}, bf16[128,256]{1,0:T(8,128)(2,1)S(1)}, u32[]{:S(2)}, u32[]{:S(2)}) collective-permute-start(bf16[128,256]{1,0:T(8,128)(2,1)} %get-tuple-element.30), channel_id=1, source_target_pairs={{0,6},{1,7},{2,0},{3,1},{4,2},{5,3},{6,4},{7,5},{8,14},{9,15},{10,... | collective-permute-start | bytes 196616 | tf_op jit(solution)/shard_map/ppermute | solution.py:285
  35.4 0.6 copy-done.5
  36.0 2.0 %shard_map.111 = (f32[8,2,128,128]{3,2,1,0:T(8,128)S(1)}, bf16[128,512]{1,0:T(8,128)(2,1)S(1)}) custom-call(s32[1]{0:T(128)} %bitcast.2.index_ref, f32[128]{0:T(128)S(1)} %copy-done.5, bf16[16,128,128]{2,1,0:T(8,128)(2,1)S(1)} %all-to-all-done.filt_ref, bf16[256,256]{1,0:T(8,128)(2,1)S(1)} %copy-done.3, bf16[512,256]{1,0:T(8,128)(2,1)S(1)} %copy-done.1, ...), custom_call_target="tpu_custom_call" | custom-call | tf_op jit(solution)/shard_map/pallas_call | solution.py:307
  38.1 0.1 all-to-all-done.1.sig_ref
  38.2 2.3 %shard_map.112 = bf16[16,80,128]{2,1,0:T(8,128)(2,1)S(1)} custom-call(bf16[16,80,128]{2,1,0:T(8,128)(2,1)S(1)} %all-to-all-done.1.sig_ref, f32[8,2,128,128]{3,2,1,0:T(8,128)S(1)} %get-tuple-element.26.gain_ref, bf16[256,256]{1,0:T(8,128)(2,1)S(1)} %copy-done.3, bf16[512,256]{1,0:T(8,128)(2,1)S(1)} %copy-done.1, f32[2,128,128]{2,1,0:T(8,128)S(1)} %copy-done.2, ...), custom_call_target="tpu_custom_call" | custom-call | tf_op jit(solution)/shard_map/pallas_call | solution.py:307
  40.5 10.8 %all_to_all.15.conv_ref = bf16[16,80,128]{2,1,0:T(8,128)(2,1)S(1)} all-to-all(bf16[16,80,128]{2,1,0:T(8,128)(2,1)S(1)} %shard_map.112), channel_id=1, replica_groups={{120,112,104,96,88,80,72,64,56,48,40,32,24,16,8,0},{121,113,105,97,89,8..., dimensions={0} | all-to-all | bytes 655360 | tf_op jit(solution)/shard_map/all_to_all | solution.py:126
  51.2 0.2 shard_map.113
  51.5 0.4 collective-permute-start.13
  51.9 1.9 %collective-permute-start.11 = (bf16[1024,128]{1,0:T(8,128)(2,1)S(1)}, bf16[1024,128]{1,0:T(8,128)(2,1)S(1)}, u32[]{:S(2)}, u32[]{:S(2)}) collective-permute-start(bf16[1024,128]{1,0:T(8,128)(2,1)S(1)} %get-tuple-element.36.refs_0_), channel_id=1, source_target_pairs={{0,4},{1,5},{2,6},{3,7},{4,0},{5,1},{6,2},{7,3},{8,12},{9,13},{10,... | collective-permute-start | bytes 786440 | tf_op jit(solution)/shard_map/ppermute | solution.py:285
  53.8 0.7 %collective-permute-start.10 = (bf16[1024,128]{1,0:T(8,128)(2,1)S(1)}, bf16[1024,128]{1,0:T(8,128)(2,1)S(1)}, u32[]{:S(2)}, u32[]{:S(2)}) collective-permute-start(bf16[1024,128]{1,0:T(8,128)(2,1)S(1)} %get-tuple-element.36.refs_0_), channel_id=1, source_target_pairs={{0,2},{1,3},{2,4},{3,5},{4,6},{5,7},{6,0},{7,1},{8,10},{9,11},{10,... | collective-permute-start | bytes 786440 | tf_op jit(solution)/shard_map/ppermute | solution.py:285
  54.5 3.8 %collective-permute-start.12 = (bf16[512,128]{1,0:T(8,128)(2,1)S(1)}, bf16[512,128]{1,0:T(8,128)(2,1)S(1)}, u32[]{:S(2)}, u32[]{:S(2)}) collective-permute-start(bf16[512,128]{1,0:T(8,128)(2,1)S(1)} %get-tuple-element.37), channel_id=1, source_target_pairs={{0,1},{1,0},{2,3},{3,2},{4,5},{5,4},{6,7},{7,6},{8,9},{9,8},{10,11... | collective-permute-start | bytes 393224 | tf_op jit(solution)/shard_map/ppermute | solution.py:289
  58.2 1.0 %collective-permute-done.12.refs_9_ = bf16[512,128]{1,0:T(8,128)(2,1)S(1)} collective-permute-done((bf16[512,128]{1,0:T(8,128)(2,1)S(1)}, bf16[512,128]{1,0:T(8,128)(2,1)S(1)}, u32[]{:S(2)}, u32[]{:S(2)}) %collective-permute-start.12) | collective-permute-done | bytes 131104 | tf_op jit(solution)/shard_map/ppermute | solution.py:289
  59.2 3.8 %collective-permute-start.17 = (bf16[1024,128]{1,0:T(8,128)(2,1)S(1)}, bf16[1024,128]{1,0:T(8,128)(2,1)S(1)}, u32[]{:S(2)}, u32[]{:S(2)}) collective-permute-start(bf16[1024,128]{1,0:T(8,128)(2,1)S(1)} %collective-permute-done.13.refs_3_), channel_id=1, source_target_pairs={{0,1},{1,0},{2,3},{3,2},{4,5},{5,4},{6,7},{7,6},{8,9},{9,8},{10,11... | collective-permute-start | bytes 786440 | tf_op jit(solution)/shard_map/ppermute | solution.py:289
  63.1 2.0 %collective-permute-start.16 = (bf16[1024,128]{1,0:T(8,128)(2,1)S(1)}, bf16[1024,128]{1,0:T(8,128)(2,1)S(1)}, u32[]{:S(2)}, u32[]{:S(2)}) collective-permute-start(bf16[1024,128]{1,0:T(8,128)(2,1)S(1)} %collective-permute-done.11.refs_2_), channel_id=1, source_target_pairs={{0,1},{1,0},{2,3},{3,2},{4,5},{5,4},{6,7},{7,6},{8,9},{9,8},{10,11... | collective-permute-start | bytes 786440 | tf_op jit(solution)/shard_map/ppermute | solution.py:289
  65.1 2.7 %collective-permute-start.15 = (bf16[1024,128]{1,0:T(8,128)(2,1)S(1)}, bf16[1024,128]{1,0:T(8,128)(2,1)S(1)}, u32[]{:S(2)}, u32[]{:S(2)}) collective-permute-start(bf16[1024,128]{1,0:T(8,128)(2,1)S(1)} %collective-permute-done.10.refs_1_), channel_id=1, source_target_pairs={{0,1},{1,0},{2,3},{3,2},{4,5},{5,4},{6,7},{7,6},{8,9},{9,8},{10,11... | collective-permute-start | bytes 786440 | tf_op jit(solution)/shard_map/ppermute | solution.py:289
  67.8 1.1 %collective-permute-done.15.refs_5_ = bf16[1024,128]{1,0:T(8,128)(2,1)S(1)} collective-permute-done((bf16[1024,128]{1,0:T(8,128)(2,1)S(1)}, bf16[1024,128]{1,0:T(8,128)(2,1)S(1)}, u32[]{:S(2)}, u32[]{:S(2)}) %collective-permute-start.15) | collective-permute-done | bytes 262176 | tf_op jit(solution)/shard_map/ppermute | solution.py:289
  68.9 1.4 %shard_map.114 = f32[1024,128]{1,0:T(8,128)} custom-call(bf16[1024,128]{1,0:T(8,128)(2,1)S(1)} %get-tuple-element.36.refs_0_, bf16[1024,128]{1,0:T(8,128)(2,1)S(1)} %collective-permute-done.10.refs_1_, bf16[1024,128]{1,0:T(8,128)(2,1)S(1)} %collective-permute-done.11.refs_2_, bf16[1024,128]{1,0:T(8,128)(2,1)S(1)} %collective-permute-done.13.refs_3_, ...), custom_call_target="tpu_custom_call" | custom-call | tf_op jit(solution)/shard_map/pallas_call | solution.py:307
  (33 shorter events, 0.1 us)
Async XLA Ops:
  0.0 18.5 %collective-permute-start.2 = (bf16[1024,128]{1,0:T(8,128)(2,1)}, bf16[1024,128]{1,0:T(8,128)(2,1)S(1)}, u32[]{:S(2)}, u32[]{:S(2)}) collective-permute-start(bf16[1024,128]{1,0:T(8,128)(2,1)} %refs_10_.3), channel_id=1, source_target_pairs={{0,6},{1,7},{2,0},{3,1},{4,2},{5,3},{6,4},{7,5},{8,14},{9,15},{10,... | collective-permute-start | bytes 786440 | tf_op jit(solution)/shard_map/ppermute | solution.py:285
  4.6 14.0 %collective-permute-start.1 = (bf16[1024,128]{1,0:T(8,128)(2,1)}, bf16[1024,128]{1,0:T(8,128)(2,1)S(1)}, u32[]{:S(2)}, u32[]{:S(2)}) collective-permute-start(bf16[1024,128]{1,0:T(8,128)(2,1)} %refs_10_.3), channel_id=1, source_target_pairs={{0,4},{1,5},{2,6},{3,7},{4,0},{5,1},{6,2},{7,3},{8,12},{9,13},{10,... | collective-permute-start | bytes 786440 | tf_op jit(solution)/shard_map/ppermute | solution.py:285
  4.6 14.9 %collective-permute-start = (bf16[1024,128]{1,0:T(8,128)(2,1)}, bf16[1024,128]{1,0:T(8,128)(2,1)S(1)}, u32[]{:S(2)}, u32[]{:S(2)}) collective-permute-start(bf16[1024,128]{1,0:T(8,128)(2,1)} %refs_10_.3), channel_id=1, source_target_pairs={{0,2},{1,3},{2,4},{3,5},{4,6},{5,7},{6,0},{7,1},{8,10},{9,11},{10,... | collective-permute-start | bytes 786440 | tf_op jit(solution)/shard_map/ppermute | solution.py:285
  5.3 16.2 %copy-start.7 = (f32[3,3,128]{2,1,0:T(4,128)S(1)}, f32[3,3,128]{2,1,0:T(4,128)}, u32[]{:S(2)}) copy-start(f32[3,3,128]{2,1,0:T(4,128)} %refs_10_.2) | copy-start | bytes 13828
  5.3 16.2 %copy-start.8 = (f32[1024]{0:T(1024)S(1)}, f32[1024]{0:T(1024)}, u32[]{:S(2)}) copy-start(f32[1024]{0:T(1024)} %param.12) | copy-start | bytes 12292
  8.0 13.5 %copy-start.6 = (bf16[3,1024,128]{2,1,0:T(8,128)(2,1)S(1)}, bf16[3,1024,128]{2,1,0:T(8,128)(2,1)}, u32[]{:S(2)}) copy-start(bf16[3,1024,128]{2,1,0:T(8,128)(2,1)} %refs_9_.1) | copy-start | bytes 2359300
  8.0 8.5 %copy-start.4 = (bf16[1024,128]{1,0:T(8,128)(2,1)S(1)}, bf16[1024,128]{1,0:T(8,128)(2,1)}, u32[]{:S(2)}) copy-start(bf16[1024,128]{1,0:T(8,128)(2,1)} %refs_10_.3) | copy-start | bytes 786436
  8.1 16.1 %all-to-all-start = ((bf16[16,128,128]{2,1,0:T(8,128)(2,1)}), bf16[16,128,128]{2,1,0:T(8,128)(2,1)S(1)}, u32[]{:S(2)}, u32[]{:S(2)}) async-start(bf16[16,128,128]{2,1,0:T(8,128)(2,1)} %get-tuple-element.24), calls=%async_computation | async-start | bytes 1048576 | tf_op jit(solution)/shard_map/all_to_all | solution.py:126
  16.6 3.8 %collective-permute-start.3 = (bf16[1024,128]{1,0:T(8,128)(2,1)S(1)}, bf16[1024,128]{1,0:T(8,128)(2,1)S(1)}, u32[]{:S(2)}, u32[]{:S(2)}) collective-permute-start(bf16[1024,128]{1,0:T(8,128)(2,1)S(1)} %copy-done.4), channel_id=1, source_target_pairs={{0,1},{1,0},{2,3},{3,2},{4,5},{5,4},{6,7},{7,6},{8,9},{9,8},{10,11... | collective-permute-start | bytes 786440 | tf_op jit(solution)/shard_map/ppermute | solution.py:289
  18.5 1.9 %collective-permute-start.6 = (bf16[1024,128]{1,0:T(8,128)(2,1)S(1)}, bf16[1024,128]{1,0:T(8,128)(2,1)S(1)}, u32[]{:S(2)}, u32[]{:S(2)}) collective-permute-start(bf16[1024,128]{1,0:T(8,128)(2,1)S(1)} %collective-permute-done.2.refs_3_), channel_id=1, source_target_pairs={{0,1},{1,0},{2,3},{3,2},{4,5},{5,4},{6,7},{7,6},{8,9},{9,8},{10,11... | collective-permute-start | bytes 786440 | tf_op jit(solution)/shard_map/ppermute | solution.py:289
  18.6 1.8 %collective-permute-start.5 = (bf16[1024,128]{1,0:T(8,128)(2,1)S(1)}, bf16[1024,128]{1,0:T(8,128)(2,1)S(1)}, u32[]{:S(2)}, u32[]{:S(2)}) collective-permute-start(bf16[1024,128]{1,0:T(8,128)(2,1)S(1)} %collective-permute-done.1.refs_2_), channel_id=1, source_target_pairs={{0,1},{1,0},{2,3},{3,2},{4,5},{5,4},{6,7},{7,6},{8,9},{9,8},{10,11... | collective-permute-start | bytes 786440 | tf_op jit(solution)/shard_map/ppermute | solution.py:289
  19.5 2.0 %collective-permute-start.4 = (bf16[1024,128]{1,0:T(8,128)(2,1)S(1)}, bf16[1024,128]{1,0:T(8,128)(2,1)S(1)}, u32[]{:S(2)}, u32[]{:S(2)}) collective-permute-start(bf16[1024,128]{1,0:T(8,128)(2,1)S(1)} %collective-permute-done.refs_1_), channel_id=1, source_target_pairs={{0,1},{1,0},{2,3},{3,2},{4,5},{5,4},{6,7},{7,6},{8,9},{9,8},{10,11... | collective-permute-start | bytes 786440 | tf_op jit(solution)/shard_map/ppermute | solution.py:289
  24.2 11.2 %copy-start.1 = (bf16[512,256]{1,0:T(8,128)(2,1)S(1)}, bf16[512,256]{1,0:T(8,128)(2,1)}, u32[]{:S(2)}) copy-start(bf16[512,256]{1,0:T(8,128)(2,1)} %constant.16.clone.mix_ref) | copy-start | bytes 786436
  24.2 11.2 %copy-start.2 = (f32[2,128,128]{2,1,0:T(8,128)S(1)}, f32[2,128,128]{2,1,0:T(8,128)}, u32[]{:S(2)}) copy-start(f32[2,128,128]{2,1,0:T(8,128)} %constant.17.clone.twiddle_ref) | copy-start | bytes 393220
  24.2 11.2 %copy-start.3 = (bf16[256,256]{1,0:T(8,128)(2,1)S(1)}, bf16[256,256]{1,0:T(8,128)(2,1)}, u32[]{:S(2)}) copy-start(bf16[256,256]{1,0:T(8,128)(2,1)} %constant.15.clone.forward_ref) | copy-start | bytes 393220
  24.2 14.0 %all-to-all-start.1 = ((bf16[16,80,128]{2,1,0:T(8,128)(2,1)}), bf16[16,80,128]{2,1,0:T(8,128)(2,1)S(1)}, u32[]{:S(2)}, u32[]{:S(2)}) async-start(bf16[16,80,128]{2,1,0:T(8,128)(2,1)} %get-tuple-element.25), calls=%async_computation.1 | async-start | bytes 655360 | tf_op jit(solution)/shard_map/all_to_all | solution.py:126
  32.7 7.7 %collective-permute-start.7 = (bf16[128,256]{1,0:T(8,128)(2,1)}, bf16[128,256]{1,0:T(8,128)(2,1)S(1)}, u32[]{:S(2)}, u32[]{:S(2)}) collective-permute-start(bf16[128,256]{1,0:T(8,128)(2,1)} %get-tuple-element.28), channel_id=1, source_target_pairs={{0,2},{1,3},{2,4},{3,5},{4,6},{5,7},{6,0},{7,1},{8,10},{9,11},{10,... | collective-permute-start | bytes 196616 | tf_op jit(solution)/shard_map/ppermute | solution.py:285
  32.7 7.7 %collective-permute-start.8 = (bf16[128,256]{1,0:T(8,128)(2,1)}, bf16[128,256]{1,0:T(8,128)(2,1)S(1)}, u32[]{:S(2)}, u32[]{:S(2)}) collective-permute-start(bf16[128,256]{1,0:T(8,128)(2,1)} %get-tuple-element.29), channel_id=1, source_target_pairs={{0,4},{1,5},{2,6},{3,7},{4,0},{5,1},{6,2},{7,3},{8,12},{9,13},{10,... | collective-permute-start | bytes 196616 | tf_op jit(solution)/shard_map/ppermute | solution.py:285
  34.6 5.8 %collective-permute-start.9 = (bf16[128,256]{1,0:T(8,128)(2,1)}, bf16[128,256]{1,0:T(8,128)(2,1)S(1)}, u32[]{:S(2)}, u32[]{:S(2)}) collective-permute-start(bf16[128,256]{1,0:T(8,128)(2,1)} %get-tuple-element.30), channel_id=1, source_target_pairs={{0,6},{1,7},{2,0},{3,1},{4,2},{5,3},{6,4},{7,5},{8,14},{9,15},{10,... | collective-permute-start | bytes 196616 | tf_op jit(solution)/shard_map/ppermute | solution.py:285
  35.4 0.7 copy-start.5
  40.4 10.8 %copy-start = (bf16[128,1024]{1,0:T(8,128)(2,1)S(1)}, bf16[128,1024]{1,0:T(8,128)(2,1)}, u32[]{:S(2)}) copy-start(bf16[128,1024]{1,0:T(8,128)(2,1)} %weight_ref.3) | copy-start | bytes 786436
  51.5 7.8 %collective-permute-start.13 = (bf16[1024,128]{1,0:T(8,128)(2,1)S(1)}, bf16[1024,128]{1,0:T(8,128)(2,1)S(1)}, u32[]{:S(2)}, u32[]{:S(2)}) collective-permute-start(bf16[1024,128]{1,0:T(8,128)(2,1)S(1)} %get-tuple-element.36.refs_0_), channel_id=1, source_target_pairs={{0,6},{1,7},{2,0},{3,1},{4,2},{5,3},{6,4},{7,5},{8,14},{9,15},{10,... | collective-permute-start | bytes 786440 | tf_op jit(solution)/shard_map/ppermute | solution.py:285
  51.9 11.2 %collective-permute-start.11 = (bf16[1024,128]{1,0:T(8,128)(2,1)S(1)}, bf16[1024,128]{1,0:T(8,128)(2,1)S(1)}, u32[]{:S(2)}, u32[]{:S(2)}) collective-permute-start(bf16[1024,128]{1,0:T(8,128)(2,1)S(1)} %get-tuple-element.36.refs_0_), channel_id=1, source_target_pairs={{0,4},{1,5},{2,6},{3,7},{4,0},{5,1},{6,2},{7,3},{8,12},{9,13},{10,... | collective-permute-start | bytes 786440 | tf_op jit(solution)/shard_map/ppermute | solution.py:285
  53.8 11.3 %collective-permute-start.10 = (bf16[1024,128]{1,0:T(8,128)(2,1)S(1)}, bf16[1024,128]{1,0:T(8,128)(2,1)S(1)}, u32[]{:S(2)}, u32[]{:S(2)}) collective-permute-start(bf16[1024,128]{1,0:T(8,128)(2,1)S(1)} %get-tuple-element.36.refs_0_), channel_id=1, source_target_pairs={{0,2},{1,3},{2,4},{3,5},{4,6},{5,7},{6,0},{7,1},{8,10},{9,11},{10,... | collective-permute-start | bytes 786440 | tf_op jit(solution)/shard_map/ppermute | solution.py:285
  54.5 4.7 %collective-permute-start.12 = (bf16[512,128]{1,0:T(8,128)(2,1)S(1)}, bf16[512,128]{1,0:T(8,128)(2,1)S(1)}, u32[]{:S(2)}, u32[]{:S(2)}) collective-permute-start(bf16[512,128]{1,0:T(8,128)(2,1)S(1)} %get-tuple-element.37), channel_id=1, source_target_pairs={{0,1},{1,0},{2,3},{3,2},{4,5},{5,4},{6,7},{7,6},{8,9},{9,8},{10,11... | collective-permute-start | bytes 393224 | tf_op jit(solution)/shard_map/ppermute | solution.py:289
  58.2 9.5 %collective-permute-start.14 = (bf16[1024,128]{1,0:T(8,128)(2,1)S(1)}, bf16[1024,128]{1,0:T(8,128)(2,1)S(1)}, u32[]{:S(2)}, u32[]{:S(2)}) collective-permute-start(bf16[1024,128]{1,0:T(8,128)(2,1)S(1)} %get-tuple-element.36.refs_0_), channel_id=1, source_target_pairs={{0,1},{1,0},{2,3},{3,2},{4,5},{5,4},{6,7},{7,6},{8,9},{9,8},{10,11... | collective-permute-start | bytes 786440 | tf_op jit(solution)/shard_map/ppermute | solution.py:289
  59.2 8.5 %collective-permute-start.17 = (bf16[1024,128]{1,0:T(8,128)(2,1)S(1)}, bf16[1024,128]{1,0:T(8,128)(2,1)S(1)}, u32[]{:S(2)}, u32[]{:S(2)}) collective-permute-start(bf16[1024,128]{1,0:T(8,128)(2,1)S(1)} %collective-permute-done.13.refs_3_), channel_id=1, source_target_pairs={{0,1},{1,0},{2,3},{3,2},{4,5},{5,4},{6,7},{7,6},{8,9},{9,8},{10,11... | collective-permute-start | bytes 786440 | tf_op jit(solution)/shard_map/ppermute | solution.py:289
  63.1 4.7 %collective-permute-start.16 = (bf16[1024,128]{1,0:T(8,128)(2,1)S(1)}, bf16[1024,128]{1,0:T(8,128)(2,1)S(1)}, u32[]{:S(2)}, u32[]{:S(2)}) collective-permute-start(bf16[1024,128]{1,0:T(8,128)(2,1)S(1)} %collective-permute-done.11.refs_2_), channel_id=1, source_target_pairs={{0,1},{1,0},{2,3},{3,2},{4,5},{5,4},{6,7},{7,6},{8,9},{9,8},{10,11... | collective-permute-start | bytes 786440 | tf_op jit(solution)/shard_map/ppermute | solution.py:289
  65.1 3.9 %collective-permute-start.15 = (bf16[1024,128]{1,0:T(8,128)(2,1)S(1)}, bf16[1024,128]{1,0:T(8,128)(2,1)S(1)}, u32[]{:S(2)}, u32[]{:S(2)}) collective-permute-start(bf16[1024,128]{1,0:T(8,128)(2,1)S(1)} %collective-permute-done.10.refs_1_), channel_id=1, source_target_pairs={{0,1},{1,0},{2,3},{3,2},{4,5},{5,4},{6,7},{7,6},{8,9},{9,8},{10,11... | collective-permute-start | bytes 786440 | tf_op jit(solution)/shard_map/ppermute | solution.py:289
